TPU v7x, 32 devices: a whole 2x2x4 slice. The times are simulated.
32 devices in a mesh: seq: 8 (over z, core), dp: 4 (over y, x).
Axes of the slice: x: 2, y: 2, z: 4, core: 2. Of those that a mesh axis runs over, the one named last changes fastest.
Arguments:
- hidden_in: bfloat16 [4, 1024, 1152], P('dp', 'seq'), may hold values from -6 to 6
- attn_norm: float32 [1152], P(('seq', 'dp')), may hold values from 0.1 to 1.9
- query_weight: bfloat16 [1152, 1152], P(('seq', 'dp')), may hold values from -0.1875 to 0.1875
- key_weight: bfloat16 [1152, 384], P(('seq', 'dp')), may hold values from -0.1875 to 0.1875
- value_weight: bfloat16 [1152, 384], P(('seq', 'dp')), may hold values from -0.1875 to 0.1875
- output_weight: bfloat16 [1152, 1152], P(('seq', 'dp')), may hold values from -1 to 1
- mlp_norm: float32 [1152], P(('seq', 'dp')), may hold values from 0.1 to 1.9
- gate_weight: bfloat16 [1152, 3072], P(('seq', 'dp')), may hold values from -0.1875 to 0.1875
- up_weight: bfloat16 [1152, 3072], P(('seq', 'dp')), may hold values from -0.1875 to 0.1875
- down_weight: bfloat16 [3072, 1152], P(('seq', 'dp')), may hold values from -0.109375 to 0.109375
- cotangent: bfloat16 [4, 1024, 1152], P('dp', 'seq'), may hold values from -6 to 6
- doc_starts: int32 [4, 8], replicated, may hold values from 0 to 1023, as said below
- keep_mask: int32 [4, 2], replicated, may hold values from 0 to 1, as said below
- keep_rate: float32 [2], replicated, may hold values from 0.5 to 0.9
- seq_order: int32 [4], replicated, may hold values from 0 to 3, each once
Outputs:
- block_output: bfloat16 [4, 1024, 1152], P('dp', 'seq')
- input_grad: float32 [4, 1024, 1152], P('dp', 'seq')
- grad_attn_norm: float32 [1152], P(('seq', 'dp'))
- grad_query: float32 [1152, 1152], P(('seq', 'dp'))
- grad_key: float32 [1152, 384], P(('seq', 'dp'))
- grad_value: float32 [1152, 384], P(('seq', 'dp'))
- grad_output: float32 [1152, 1152], P(('seq', 'dp'))
- grad_mlp_norm: float32 [1152], P(('seq', 'dp'))
- grad_gate: float32 [1152, 3072], P(('seq', 'dp'))
- grad_up: float32 [1152, 3072], P(('seq', 'dp'))
- grad_down: float32 [3072, 1152], P(('seq', 'dp'))
Inputs may be any that keep to these rules, and one draw needn't show every extreme that they name: `doc_starts`: each row lists the starts of 8 documents of one sample in non-decreasing order, the first 0; equal starts are empty documents; every sample has a document of 640 tokens or more. `keep_mask`: column 0 is the attention branch, column 1 the feed-forward branch; column 0 holds both values. `seq_order`: each sample stands once.
All inputs are finite; a program needn't handle non-finite values.
Results may differ from a plain program's by a relative error of at most 0.035.
Values may be sent and summed in bfloat16 or wider, within the bound.
A program may use at most 192 MiB of HBM per device.

v0:
```python
import math

import jax
import jax.numpy as jnp
from jax import lax
from jax.sharding import PartitionSpec as P

H = 18
KV = 6
HD = 64


EPSILON = 1e-05
ROPE_BASE = 10000.0
MASKED = -1e30
FLOOR = -1e29


def normalize(values, gain_vec):
    return (
        values * lax.rsqrt(jnp.mean(values * values, axis=-1, keepdims=True) + EPSILON) * gain_vec
    )


def rotary(vectors, positions):
    half_size = vectors.shape[-1] // 2
    inverse_freq = ROPE_BASE ** (
        -2.0 * jnp.arange(half_size, dtype=jnp.float32) / vectors.shape[-1]
    )
    angles = positions.astype(jnp.float32)[:, None] * inverse_freq[None, :]
    shape_out = (positions.shape[0],) + (1,) * (vectors.ndim - 2) + (half_size,)
    cosine = jnp.cos(angles).reshape(shape_out)
    sine_table = jnp.sin(angles).reshape(shape_out)
    first_half = vectors[..., :half_size]
    second_half = vectors[..., half_size:]
    return jnp.concatenate(
        [
            first_half * cosine - second_half * sine_table,
            second_half * cosine + first_half * sine_table,
        ],
        axis=-1,
    )


def contract_rows(left_rows, right_rows):
    return lax.dot_general(
        left_rows, right_rows, (((0,), (0,)), ((), ())), preferred_element_type=jnp.float32
    )


def contract_cols(left_mat, right_mat):
    return lax.dot_general(
        left_mat, right_mat, (((1,), (1,)), ((), ())), preferred_element_type=jnp.float32
    )


def doc_index(doc_begin, positions):
    return jnp.sum((doc_begin[None, :] <= positions[:, None]).astype(jnp.int32), axis=1) - 1


def shards(
    hidden_in,
    attn_norm,
    query_weight,
    key_weight,
    value_weight,
    output_weight,
    mlp_norm,
    gate_weight,
    up_weight,
    down_weight,
    cotangent,
    doc_starts,
    keep_mask,
    keep_rate,
    seq_order,
):
    tok_rows = hidden_in.shape[1]
    length = tok_rows * lax.axis_size("seq")
    samples = lax.axis_size("dp")
    groups = H // KV
    score_scale = 1.0 / math.sqrt(HD)
    data_pick = jnp.arange(samples) == lax.axis_index("dp")
    sample = jnp.sum(jnp.where(data_pick, seq_order, 0))
    owner_pick = jnp.arange(samples) == sample
    doc_begin = jnp.sum(jnp.where(owner_pick[:, None], doc_starts, 0), axis=0)
    keep_flags = jnp.sum(jnp.where(owner_pick[:, None], keep_mask, 0), axis=0).astype(jnp.float32)
    attn_scale = keep_flags[0] / keep_rate[0]
    mlp_scale = keep_flags[1] / keep_rate[1]
    positions = lax.axis_index("seq") * tok_rows + jnp.arange(tok_rows)
    query_docs = doc_index(doc_begin, positions)
    row_values = hidden_in[0].astype(jnp.float32)
    attn_full = (
        lax.all_gather(attn_norm.astype(jnp.bfloat16), ("seq", "dp"), axis=0, tiled=True).astype(
            attn_norm.dtype
        ),
        lax.all_gather(query_weight, ("seq", "dp"), axis=0, tiled=True),
        lax.all_gather(key_weight, ("seq", "dp"), axis=0, tiled=True),
        lax.all_gather(value_weight, ("seq", "dp"), axis=0, tiled=True),
        lax.all_gather(output_weight, ("seq", "dp"), axis=0, tiled=True),
    )
    norm_one, weight_query, weight_key, weight_value, weight_output = attn_full
    normed_first_f, first_back = jax.vjp(normalize, row_values, norm_one)
    normed_first = normed_first_f.astype(jnp.bfloat16)
    query_pre = jnp.dot(normed_first, weight_query, preferred_element_type=jnp.float32).reshape(
        tok_rows, KV, groups, HD
    )
    key_pre = jnp.dot(normed_first, weight_key, preferred_element_type=jnp.float32).reshape(
        tok_rows, KV, HD
    )
    queries = rotary(query_pre, positions).astype(jnp.bfloat16)
    keys_local = rotary(key_pre, positions).astype(jnp.bfloat16)
    values_local = (
        jnp.dot(normed_first, weight_value, preferred_element_type=jnp.float32)
        .astype(jnp.bfloat16)
        .reshape(tok_rows, KV, HD)
    )

    def allowed_pairs(first_row, count):
        key_pos = first_row + jnp.arange(count)
        key_docs = doc_index(doc_begin, key_pos)
        return (key_pos[None, :] <= positions[:, None]) & (key_docs[None, :] == query_docs[:, None])

    top_old = jnp.full((KV, groups, tok_rows), FLOOR, jnp.float32)
    keys_piece = lax.all_gather(keys_local, "seq", axis=0, tiled=True)
    values_piece = lax.all_gather(values_local, "seq", axis=0, tiled=True)
    allowed = allowed_pairs(jnp.int32(0), keys_piece.shape[0])
    scores = (
        jnp.einsum("tkgd,skd->kgts", queries, keys_piece, preferred_element_type=jnp.float32)
        * score_scale
    )
    scores = jnp.where(allowed, scores, MASKED)
    top_new = jnp.maximum(top_old, jnp.max(scores, axis=-1))
    weights = jnp.exp(scores - top_new[..., None])
    total_new = jnp.sum(weights, axis=-1)
    mixed_new = jnp.einsum(
        "kgts,skd->kgtd",
        weights.astype(jnp.bfloat16),
        values_piece,
        preferred_element_type=jnp.float32,
    )
    log_total = top_new + jnp.log(total_new)
    attended = mixed_new / total_new[..., None]
    attended_low = (
        jnp.transpose(attended, (2, 0, 1, 3)).reshape(tok_rows, H * HD).astype(jnp.bfloat16)
    )
    branch_attn = jnp.dot(attended_low, weight_output, preferred_element_type=jnp.float32)
    middle = row_values + attn_scale * branch_attn
    mlp_full = (
        lax.all_gather(mlp_norm.astype(jnp.bfloat16), ("seq", "dp"), axis=0, tiled=True).astype(
            mlp_norm.dtype
        ),
        lax.all_gather(gate_weight, ("seq", "dp"), axis=0, tiled=True),
        lax.all_gather(up_weight, ("seq", "dp"), axis=0, tiled=True),
        lax.all_gather(down_weight, ("seq", "dp"), axis=0, tiled=True),
    )
    norm_two, weight_gate, weight_up, weight_down = mlp_full
    normed_second_f, second_back = jax.vjp(normalize, middle, norm_two)
    normed_second = normed_second_f.astype(jnp.bfloat16)
    gate_pre = jnp.dot(normed_second, weight_gate, preferred_element_type=jnp.float32)
    up_pre = jnp.dot(normed_second, weight_up, preferred_element_type=jnp.float32)
    gate_act, silu_back = jax.vjp(jax.nn.silu, gate_pre)
    activated = (gate_act * up_pre).astype(jnp.bfloat16)
    branch_mlp = jnp.dot(activated, weight_down, preferred_element_type=jnp.float32)
    block_output = (middle + mlp_scale * branch_mlp).astype(jnp.bfloat16)[None]
    grad_out = cotangent[0].astype(jnp.float32)
    back_gate, back_up, back_down = (
        lax.all_gather(gate_weight, ("seq", "dp"), axis=0, tiled=True),
        lax.all_gather(up_weight, ("seq", "dp"), axis=0, tiled=True),
        lax.all_gather(down_weight, ("seq", "dp"), axis=0, tiled=True),
    )
    grad_down_in = (mlp_scale * grad_out).astype(jnp.bfloat16)
    grad_down_w = contract_rows(activated, grad_down_in)
    grad_activated = contract_cols(grad_down_in, back_down)
    grad_gate_in = silu_back(grad_activated * up_pre)[0].astype(jnp.bfloat16)
    grad_up_in = (grad_activated * gate_act).astype(jnp.bfloat16)
    grad_gate_w = contract_rows(normed_second, grad_gate_in)
    grad_up_w = contract_rows(normed_second, grad_up_in)
    grad_normed_second = contract_cols(grad_gate_in, back_gate) + contract_cols(grad_up_in, back_up)
    grad_middle_part, grad_norm_two = second_back(grad_normed_second)
    grad_middle = grad_out + grad_middle_part
    mlp_sums = (
        lax.psum_scatter(grad_norm_two, ("seq", "dp"), scatter_dimension=0, tiled=True),
        lax.psum_scatter(grad_gate_w, ("seq", "dp"), scatter_dimension=0, tiled=True),
        lax.psum_scatter(grad_up_w, ("seq", "dp"), scatter_dimension=0, tiled=True),
        lax.psum_scatter(grad_down_w, ("seq", "dp"), scatter_dimension=0, tiled=True),
    )
    back_query, back_key, back_value, back_output = (
        lax.all_gather(query_weight, ("seq", "dp"), axis=0, tiled=True),
        lax.all_gather(key_weight, ("seq", "dp"), axis=0, tiled=True),
        lax.all_gather(value_weight, ("seq", "dp"), axis=0, tiled=True),
        lax.all_gather(output_weight, ("seq", "dp"), axis=0, tiled=True),
    )
    grad_branch_attn = (attn_scale * grad_middle).astype(jnp.bfloat16)
    grad_output_w = contract_rows(attended_low, grad_branch_attn)
    grad_attended = contract_cols(grad_branch_attn, back_output).astype(jnp.bfloat16)
    grad_heads = grad_attended.reshape(tok_rows, KV, groups, HD)
    row_delta = jnp.einsum("tkgd,kgtd->kgt", grad_heads.astype(jnp.float32), attended)
    gathered_keys, gathered_values = (
        lax.all_gather(keys_local, "seq", axis=0, tiled=True),
        lax.all_gather(values_local, "seq", axis=0, tiled=True),
    )
    block_rows = min(512, length)
    block_count = length // block_rows
    key_blocks = gathered_keys.reshape(block_count, block_rows, KV, HD)
    value_blocks = gathered_values.reshape(block_count, block_rows, KV, HD)

    def back_block(grad_query_acc, inputs):
        block_index, keys_block, values_block = inputs
        allowed = allowed_pairs(block_index * block_rows, block_rows)
        scores = (
            jnp.einsum("tkgd,skd->kgts", queries, keys_block, preferred_element_type=jnp.float32)
            * score_scale
        )
        weights = jnp.where(allowed, jnp.exp(scores - log_total[..., None]), 0.0)
        grad_weights = jnp.einsum(
            "tkgd,skd->kgts", grad_heads, values_block, preferred_element_type=jnp.float32
        )
        grad_scores = (weights * (grad_weights - row_delta[..., None])).astype(jnp.bfloat16)
        grad_query_acc = grad_query_acc + jnp.einsum(
            "kgts,skd->tkgd", grad_scores, keys_block, preferred_element_type=jnp.float32
        )
        grad_keys_block = (
            jnp.einsum("kgts,tkgd->skd", grad_scores, queries, preferred_element_type=jnp.float32)
            * score_scale
        )
        grad_values_block = jnp.einsum(
            "kgts,tkgd->skd",
            weights.astype(jnp.bfloat16),
            grad_heads,
            preferred_element_type=jnp.float32,
        )
        return (grad_query_acc, jnp.stack([grad_keys_block, grad_values_block], axis=1))

    grad_queries, kv_terms = lax.scan(
        back_block,
        jnp.zeros((tok_rows, KV, groups, HD), jnp.float32),
        (jnp.arange(block_count), key_blocks, value_blocks),
    )
    kv_terms = kv_terms.reshape(length, 2, KV, HD)
    kv_sums = lax.psum_scatter(
        kv_terms.astype(jnp.bfloat16), "seq", scatter_dimension=0, tiled=True
    ).astype(jnp.float32)

    def rotate_local(vectors):
        return rotary(vectors, positions)

    grad_query_in = (
        jax.vjp(rotate_local, query_pre)[1](grad_queries * score_scale)[0]
        .reshape(tok_rows, H * HD)
        .astype(jnp.bfloat16)
    )
    grad_key_in = (
        jax.vjp(rotate_local, key_pre)[1](kv_sums[:, 0])[0]
        .reshape(tok_rows, KV * HD)
        .astype(jnp.bfloat16)
    )
    grad_value_in = kv_sums[:, 1].reshape(tok_rows, KV * HD).astype(jnp.bfloat16)
    grad_query_w = contract_rows(normed_first, grad_query_in)
    grad_key_w = contract_rows(normed_first, grad_key_in)
    grad_value_w = contract_rows(normed_first, grad_value_in)
    grad_normed_first = (
        contract_cols(grad_query_in, back_query)
        + contract_cols(grad_key_in, back_key)
        + contract_cols(grad_value_in, back_value)
    )
    grad_rows_part, grad_norm_one = first_back(grad_normed_first)
    input_grad = (grad_middle + grad_rows_part)[None]
    attn_sums = (
        lax.psum_scatter(grad_norm_one, ("seq", "dp"), scatter_dimension=0, tiled=True),
        lax.psum_scatter(grad_query_w, ("seq", "dp"), scatter_dimension=0, tiled=True),
        lax.psum_scatter(grad_key_w, ("seq", "dp"), scatter_dimension=0, tiled=True),
        lax.psum_scatter(grad_value_w, ("seq", "dp"), scatter_dimension=0, tiled=True),
        lax.psum_scatter(grad_output_w, ("seq", "dp"), scatter_dimension=0, tiled=True),
    )
    return (
        block_output,
        input_grad,
        attn_sums[0],
        attn_sums[1],
        attn_sums[2],
        attn_sums[3],
        attn_sums[4],
        mlp_sums[0],
        mlp_sums[1],
        mlp_sums[2],
        mlp_sums[3],
    )


def solution(mesh):
    placed = (
        P("dp", "seq", None),
        P(("seq", "dp")),
        P(("seq", "dp"), None),
        P(("seq", "dp"), None),
        P(("seq", "dp"), None),
        P(("seq", "dp"), None),
        P(("seq", "dp")),
        P(("seq", "dp"), None),
        P(("seq", "dp"), None),
        P(("seq", "dp"), None),
        P("dp", "seq", None),
        P(),
        P(),
        P(),
        P(),
    )
    return jax.shard_map(
        shards,
        mesh=mesh,
        in_specs=placed,
        out_specs=(
            P("dp", "seq", None),
            P("dp", "seq", None),
            P(("seq", "dp")),
            P(("seq", "dp"), None),
            P(("seq", "dp"), None),
            P(("seq", "dp"), None),
            P(("seq", "dp"), None),
            P(("seq", "dp")),
            P(("seq", "dp"), None),
            P(("seq", "dp"), None),
            P(("seq", "dp"), None),
        ),
        check_vma=False,
    )
```

profile of v0, /device:TPU:0, one launch (start us, length us, event | category | flops | bytes accessed | tf_op | source)
XLA Modules:
  0.0 1806.0 jit_solution(16777772165942618157)
XLA Ops:
  15.2 42.1 %all-reduce.21 = (bf16[1152]{0:T(1024)(128)(2,1)S(1)}, bf16[1152]{0:T(1024)(128)(2,1)S(1)}) all-reduce(bf16[1152]{0:T(1024)(128)(2,1)S(1)} %dynamic-update-slice, bf16[1152]{0:T(1024)(128)(2,1)S(1)} %dynamic-update-slice.1), channel_id=1, replica_groups=mesh['seq'=8,'dp'=4] {'seq','dp'}, use_global_device_ids=true, to_apply=%add.4 | all-reduce | flops 2304 | bytes 9216
  57.3 73.9 %all-gather = bf16[32,36,384]{2,1,0:T(8,128)(2,1)S(1)} all-gather(bf16[1,36,384]{2,1,0:T(8,128)(2,1)} %bitcast.287), channel_id=1, replica_groups=mesh['seq'=8,'dp'=4] {'seq','dp'}, dimensions={0}, use_global_device_ids=true | all-gather | bytes 912384 | tf_op jit(solution)/shard_map/all_gather | solution.py:98
  133.2 15.0 all_gather.44
  149.2 73.5 %all-gather.2 = bf16[32,36,384]{2,1,0:T(8,128)(2,1)S(1)} all-gather(bf16[1,36,384]{2,1,0:T(8,128)(2,1)S(1)} %bitcast.288), channel_id=1, replica_groups=mesh['seq'=8,'dp'=4] {'seq','dp'}, dimensions={0}, use_global_device_ids=true | all-gather | bytes 912384 | tf_op jit(solution)/shard_map/all_gather | solution.py:99
  225.6 17.1 all_gather.47
  254.8 5.1 reshape.327
  271.2 9.1 reshape.329
  280.3 19.3 %all-gather.20.cloned.1.call-done = bf16[32,36,3072]{2,1,0:T(8,128)(2,1)} async-done(((bf16[1,36,3072]{2,1,0:T(8,128)(2,1)}), bf16[32,36,3072]{2,1,0:T(8,128)(2,1)}) %all-gather.20.cloned.1.call-update) | async-done | bytes 7077904 | tf_op jit(solution)/shard_map/all_gather | solution.py:154
  299.6 9.2 reshape.331
  308.9 5.7 fusion.103
  318.1 55.5 %all-gather.12.cloned.1.call-done = bf16[3072,1152]{1,0:T(8,128)(2,1)} async-done(((bf16[96,1152]{1,0:T(8,128)(2,1)}), bf16[3072,1152]{1,0:T(8,128)(2,1)}) %all-gather.12.cloned.1.call-update) | async-done | bytes 7077904 | tf_op jit(solution)/shard_map/all_gather | solution.py:155
  373.6 7.5 multiply_convert_fusion
  383.5 6.4 multiply_reduce_fusion
  392.5 15.7 while.15
  408.2 6.1 copy.91
  414.3 6.3 reshape.343
  420.9 7.1 fusion.83
  435.1 7.0 fusion.107
  442.1 7.1 fusion.106
  457.9 1056.4 %fusion.99 = (f32[48,1152]{1,0:T(8,128)S(1)}, f32[48,384]{1,0:T(8,128)S(1)}, f32[48,384]{1,0:T(8,128)S(1)}, f32[48,1152]{1,0:T(8,128)S(1)}, f32[40,3072]{1,0:T(8,128)}, /*index=5*/f32[40,3072]{1,0:T(8,128)}) fusion(f32[1152,1152]{1,0:T(8,128)} %fusion.75, f32[1152,384]{1,0:T(8,128)} %fusion.77, f32[1152,384]{1,0:T(8,128)} %fusion.79, ...), kind=kCustom, calls=%all-reduce-scatter.6 | all-reduce-scatter fusion | flops 12582914 | bytes 44040192
  1514.3 19.6 %collective-permute-start.14 = (f32[48,384]{1,0:T(8,128)S(1)}, f32[48,384]{1,0:T(8,128)S(1)}, u32[]{:S(2)}, u32[]{:S(2)}) collective-permute-start(f32[48,384]{1,0:T(8,128)S(1)} %get-tuple-element.313), channel_id=1, source_target_pairs={{0,7},{1,8},{2,9},{3,10},{4,11},{5,12},{6,13},{7,14},{8,15},{9,16}... | collective-permute-start | bytes 221192
  1533.9 17.1 collective-permute-start.13
  1557.0 5.6 collective-permute-start.15
  1619.2 5.4 collective-permute-start.2
  1646.5 6.2 collective-permute-start.25
  1664.5 50.5 %all-reduce.20 = (f32[1152]{0:T(1024)S(1)}, f32[1152]{0:T(1024)S(1)}) all-reduce(f32[1152]{0:T(1024)S(1)} %get-tuple-element.274, f32[1152]{0:T(1024)S(1)} %copy-done.65), channel_id=3, replica_groups=mesh['seq'=8,'dp'=4] {'seq','dp'}, use_global_device_ids=true, to_apply=%region_16.17.clone | all-reduce | flops 2304 | bytes 18432
  1717.2 5.7 concatenate.11
  1722.9 7.2 concatenate.12
  1743.9 9.2 concatenate.10
  1753.2 14.6 concatenate.13
  1773.9 8.9 concatenate.14
  1782.9 13.4 concatenate.15
  (376 shorter events, 192.8 us)
Async XLA Ops:
  7.2 240.4 %all-gather.14.cloned.1.call-start = ((), (), s32[]{:S(2)}) async-start(), calls=%async_computation.4 | async-start | bytes 3041280 | tf_op jit(solution)/shard_map/all_gather | solution.py:97
  7.9 246.9 %all-gather.16.cloned.1.call-start = ((), (), s32[]{:S(2)}) async-start(), calls=%async_computation.5 | async-start | bytes 3041280 | tf_op jit(solution)/shard_map/all_gather | solution.py:100
  8.7 262.5 %all-gather.18.cloned.1.call-start = ((), (), s32[]{:S(2)}) async-start(), calls=%async_computation.6 | async-start | bytes 8110080 | tf_op jit(solution)/shard_map/all_gather | solution.py:153
  9.4 290.2 %all-gather.20.cloned.1.call-start = ((), (), s32[]{:S(2)}) async-start(), calls=%async_computation.7 | async-start | bytes 8110080 | tf_op jit(solution)/shard_map/all_gather | solution.py:154
  10.0 363.6 %all-gather.12.cloned.1.call-start = ((), (), s32[]{:S(2)}) async-start(), calls=%async_computation.2 | async-start | bytes 7299072 | tf_op jit(solution)/shard_map/all_gather | solution.py:155
  10.6 442.7 %reduce-scatter.19.cloned.1.call-start = ((), (), s32[]{:S(2)}) async-start(), calls=%async_computation.8 | async-start | bytes 1769472
  420.6 1378.3 %reduce-scatter.17.cloned.1.call-start = ((), (), s32[]{:S(2)}) async-start(), calls=%async_computation.3 | async-start | bytes 14598144 | tf_op jit(solution)/shard_map/reduce_scatter | solution.py:186
  1514.3 62.8 %collective-permute-start.14 = (f32[48,384]{1,0:T(8,128)S(1)}, f32[48,384]{1,0:T(8,128)S(1)}, u32[]{:S(2)}, u32[]{:S(2)}) collective-permute-start(f32[48,384]{1,0:T(8,128)S(1)} %get-tuple-element.313), channel_id=1, source_target_pairs={{0,7},{1,8},{2,9},{3,10},{4,11},{5,12},{6,13},{7,14},{8,15},{9,16}... | collective-permute-start | bytes 221192
  1533.9 46.4 %collective-permute-start.13 = (f32[48,384]{1,0:T(8,128)S(1)}, f32[48,384]{1,0:T(8,128)S(1)}, u32[]{:S(2)}, u32[]{:S(2)}) collective-permute-start(f32[48,384]{1,0:T(8,128)S(1)} %get-tuple-element.313), channel_id=1, source_target_pairs={{0,6},{1,7},{2,8},{3,9},{4,10},{5,11},{6,12},{7,13},{8,14},{9,15},... | collective-permute-start | bytes 221192
  1551.6 19.0 %collective-permute-start.23 = (f32[36,384]{1,0:T(8,128)}, f32[36,384]{1,0:T(8,128)}, u32[]{:S(2)}, u32[]{:S(2)}) collective-permute-start(f32[36,384]{1,0:T(8,128)} %slice.48), channel_id=1, source_target_pairs={{0,8},{1,9},{2,10},{3,11},{4,12},{5,13},{6,14},{7,15},{8,16},{9,17... | collective-permute-start | bytes 165896
  1557.0 17.8 collective-permute-start.15
  1566.6 20.9 %collective-permute-start.12 = (f32[48,384]{1,0:T(8,128)S(1)}, f32[48,384]{1,0:T(8,128)S(1)}, u32[]{:S(2)}, u32[]{:S(2)}) collective-permute-start(f32[48,384]{1,0:T(8,128)S(1)} %get-tuple-element.313), channel_id=1, source_target_pairs={{0,5},{1,6},{2,7},{3,8},{4,9},{5,10},{6,11},{7,12},{8,13},{9,14},{... | collective-permute-start | bytes 221192
  1570.7 20.7 %collective-permute-start.11 = (f32[48,384]{1,0:T(8,128)S(1)}, f32[48,384]{1,0:T(8,128)S(1)}, u32[]{:S(2)}, u32[]{:S(2)}) collective-permute-start(f32[48,384]{1,0:T(8,128)S(1)} %get-tuple-element.313), channel_id=1, source_target_pairs={{0,4},{1,5},{2,6},{3,7},{4,8},{5,9},{6,10},{7,11},{8,12},{9,13},{1... | collective-permute-start | bytes 221192
  1574.8 17.9 collective-permute-start.10
  1577.1 18.5 %collective-permute-start.9 = (f32[48,384]{1,0:T(8,128)S(1)}, f32[48,384]{1,0:T(8,128)S(1)}, u32[]{:S(2)}, u32[]{:S(2)}) collective-permute-start(f32[48,384]{1,0:T(8,128)S(1)} %get-tuple-element.313), channel_id=1, source_target_pairs={{0,2},{1,3},{2,4},{3,5},{4,6},{5,7},{6,8},{7,9},{8,10},{9,11},{10,... | collective-permute-start | bytes 221192
  1580.3 16.7 collective-permute-start.8
  1606.8 17.9 collective-permute-start.6
  1614.0 17.9 collective-permute-start.4
  1616.3 19.7 %collective-permute-start.3 = (f32[48,1152]{1,0:T(8,128)S(1)}, f32[48,1152]{1,0:T(8,128)S(1)}, u32[]{:S(2)}, u32[]{:S(2)}) collective-permute-start(f32[48,1152]{1,0:T(8,128)S(1)} %get-tuple-element.312), channel_id=1, source_target_pairs={{0,4},{1,5},{2,6},{3,7},{4,8},{5,9},{6,10},{7,11},{8,12},{9,13},{1... | collective-permute-start | bytes 663560
  1619.2 18.4 %collective-permute-start.2 = (f32[48,1152]{1,0:T(8,128)S(1)}, f32[48,1152]{1,0:T(8,128)S(1)}, u32[]{:S(2)}, u32[]{:S(2)}) collective-permute-start(f32[48,1152]{1,0:T(8,128)S(1)} %get-tuple-element.312), channel_id=1, source_target_pairs={{0,3},{1,4},{2,5},{3,6},{4,7},{5,8},{6,9},{7,10},{8,11},{9,12},{10... | collective-permute-start | bytes 663560
  1636.0 16.7 collective-permute-start.29
  1637.6 17.1 collective-permute-start.28
  1640.4 19.2 %collective-permute-start.27 = (f32[48,1152]{1,0:T(8,128)S(1)}, f32[48,1152]{1,0:T(8,128)S(1)}, u32[]{:S(2)}, u32[]{:S(2)}) collective-permute-start(f32[48,1152]{1,0:T(8,128)S(1)} %get-tuple-element.315), channel_id=1, source_target_pairs={{0,4},{1,5},{2,6},{3,7},{4,8},{5,9},{6,10},{7,11},{8,12},{9,13},{1... | collective-permute-start | bytes 663560
  1642.2 88.6 %collective-permute-start.26 = (f32[48,1152]{1,0:T(8,128)S(1)}, f32[48,1152]{1,0:T(8,128)}, u32[]{:S(2)}, u32[]{:S(2)}) collective-permute-start(f32[48,1152]{1,0:T(8,128)S(1)} %get-tuple-element.315), channel_id=1, source_target_pairs={{0,3},{1,4},{2,5},{3,6},{4,7},{5,8},{6,9},{7,10},{8,11},{9,12},{10... | collective-permute-start | bytes 663560
  1646.5 89.3 %collective-permute-start.25 = (f32[48,1152]{1,0:T(8,128)S(1)}, f32[48,1152]{1,0:T(8,128)}, u32[]{:S(2)}, u32[]{:S(2)}) collective-permute-start(f32[48,1152]{1,0:T(8,128)S(1)} %get-tuple-element.315), channel_id=1, source_target_pairs={{0,2},{1,3},{2,4},{3,5},{4,6},{5,7},{6,8},{7,9},{8,10},{9,11},{10,... | collective-permute-start | bytes 663560
  1652.7 84.4 %collective-permute-start.24 = (f32[48,1152]{1,0:T(8,128)S(1)}, f32[48,1152]{1,0:T(8,128)}, u32[]{:S(2)}, u32[]{:S(2)}) collective-permute-start(f32[48,1152]{1,0:T(8,128)S(1)} %get-tuple-element.315), channel_id=1, source_target_pairs={{0,1},{1,2},{2,3},{3,4},{4,5},{5,6},{6,7},{7,8},{8,9},{9,10},{10,1... | collective-permute-start | bytes 663560
  1654.7 84.8 %collective-permute-start.34 = (f32[40,3072]{1,0:T(8,128)}, f32[40,3072]{1,0:T(8,128)}, u32[]{:S(2)}, u32[]{:S(2)}) collective-permute-start(f32[40,3072]{1,0:T(8,128)} %get-tuple-element.316), channel_id=1, source_target_pairs={{0,3},{1,4},{2,5},{3,6},{4,7},{5,8},{6,9},{7,10},{8,11},{9,12},{10... | collective-permute-start | bytes 1474568
  1659.6 108.9 %collective-permute-start.33 = (f32[40,3072]{1,0:T(8,128)}, f32[40,3072]{1,0:T(8,128)}, u32[]{:S(2)}, u32[]{:S(2)}) collective-permute-start(f32[40,3072]{1,0:T(8,128)} %get-tuple-element.316), channel_id=1, source_target_pairs={{0,2},{1,3},{2,4},{3,5},{4,6},{5,7},{6,8},{7,9},{8,10},{9,11},{10,... | collective-permute-start | bytes 1474568
  1730.8 43.1 %collective-permute-start.32 = (f32[40,3072]{1,0:T(8,128)}, f32[40,3072]{1,0:T(8,128)}, u32[]{:S(2)}, u32[]{:S(2)}) collective-permute-start(f32[40,3072]{1,0:T(8,128)} %get-tuple-element.316), channel_id=1, source_target_pairs={{0,1},{1,2},{2,3},{3,4},{4,5},{5,6},{6,7},{7,8},{8,9},{9,10},{10,1... | collective-permute-start | bytes 1474568
  1735.8 47.1 %collective-permute-start.38 = (f32[40,3072]{1,0:T(8,128)}, f32[40,3072]{1,0:T(8,128)S(1)}, u32[]{:S(2)}, u32[]{:S(2)}) collective-permute-start(f32[40,3072]{1,0:T(8,128)} %get-tuple-element.317), channel_id=1, source_target_pairs={{0,3},{1,4},{2,5},{3,6},{4,7},{5,8},{6,9},{7,10},{8,11},{9,12},{10... | collective-permute-start | bytes 1474568
  1737.1 45.7 %collective-permute-start.37 = (f32[40,3072]{1,0:T(8,128)}, f32[40,3072]{1,0:T(8,128)}, u32[]{:S(2)}, u32[]{:S(2)}) collective-permute-start(f32[40,3072]{1,0:T(8,128)} %get-tuple-element.317), channel_id=1, source_target_pairs={{0,2},{1,3},{2,4},{3,5},{4,6},{5,7},{6,8},{7,9},{8,10},{9,11},{10,... | collective-permute-start | bytes 1474568
  1739.5 43.3 %collective-permute-start.36 = (f32[40,3072]{1,0:T(8,128)}, f32[40,3072]{1,0:T(8,128)}, u32[]{:S(2)}, u32[]{:S(2)}) collective-permute-start(f32[40,3072]{1,0:T(8,128)} %get-tuple-element.317), channel_id=1, source_target_pairs={{0,1},{1,2},{2,3},{3,4},{4,5},{5,6},{6,7},{7,8},{8,9},{9,10},{10,1... | collective-permute-start | bytes 1474568
  (98 other events, 4481.4 us)
Sparse Core Ops, SparseCore 0:
  10.9 62.4 all-gather.13
  76.4 59.4 all-gather.15
  138.7 82.6 all-gather.17
  224.1 75.4 all-gather.19
  302.4 71.1 all-gather.11
  420.8 32.4 reduce-scatter.18
  459.8 201.6 reduce-scatter.16
where the time goes:
time: 1820 us; the launch traced here: 1810 us
  blocking collectives  1330 us (73%)
  starting transfers between devices  154 us (8%)
  local copies, waits for them, and re-layouts  125 us (7%)
  matrix products  84.1 us (5%)
  waiting for transfers between devices  83.6 us (5%)
  between operations  18.6 us (1%)
    unnamed x3, blocking collectives  1150 us
    unnamed x41, starting transfers between devices  153 us
    unnamed x187, local copies, waits for them, and re-layouts  113 us
    all_gather x1, blocking collectives, shards(): lax.all_gather(key_weight, ('seq', 'dp'), axis=0, tiled=True)  73.9 us
    all_gather x1, blocking collectives, shards(): lax.all_gather(value_weight, ('seq', 'dp'), axis=0, tiled=True)  73.5 us
    all_gather x1, waiting for transfers between devices, shards(): lax.all_gather(down_weight, ('seq', 'dp'), axis=0, tiled=True)  55.5 us
  transfers between devices with their start and end apart: 47, of which 5 were waited for; matrix products, arithmetic and copies ran while one was open for 68% of the time, Pallas kernels for 0%

commit v1 on v0

v1 whole, which is shorter than its diff:
```python
import math

import jax
import jax.numpy as jnp
from jax import lax
from jax.sharding import PartitionSpec as P

H = 18
KV = 6
HD = 64


EPSILON = 1e-05
ROPE_BASE = 10000.0
MASKED = -1e30


def contract_rows(left_rows, right_rows):
    return lax.dot_general(
        left_rows, right_rows, (((0,), (0,)), ((), ())), preferred_element_type=jnp.float32
    )


def contract_cols(left_mat, right_mat):
    return lax.dot_general(
        left_mat, right_mat, (((1,), (1,)), ((), ())), preferred_element_type=jnp.float32
    )


def low(v):
    return v.astype(jnp.bfloat16)


def dot(a, b):
    return jnp.dot(a, b, preferred_element_type=jnp.float32)


def swap_halves(vectors):
    half = HD // 2
    return jnp.concatenate([vectors[..., half:], vectors[..., :half]], axis=-1)


def shards(
    hidden_in,
    attn_norm,
    query_weight,
    key_weight,
    value_weight,
    output_weight,
    mlp_norm,
    gate_weight,
    up_weight,
    down_weight,
    cotangent,
    doc_starts,
    keep_mask,
    keep_rate,
    seq_order,
):
    tok = hidden_in.shape[1]
    ns, nd = lax.axis_size("seq"), lax.axis_size("dp")
    length = tok * ns
    rows = query_weight.shape[0]
    ffr = down_weight.shape[0]
    dim = hidden_in.shape[2]
    groups = H // KV
    nq, nk = H * HD, KV * HD
    score_scale = 1.0 / math.sqrt(HD)
    me_s, me_d = lax.axis_index("seq"), lax.axis_index("dp")
    sample = jnp.sum(jnp.where(jnp.arange(nd) == me_d, seq_order, 0))
    pick = jnp.arange(nd) == sample
    doc_begin = jnp.sum(jnp.where(pick[:, None], doc_starts, 0), axis=0)
    keep_flags = jnp.sum(jnp.where(pick[:, None], keep_mask, 0), axis=0).astype(jnp.float32)
    attn_scale = keep_flags[0] / keep_rate[0]
    mlp_scale = keep_flags[1] / keep_rate[1]
    positions = me_s * tok + jnp.arange(tok)
    first = jnp.max(jnp.where(doc_begin[None, :] <= positions[:, None], doc_begin[None, :], 0), axis=1)
    gain_one, gain_two = attn_norm[:, None], mlp_norm[:, None]

    qkv_rows = low(jnp.concatenate([query_weight, key_weight, value_weight], axis=1).astype(jnp.float32) * gain_one)
    w_qkv = lax.all_gather(qkv_rows, ("seq", "dp"), axis=0, tiled=True)
    w_out = lax.all_gather(output_weight, ("seq", "dp"), axis=0, tiled=True)

    def split_hidden(w):
        w = low(w.astype(jnp.float32) * gain_two).reshape(rows, ns, nd, ffr)
        w = jnp.transpose(w, (0, 2, 1, 3)).reshape(rows, nd * ns * ffr)
        return w

    gu = jnp.concatenate(
        [split_hidden(gate_weight).reshape(rows, nd, -1), split_hidden(up_weight).reshape(rows, nd, -1)], axis=2
    )
    gu = lax.all_to_all(gu, "dp", split_axis=1, concat_axis=0, tiled=True).reshape(nd * rows, -1)
    w_gu = lax.all_gather(gu, "seq", axis=0, tiled=True)
    w_down = lax.all_gather(down_weight, "seq", axis=0, tiled=True)
    hid = w_down.shape[0]

    x = hidden_in[0].astype(jnp.float32)
    r_one = lax.rsqrt(jnp.mean(x * x, axis=-1, keepdims=True) + EPSILON)
    xn = low(x * r_one)
    qkv = dot(xn, w_qkv)
    inverse_freq = ROPE_BASE ** (-2.0 * jnp.arange(HD // 2, dtype=jnp.float32) / HD)
    angles = positions.astype(jnp.float32)[:, None] * inverse_freq[None, :]
    cosine = jnp.tile(jnp.cos(angles), (1, 2))[:, None, :]
    sine = jnp.concatenate([-jnp.sin(angles), jnp.sin(angles)], axis=1)[:, None, :]

    def turn(v):
        return v * cosine + swap_halves(v) * sine

    def turn_back(v):
        return v * cosine - swap_halves(v) * sine

    queries = low(turn(qkv[:, :nq].reshape(tok, H, HD))).reshape(tok, KV, groups, HD)
    keys = low(turn(qkv[:, nq : nq + nk].reshape(tok, KV, HD)))
    kv = jnp.concatenate([keys.reshape(tok, nk), low(qkv[:, nq + nk :])], axis=1)
    kv_all = lax.all_gather(kv, "seq", axis=0, tiled=True)
    k_all, v_all = kv_all[:, :nk].reshape(length, KV, HD), kv_all[:, nk:].reshape(length, KV, HD)
    key_pos = jnp.arange(length)
    allowed = (key_pos[None, :] <= positions[:, None]) & (key_pos[None, :] >= first[:, None])
    scores = jnp.einsum("tkgd,skd->kgts", queries, k_all, preferred_element_type=jnp.float32) * score_scale
    scores = jnp.where(allowed, scores, MASKED)
    expo = jnp.exp(scores - jnp.max(scores, axis=-1, keepdims=True))
    probs = low(expo / jnp.sum(expo, axis=-1, keepdims=True))
    attended = jnp.einsum("kgts,skd->tkgd", probs, v_all, preferred_element_type=jnp.float32)
    att = low(attended.reshape(tok, nq))
    middle = x + attn_scale * dot(att, w_out)
    r_two = lax.rsqrt(jnp.mean(middle * middle, axis=-1, keepdims=True) + EPSILON)
    mn = low(middle * r_two)

    cot = cotangent[0].astype(jnp.float32)
    side = lax.all_gather(jnp.concatenate([xn, low(mlp_scale * cot), att], axis=1), "dp", axis=0, tiled=True)
    xn_all, gd_all, att_all = side[:, :dim], side[:, dim : 2 * dim], side[:, 2 * dim :]
    mn_all = lax.all_gather(mn, "dp", axis=0, tiled=True)
    gate, up = dot(mn_all, w_gu[:, :hid]), dot(mn_all, w_gu[:, hid:])
    sig = jax.nn.sigmoid(gate)
    act_gate = gate * sig
    act = low(act_gate * up)
    g_act = contract_cols(gd_all, w_down)
    gg = low(g_act * up * (sig * (1.0 + gate * (1.0 - sig))))
    gu_in = low(g_act * act_gate)
    gboth = jnp.concatenate([gg, gu_in], axis=1)
    g_mn = lax.psum_scatter(low(contract_cols(gboth, w_gu)), "dp", scatter_dimension=0, tiled=True).astype(jnp.float32)
    branch = lax.psum_scatter(low(dot(act, w_down)), "dp", scatter_dimension=0, tiled=True).astype(jnp.float32)
    block_output = low(middle + mlp_scale * branch)[None]
    m_gu = lax.psum_scatter(low(contract_rows(mn_all, gboth)), "seq", scatter_dimension=0, tiled=True)
    m_down = lax.psum_scatter(low(contract_rows(act, gd_all)), "seq", scatter_dimension=0, tiled=True)

    def norm_back(e, v, r):
        return r * e - v * (r * r * r) * jnp.mean(e * v, axis=-1, keepdims=True)

    g_mid = cot + norm_back(g_mn, middle, r_two)
    gba = low(attn_scale * g_mid)
    g_att = low(contract_cols(gba, w_out)).reshape(tok, KV, groups, HD)
    g_probs = jnp.einsum("tkgd,skd->kgts", g_att, v_all, preferred_element_type=jnp.float32)
    delta = jnp.einsum("tkgd,tkgd->kgt", g_att.astype(jnp.float32), attended)
    g_scores = low(probs.astype(jnp.float32) * (g_probs - delta[..., None]))
    g_q = jnp.einsum("kgts,skd->tkgd", g_scores, k_all, preferred_element_type=jnp.float32) * score_scale
    g_k = jnp.einsum("kgts,tkgd->skd", g_scores, queries, preferred_element_type=jnp.float32) * score_scale
    g_v = jnp.einsum("kgts,tkgd->skd", probs, g_att, preferred_element_type=jnp.float32)
    g_kv = low(jnp.concatenate([g_k.reshape(length, nk), g_v.reshape(length, nk)], axis=1))
    g_kv = lax.psum_scatter(g_kv, "seq", scatter_dimension=0, tiled=True).astype(jnp.float32)
    g_q_in = low(turn_back(g_q.reshape(tok, H, HD))).reshape(tok, nq)
    g_k_in = low(turn_back(g_kv[:, :nk].reshape(tok, KV, HD))).reshape(tok, nk)
    g_qkv = jnp.concatenate([g_q_in, g_k_in, low(g_kv[:, nk:])], axis=1)
    g_xn = contract_cols(g_qkv, w_qkv)
    input_grad = (g_mid + norm_back(g_xn, x, r_one))[None]

    cut = jnp.concatenate([g_qkv.reshape(tok, nd, -1), gba.reshape(tok, nd, -1)], axis=2)
    wq = g_qkv.shape[1] // nd
    cut = lax.all_to_all(cut, "dp", split_axis=1, concat_axis=0, tiled=True).reshape(nd * tok, -1)
    m_att = jnp.concatenate([contract_rows(xn_all, cut[:, :wq]), contract_rows(att_all, cut[:, wq:])], axis=1)
    m_att = lax.psum_scatter(low(m_att), "seq", scatter_dimension=0, tiled=True)

    back = jnp.concatenate([m_gu, m_att], axis=1)
    back = lax.all_to_all(back.reshape(nd, rows, 1, -1), "dp", split_axis=0, concat_axis=2, tiled=True)
    back = back.reshape(rows, nd, -1).astype(jnp.float32)

    def whole_hidden(m):
        return jnp.transpose(m.reshape(rows, nd, ns, ffr), (0, 2, 1, 3)).reshape(rows, -1)

    m_gate, m_up = whole_hidden(back[:, :, :hid]), whole_hidden(back[:, :, hid : 2 * hid])
    m_qkv = back[:, :, 2 * hid : 2 * hid + wq].reshape(rows, -1)
    g_out = back[:, :, 2 * hid + wq :].reshape(rows, -1)

    def weigh(w, m):
        return jnp.sum(w.astype(jnp.float32) * m, axis=1)

    m_q, m_k, m_v = m_qkv[:, :nq], m_qkv[:, nq : nq + nk], m_qkv[:, nq + nk :]
    g_norm_one = weigh(query_weight, m_q) + weigh(key_weight, m_k) + weigh(value_weight, m_v)
    g_norm_two = weigh(gate_weight, m_gate) + weigh(up_weight, m_up)
    return (
        block_output,
        input_grad,
        g_norm_one,
        m_q * gain_one,
        m_k * gain_one,
        m_v * gain_one,
        g_out,
        g_norm_two,
        m_gate * gain_two,
        m_up * gain_two,
        m_down.astype(jnp.float32),
    )


def solution(mesh):
    placed = (
        P("dp", "seq", None),
        P(("seq", "dp")),
        P(("seq", "dp"), None),
        P(("seq", "dp"), None),
        P(("seq", "dp"), None),
        P(("seq", "dp"), None),
        P(("seq", "dp")),
        P(("seq", "dp"), None),
        P(("seq", "dp"), None),
        P(("seq", "dp"), None),
        P("dp", "seq", None),
        P(),
        P(),
        P(),
        P(),
    )
    return jax.shard_map(
        shards,
        mesh=mesh,
        in_specs=placed,
        out_specs=(
            P("dp", "seq", None),
            P("dp", "seq", None),
            P(("seq", "dp")),
            P(("seq", "dp"), None),
            P(("seq", "dp"), None),
            P(("seq", "dp"), None),
            P(("seq", "dp"), None),
            P(("seq", "dp")),
            P(("seq", "dp"), None),
            P(("seq", "dp"), None),
            P(("seq", "dp"), None),
        ),
        check_vma=False,
    )
```

time: 1820 us -> 573 us (0.31)
  blocking collectives: 1330 us -> 23.2 us
  waiting for transfers between devices: 83.6 us -> 386 us
  starting transfers between devices: 154 us -> 4.43 us
  local copies, waits for them, and re-layouts: 125 us -> 46.4 us
  matrix products: 84.1 us -> 63.3 us
  other arithmetic: 11.1 us -> 30.6 us
    unnamed x3 -> x0, blocking collectives: 1150 us -> none
    all_gather x4 -> x0, blocking collectives: 180 us -> none  [the longest x1 73.9 us: shards(): lax.all_gather(key_weight, ('seq', 'dp'), axis=0, tiled=True)]
    unnamed x41 -> x1, starting transfers between devices: 153 us -> 0.04 us
    all_gather x5 -> x7, waiting for transfers between devices: 74.9 us -> 226 us  [the longest x1 66 us: shards(): w_qkv = lax.all_gather(qkv_rows, ('seq', 'dp'), axis=0, tiled=True)]
    reduce_scatter x1 -> x5, waiting for transfers between devices: 0.01 us -> 140 us  [the longest x1 38.7 us: shards(): lax.psum_scatter(low(contract_rows(mn_all, gboth)), 'seq', scatter_dimens...]
    unnamed x187 -> x104, local copies, waits for them, and re-layouts: 113 us -> 23 us
    all_to_all x0 -> x2, blocking collectives: none -> 23.2 us  [the longest x1 11.8 us: shards(): lax.all_to_all(cut, 'dp', split_axis=1, concat_axis=0, tiled=True)]
  transfers between devices with their start and end apart: 47 -> 14, of which waited for: 5 -> 13; matrix products, arithmetic and copies ran while one was open for 68% -> 17% of each run, Pallas kernels for 0% -> 0%
where the time goes in v1:
time: 573 us; the launch traced here: 571 us
  waiting for transfers between devices  386 us (67%)
  matrix products  63.3 us (11%)
  local copies, waits for them, and re-layouts  46.4 us (8%)
  other arithmetic  30.6 us (5%)
  blocking collectives  23.2 us (4%)
  between operations  17.5 us (3%)
    all_gather x1, waiting for transfers between devices, shards(): w_qkv = lax.all_gather(qkv_rows, ('seq', 'dp'), axis=0, tiled=True)  66 us
    all_gather x1, waiting for transfers between devices, shards(): lax.all_gather(jnp.concatenate([xn, low(mlp_scale * cot), att], axis=1),...  48.7 us
    reduce_scatter x1, waiting for transfers between devices, shards(): lax.psum_scatter(low(contract_rows(mn_all, gboth)), 'seq', scatter_dimens...  38.7 us
    reduce_scatter x1, waiting for transfers between devices, shards(): m_att = lax.psum_scatter(low(m_att), 'seq', scatter_dimension=0, tiled=True)  35.7 us
    all_gather x1, waiting for transfers between devices, shards(): w_out = lax.all_gather(output_weight, ('seq', 'dp'), axis=0, tiled=True)  30.4 us
    reduce_scatter x1, waiting for transfers between devices, shards(): lax.psum_scatter(low(contract_cols(gboth, w_gu)), 'dp', scatter_dimension...  28.6 us
    all_gather x1, waiting for transfers between devices, shards(): mn_all = lax.all_gather(mn, 'dp', axis=0, tiled=True)  28.3 us
    reduce_scatter x1, waiting for transfers between devices, shards(): lax.psum_scatter(low(dot(act, w_down)), 'dp', scatter_dimension=0, tiled=...  27.2 us
  transfers between devices with their start and end apart: 14, of which 13 were waited for; matrix products, arithmetic and copies ran while one was open for 17% of the time, Pallas kernels for 0%

profile of v1, /device:TPU:0, one launch (start us, length us, event | category | flops | bytes accessed | tf_op | source)
XLA Modules:
  0.0 571.4 jit_solution(3864397169084149112)
XLA Ops:
  12.6 66.0 %all-gather.20.cloned.1.call-done = bf16[32,36,1920]{2,1,0:T(8,128)(2,1)} async-done(((bf16[1,36,1920]{2,1,0:T(8,128)(2,1)}), bf16[32,36,1920]{2,1,0:T(8,128)(2,1)}) %all-gather.20.cloned.1.call-update) | async-done | bytes 4423696 | tf_op jit(solution)/shard_map/all_gather | solution.py:81
  78.6 7.1 %reshape.251 = bf16[1152,1920]{1,0:T(8,128)(2,1)} reshape(bf16[32,36,1920]{2,1,0:T(8,128)(2,1)} %all-gather.20.cloned.1.call-done) | data formatting | bytes 8847360
  85.7 3.1 fusion.64
  92.1 11.4 %all_to_all.39 = bf16[36,4,1536]{2,0,1:T(8,128)(2,1)S(1)} all-to-all(bf16[36,4,1536]{2,0,1:T(8,128)(2,1)S(1)} %copy.191), channel_id=1, replica_groups=mesh['seq'=8,'dp'=4] {'dp'}, dimensions={1} | all-to-all | bytes 884736 | tf_op jit(solution)/shard_map/all_to_all | solution.py:92
  108.7 30.4 %all-gather.22.cloned.1.call-done = bf16[32,36,1152]{2,1,0:T(8,128)(2,1)} async-done(((bf16[1,36,1152]{2,1,0:T(8,128)(2,1)}), bf16[32,36,1152]{2,1,0:T(8,128)(2,1)}) %all-gather.22.cloned.1.call-update) | async-done | bytes 2654224 | tf_op jit(solution)/shard_map/all_gather | solution.py:82
  139.2 3.6 reshape.253
  147.6 17.6 %all-gather.10.cloned.1.call-done = bf16[1024,768]{1,0:T(8,128)(2,1)} async-done(((bf16[128,768]{1,0:T(8,128)(2,1)}), bf16[1024,768]{1,0:T(8,128)(2,1)}) %all-gather.10.cloned.1.call-update) | async-done | bytes 1572880 | tf_op jit(solution)/shard_map/all_gather | solution.py:115
  172.6 7.8 %fusion.63 = (f32[6,3,128]{2,1,0:T(4,128)S(1)}, f32[6,3,128,1024]{2,3,1,0:T(8,128)}) fusion(pred[128,1024]{0,1:T(8,128)(4,1)S(1)} %copy-done.30, bf16[1024,6,64,1]{0,2,3,1:T(8,128)(2,1)} %bitcast.177, bf16[128,6,3,64]{0,3,2,1:T(8,128)(2,1)S(1)} %copy-done.14), kind=kOutput, calls=%fused_computation.147 | convolution fusion | flops 311428096 | bytes 10658816 | tf_op jit(solution)/shard_map/sub | solution.py:121
  180.4 5.0 divide_convert_fusion
  197.4 11.0 %all-gather.14.cloned.1.call-done = bf16[1152,1536]{1,0:T(8,128)(2,1)} async-done(((bf16[144,1536]{1,0:T(8,128)(2,1)}), bf16[1152,1536]{1,0:T(8,128)(2,1)}) %all-gather.14.cloned.1.call-update) | async-done | bytes 3538960 | tf_op jit(solution)/shard_map/all_gather | solution.py:93
  208.4 28.3 %all-gather.12.cloned.1.call-done = bf16[512,1152]{1,0:T(8,128)(2,1)} async-done(((bf16[128,1152]{1,0:T(8,128)(2,1)}), bf16[512,1152]{1,0:T(8,128)(2,1)}) %all-gather.12.cloned.1.call-update) | async-done | bytes 1179664 | tf_op jit(solution)/shard_map/all_gather | solution.py:132
  236.7 4.2 fusion.10
  240.9 23.7 %all-gather.16.cloned.1.call-done = bf16[768,1152]{1,0:T(8,128)(2,1)} async-done(((bf16[96,1152]{1,0:T(8,128)(2,1)}), bf16[768,1152]{1,0:T(8,128)(2,1)}) %all-gather.16.cloned.1.call-update) | async-done | bytes 1769488 | tf_op jit(solution)/shard_map/all_gather | solution.py:94
  264.6 48.7 %all-gather.18.cloned.1.call-done = bf16[512,3456]{1,0:T(8,128)(2,1)} async-done(((bf16[128,3456]{1,0:T(8,128)(2,1)}), bf16[512,3456]{1,0:T(8,128)(2,1)}) %all-gather.18.cloned.1.call-update) | async-done | bytes 3538960 | tf_op jit(solution)/shard_map/all_gather | solution.py:130
  313.3 3.2 fusion.19
  316.5 4.1 multiply_convert_fusion.1
  321.8 3.3 convolution_convert_fusion.2
  325.2 28.6 %reduce-scatter.13.cloned.1.call-done = bf16[128,1152]{1,0:T(8,128)(2,1)} async-done(((bf16[512,1152]{1,0:T(8,128)(2,1)}), bf16[128,1152]{1,0:T(8,128)(2,1)}) %reduce-scatter.13.cloned.1.call-update) | async-done | bytes 294928 | tf_op jit(solution)/shard_map/reduce_scatter | solution.py:141
  359.8 4.0 bitcast_convert_fusion
  363.9 4.0 fusion.2
  371.9 3.7 convolution_convert_fusion.1
  376.9 5.3 convolution_convert_fusion
  383.4 3.3 convolution_multiply_fusion.1
  387.5 18.8 %reduce-scatter.19.cloned.1.call-done = bf16[128,768]{1,0:T(8,128)(2,1)} async-done(((bf16[1024,768]{1,0:T(8,128)(2,1)}), bf16[128,768]{1,0:T(8,128)(2,1)}) %reduce-scatter.19.cloned.1.call-update) | async-done | bytes 196624
  408.1 11.8 %all_to_all.40 = bf16[128,4,768]{0,2,1:T(8,128)(2,1)S(1)} all-to-all(bf16[128,4,768]{0,2,1:T(8,128)(2,1)S(1)} %pad_maximum_fusion.6), channel_id=1, replica_groups=mesh['seq'=8,'dp'=4] {'dp'}, dimensions={1} | all-to-all | bytes 1572864 | tf_op jit(solution)/shard_map/all_to_all | solution.py:169
  428.4 3.4 convolution_convert_fusion.3
  431.7 9.7 %reduce-scatter.17.cloned.1.call-done = bf16[96,1152]{1,0:T(8,128)(2,1)} async-done(((bf16[768,1152]{1,0:T(8,128)(2,1)}), bf16[96,1152]{1,0:T(8,128)(2,1)}) %reduce-scatter.17.cloned.1.call-update) | async-done | bytes 221200 | tf_op jit(solution)/shard_map/reduce_scatter | solution.py:145
  443.1 3.7 fusion.30
  446.9 38.7 %reduce-scatter.15.cloned.1.call-done = bf16[144,1536]{1,0:T(8,128)(2,1)} async-done(((bf16[1152,1536]{1,0:T(8,128)(2,1)}), bf16[144,1536]{1,0:T(8,128)(2,1)}) %reduce-scatter.15.cloned.1.call-update) | async-done | bytes 442384 | tf_op jit(solution)/shard_map/reduce_scatter | solution.py:144
  485.6 35.7 %reduce-scatter.21.cloned.1.call-done = bf16[144,768]{1,0:T(8,128)(2,1)} async-done(((bf16[1152,768]{1,0:T(8,128)(2,1)}), bf16[144,768]{1,0:T(8,128)(2,1)}) %reduce-scatter.21.cloned.1.call-update) | async-done | bytes 221200 | tf_op jit(solution)/shard_map/reduce_scatter | solution.py:171
  523.5 3.5 all-to-all-start.2
  527.0 27.2 %reduce-scatter.11.cloned.1.call-done = bf16[128,1152]{1,0:T(8,128)(2,1)} async-done(((bf16[512,1152]{1,0:T(8,128)(2,1)}), bf16[128,1152]{1,0:T(8,128)(2,1)}) %reduce-scatter.11.cloned.1.call-update) | async-done | bytes 294928 | tf_op jit(solution)/shard_map/reduce_scatter | solution.py:142
  (228 shorter events, 73.9 us)
Async XLA Ops:
  7.2 5.3 copy-start.4
  7.2 71.4 %all-gather.20.cloned.1.call-start = ((), (), s32[]{:S(2)}) async-start(), calls=%async_computation.18 | async-start | bytes 5068800 | tf_op jit(solution)/shard_map/all_gather | solution.py:81
  9.0 130.2 %all-gather.22.cloned.1.call-start = ((), (), s32[]{:S(2)}) async-start(), calls=%async_computation.19 | async-start | bytes 3041280 | tf_op jit(solution)/shard_map/all_gather | solution.py:82
  9.7 155.5 %all-gather.10.cloned.1.call-start = ((), (), s32[]{:S(2)}) async-start(), calls=%async_computation.9 | async-start | bytes 1769472 | tf_op jit(solution)/shard_map/all_gather | solution.py:115
  10.8 78.3 %copy-start.26 = (f32[128,64]{0,1:T(8,128)}, f32[128,64]{0,1:T(8,128)S(1)}, u32[]{:S(2)}) copy-start(f32[128,64]{0,1:T(8,128)S(1)} %pad_maximum_fusion.11) | copy-start | bytes 98308
  12.5 73.2 %copy-start.37 = (f32[128]{0:T(128)}, f32[128]{0:T(128)S(1)}, u32[]{:S(2)}) copy-start(f32[128]{0:T(128)S(1)} %get-tuple-element.48) | copy-start | bytes 1540
  12.6 73.1 %copy-start.10 = (bf16[128,1152]{1,0:T(8,128)(2,1)}, bf16[128,1152]{1,0:T(8,128)(2,1)S(1)}, u32[]{:S(2)}) copy-start(bf16[128,1152]{1,0:T(8,128)(2,1)S(1)} %fusion.25) | copy-start | bytes 884740
  90.0 118.4 %all-gather.14.cloned.1.call-start = ((), (), s32[]{:S(2)}) async-start(), calls=%async_computation.11 | async-start | bytes 3981312 | tf_op jit(solution)/shard_map/all_gather | solution.py:93
  92.0 12.4 %copy-start.45 = (s32[4]{0:T(128)S(1)}, s32[4]{0:T(128)}, u32[]{:S(2)}) copy-start(s32[4]{0:T(128)} %param.29) | copy-start | bytes 52
  92.0 13.7 %copy-start.39 = (s32[4,2]{0,1:T(2,128)S(1)}, s32[4,2]{0,1:T(2,128)}, u32[]{:S(2)}) copy-start(s32[4,2]{0,1:T(2,128)} %param.27) | copy-start | bytes 100
  92.0 13.8 %copy-start.36 = (f32[2]{0:T(128)S(1)}, f32[2]{0:T(128)}, u32[]{:S(2)}) copy-start(f32[2]{0:T(128)} %param.28) | copy-start | bytes 28
  92.0 15.8 %copy-start.35 = (s32[4,8]{1,0:T(4,128)S(1)}, s32[4,8]{1,0:T(4,128)}, u32[]{:S(2)}) copy-start(s32[4,8]{1,0:T(4,128)} %param.26) | copy-start | bytes 388
  104.4 132.4 %all-gather.12.cloned.1.call-start = ((), (), s32[]{:S(2)}) async-start(), calls=%async_computation.10 | async-start | bytes 1474560 | tf_op jit(solution)/shard_map/all_gather | solution.py:132
  167.9 4.7 copy-start.30
  180.4 5.1 copy-start.2
  189.4 75.2 %all-gather.16.cloned.1.call-start = ((), (), s32[]{:S(2)}) async-start(), calls=%async_computation.12 | async-start | bytes 1990656 | tf_op jit(solution)/shard_map/all_gather | solution.py:94
  190.0 123.3 %all-gather.18.cloned.1.call-start = ((), (), s32[]{:S(2)}) async-start(), calls=%async_computation.14 | async-start | bytes 4423680 | tf_op jit(solution)/shard_map/all_gather | solution.py:130
  197.1 156.7 %reduce-scatter.13.cloned.1.call-start = ((), (), s32[]{:S(2)}) async-start(), calls=%async_computation.15 | async-start | bytes 1474560 | tf_op jit(solution)/shard_map/reduce_scatter | solution.py:141
  325.1 81.1 %reduce-scatter.19.cloned.1.call-start = ((), (), s32[]{:S(2)}) async-start(), calls=%async_computation.20 | async-start | bytes 1769472
  371.8 69.5 %reduce-scatter.17.cloned.1.call-start = ((), (), s32[]{:S(2)}) async-start(), calls=%async_computation.17 | async-start | bytes 1990656 | tf_op jit(solution)/shard_map/reduce_scatter | solution.py:145
  375.6 110.0 %reduce-scatter.15.cloned.1.call-start = ((), (), s32[]{:S(2)}) async-start(), calls=%async_computation.16 | async-start | bytes 3981312 | tf_op jit(solution)/shard_map/reduce_scatter | solution.py:144
  382.2 139.1 %reduce-scatter.21.cloned.1.call-start = ((), (), s32[]{:S(2)}) async-start(), calls=%async_computation.21 | async-start | bytes 1990656 | tf_op jit(solution)/shard_map/reduce_scatter | solution.py:171
  386.7 20.8 %copy-start.28 = (f32[128,64]{0,1:T(8,128)S(1)}, f32[128,64]{0,1:T(8,128)}, u32[]{:S(2)}) copy-start(f32[128,64]{0,1:T(8,128)} %copy-done.26) | copy-start | bytes 98308
  407.6 12.4 %copy-start.22 = (bf16[128,384]{0,1:T(8,128)(2,1)}, bf16[128,384]{0,1:T(8,128)(2,1)S(1)}, u32[]{:S(2)}) copy-start(bf16[128,384]{0,1:T(8,128)(2,1)S(1)} %fusion.44) | copy-start | bytes 294916
  426.9 127.4 %reduce-scatter.11.cloned.1.call-start = ((), (), s32[]{:S(2)}) async-start(), calls=%async_computation.13 | async-start | bytes 1474560 | tf_op jit(solution)/shard_map/reduce_scatter | solution.py:142
  431.7 11.4 %copy-start.21 = (bf16[128,384]{0,1:T(8,128)(2,1)S(1)}, bf16[128,384]{0,1:T(8,128)(2,1)}, u32[]{:S(2)}) copy-start(bf16[128,384]{0,1:T(8,128)(2,1)} %copy-done.20) | copy-start | bytes 294916
  431.7 11.4 %copy-start.23 = (bf16[128,384]{0,1:T(8,128)(2,1)S(1)}, bf16[128,384]{0,1:T(8,128)(2,1)}, u32[]{:S(2)}) copy-start(bf16[128,384]{0,1:T(8,128)(2,1)} %copy-done.22) | copy-start | bytes 294916
  522.5 31.8 %copy-start.9 = (bf16[128,1152]{1,0:T(8,128)(2,1)S(1)}, bf16[128,1152]{1,0:T(8,128)(2,1)}, u32[]{:S(2)}) copy-start(bf16[128,1152]{1,0:T(8,128)(2,1)} %reduce-scatter.13.cloned.1.call-done) | copy-start | bytes 884740
  522.5 31.8 %copy-start.13 = (bf16[1,128,1152]{2,1,0:T(8,128)(2,1)S(1)}, bf16[1,128,1152]{2,1,0:T(8,128)(2,1)}, u32[]{:S(2)}) copy-start(bf16[1,128,1152]{2,1,0:T(8,128)(2,1)} %param.25) | copy-start | bytes 884740
  522.5 31.8 %copy-start.38 = (f32[128]{0:T(128)S(1)}, f32[128]{0:T(128)}, u32[]{:S(2)}) copy-start(f32[128]{0:T(128)} %copy-done.37) | copy-start | bytes 1540
  522.5 31.7 %copy-start.40 = (f32[128]{0:T(128)S(1)}, f32[128]{0:T(128)}, u32[]{:S(2)}) copy-start(f32[128]{0:T(128)} %get-tuple-element.47) | copy-start | bytes 1540
  523.5 32.9 %all-to-all-start.2 = ((bf16[4,36,1,2304]{3,1,2,0:T(8,128)(2,1)}), bf16[4,36,1,2304]{3,1,2,0:T(8,128)(2,1)S(1)}, u32[]{:S(2)}, u32[]{:S(2)}) async-start(bf16[4,36,1,2304]{3,1,2,0:T(8,128)(2,1)} %bitcast.63), calls=%async_computation.5 | async-start | bytes 1474560 | tf_op jit(solution)/shard_map/all_to_all | solution.py:174
  (31 other events, 55.4 us)
Sparse Core Ops, SparseCore 0:
  11.5 67.0 all-gather.19
  81.5 57.6 all-gather.21
  141.4 23.7 all-gather.9
  167.3 41.0 all-gather.13
  210.1 26.5 all-gather.11
  238.2 26.3 all-gather.15
  266.5 46.7 all-gather.17
  325.2 28.5 reduce-scatter.12
  372.0 34.2 reduce-scatter.18
  408.4 32.9 reduce-scatter.16
  443.7 41.8 reduce-scatter.14
  487.9 33.3 reduce-scatter.20
  524.5 29.7 reduce-scatter.10

commit v2 on v1

--- a/solution.py
+++ b/solution.py
@@ -3,6 +3,8 @@
 import jax
 import jax.numpy as jnp
 from jax import lax
+from jax.experimental import pallas as pl
+from jax.experimental.pallas import tpu as pltpu
 from jax.sharding import PartitionSpec as P
 
 H = 18
@@ -202,6 +204,530 @@
     )
 
 
+MESH = pl.DeviceIdType.MESH
+LIMIT = 60 * 2**20
+BF, F32 = jnp.bfloat16, jnp.float32
+
+
+def dot_nn(a, b):
+    return lax.dot_general(a, b, (((1,), (0,)), ((), ())), preferred_element_type=F32)
+
+
+def dot_nt(a, b):
+    return lax.dot_general(a, b, (((1,), (1,)), ((), ())), preferred_element_type=F32)
+
+
+def dot_tn(a, b):
+    return lax.dot_general(a, b, (((0,), (0,)), ((), ())), preferred_element_type=F32)
+
+
+class Net:
+    def __init__(self, sends, recvs):
+        self.sends, self.recvs, self.count, self.open = sends, recvs, 0, []
+        self.s, self.d = lax.axis_index("seq"), lax.axis_index("dp")
+        self.z, self.c = lax.div(self.s, 2), lax.rem(self.s, 2)
+        y, x = lax.div(self.d, 2), lax.rem(self.d, 2)
+        self.plane = (y * 2 + 1 - x, (1 - y) * 2 + x, 3 - self.d)
+        self.mate = self.at(self.z, 1 - self.c)
+
+    def at(self, z, core):
+        return {"seq": z * 2 + core, "dp": self.d}
+
+    def across(self, kind):
+        return {"seq": self.s, "dp": self.plane[kind]}
+
+    def greet(self):
+        barrier = pltpu.get_barrier_semaphore()
+        peers = [self.mate] + [self.across(k) for k in range(3)]
+        peers += [self.at(lax.rem(self.z + k, 4), self.c) for k in (1, 2, 3)]
+        for peer in peers:
+            pl.semaphore_signal(barrier, inc=1, device_id=peer, device_id_type=MESH)
+        pl.semaphore_wait(barrier, len(peers))
+
+    def copy(self, src, dst, send, recv, peer):
+        return pltpu.make_async_remote_copy(
+            src_ref=src,
+            dst_ref=dst,
+            send_sem=self.sends.at[send],
+            recv_sem=self.recvs.at[recv],
+            device_id=peer,
+            device_id_type=MESH,
+        )
+
+    def push(self, src, dst, recv, peer, when=None):
+        copy = self.copy(src, dst, self.count, recv, peer)
+        self.count += 1
+        if when is None:
+            copy.start()
+        else:
+            pl.when(when)(copy.start)
+        self.open.append((copy, when))
+
+    def arrive(self, dst, recv, when=None):
+        copy = self.copy(dst, dst, 0, recv, self.mate)
+        if when is None:
+            copy.wait_recv()
+        else:
+            pl.when(when)(copy.wait_recv)
+
+    def finish(self):
+        for copy, when in self.open:
+            if when is None:
+                copy.wait_send()
+            else:
+                pl.when(when)(copy.wait_send)
+        self.open = []
+
+    def order(self, step):
+        if step == 0:
+            return self.z
+        table = ((1, 0, 3, 2), (2, 2, 1, 1), (3, 3, 0, 0))[step - 1]
+        z = self.z
+        return jnp.where(z == 0, table[0], jnp.where(z == 1, table[1], jnp.where(z == 2, table[2], table[3])))
+
+
+class Chain:
+    def __init__(self, net, block, base):
+        self.net, self.block, self.base = net, block, base
+
+    def start(self):
+        net = self.net
+        own = self.block(net.z, net.c)
+        net.push(own, own, self.base + net.z, net.at(net.z + 1, net.c), net.z < 3)
+        net.push(own, own, self.base + net.z, net.at(net.z - 1, net.c), net.z > 0)
+
+    def step(self, k):
+        net = self.net
+        b = net.order(k)
+        block = self.block(b, net.c)
+        net.arrive(block, self.base + b)
+        to = jnp.where(b < net.z, net.z + 1, net.z - 1)
+        net.push(block, block, self.base + b, net.at(to, net.c), (to >= 0) & (to <= 3))
+
+
+class Lines(Chain):
+    def start(self):
+        super().start()
+        self.give(0)
+
+    def give(self, k):
+        net = self.net
+        b = net.order(k)
+        block = self.block(b, net.c)
+        net.push(block, block, self.base + 4 + b, net.mate)
+
+    def take(self):
+        net = self.net
+        for b in range(4):
+            net.arrive(self.block(b, 1 - net.c), self.base + 4 + b)
+
+
+class Slices(Chain):
+    def __init__(self, net, full, rows, base):
+        self.full, self.rows, self.half = full, rows, full.shape[2] // 2
+        super().__init__(net, lambda z, core: self.part(net.d, z, core), base)
+
+    def part(self, slot, z, core, cols=slice(None)):
+        first = pl.multiple_of((z * 2 + core) * self.rows, 16)
+        return self.full.at[slot, pl.ds(first, self.rows), cols]
+
+    def spread(self, k):
+        net = self.net
+        b = net.order(k)
+        block = self.part(net.d, b, net.c)
+        net.push(block, block, self.base + 4 + b, net.across(0))
+        net.push(block, block, self.base + 8 + b, net.across(1))
+        net.push(block, block, self.base + 20 + b, net.mate)
+
+    def pass_on(self, k):
+        net = self.net
+        b = net.order(k)
+        for kind in (0, 1):
+            block = self.part(net.plane[kind], b, net.c)
+            net.arrive(block, self.base + 4 + 4 * kind + b)
+            half = self.part(net.plane[kind], b, net.c, pl.ds(kind * self.half, self.half))
+            net.push(half, half, self.base + 12 + 4 * kind + b, net.across(1 - kind))
+            net.push(block, block, self.base + 24 + 4 * kind + b, net.mate)
+
+    def corner(self, k):
+        net = self.net
+        b = net.order(k)
+        for kind in (0, 1):
+            half = self.part(net.plane[2], b, net.c, pl.ds(kind * self.half, self.half))
+            net.arrive(half, self.base + 12 + 4 * kind + b)
+        block = self.part(net.plane[2], b, net.c)
+        net.push(block, block, self.base + 32 + b, net.mate)
+
+    def take(self):
+        net = self.net
+        for b in range(4):
+            net.arrive(self.part(net.d, b, 1 - net.c), self.base + 20 + b)
+            for kind in range(3):
+                net.arrive(self.part(net.plane[kind], b, 1 - net.c), self.base + 24 + 4 * kind + b)
+
+
+def exchange(net, send, land, base):
+    for kind in range(3):
+        net.push(send.at[net.plane[kind]], land.at[net.d], base + kind, net.across(kind))
+    land[net.d] = send[net.d]
+
+
+def settle(net, land, wide, rows, base):
+    for kind in range(3):
+        net.arrive(land.at[net.plane[kind]], base + kind)
+    for j in range(4):
+        wide[pl.ds(j * rows, rows), : land.shape[2]] = land[j, :rows, :].astype(F32)
+
+
+def share(net, full, base):
+    for kind in range(3):
+        net.push(full.at[net.d], full.at[net.d], base + kind, net.across(kind))
+
+
+def shared(net, full, base):
+    for kind in range(3):
+        net.arrive(full.at[net.plane[kind]], base + kind)
+
+
+def turned(tile, cosine, sine):
+    lane = lax.broadcasted_iota(jnp.int32, tile.shape, 1)
+    other = jnp.where(lax.rem(lane, HD) < HD // 2, pltpu.roll(tile, 128 - HD // 2, 1), pltpu.roll(tile, HD // 2, 1))
+    return tile * cosine + other * sine
+
+
+def front_kernel(
+    x_in, cot_in, first_in, scale_in, cos_in, sin_in, att_send, gu_send, down,
+    wa, wb, wgu, wd, xn_all, gd_all, mn_all, q_heads, k_heads, v_heads, probs, att, middle,
+    att_land, gu_land, wide, kv_all, o_heads, bias, sends, recvs,
+):
+    net = Net(sends, recvs)
+    tok, dim = x_in.shape[1], x_in.shape[2]
+    rows = dim // 32
+    blk = 4 * rows
+    ffr = down.shape[0]
+    d, z, c, s = net.d, net.z, net.c, net.s
+
+    a = Slices(net, wa, blk, 16)
+    b = Slices(net, wb, blk, 56)
+    gu = Lines(net, lambda zz, core: wgu.at[pl.ds(pl.multiple_of((zz * 2 + core) * blk, 16), blk)], 96)
+    dn = Lines(net, lambda zz, core: wd.at[pl.ds(pl.multiple_of((zz * 2 + core) * ffr, 16), ffr)], 104)
+    kv = Lines(net, lambda zz, core: kv_all.at[zz * 2 + core], 112)
+
+    net.greet()
+    exchange(net, att_send, att_land, 0)
+    x = x_in[0].astype(F32)
+    xn = (x * lax.rsqrt(jnp.mean(x * x, axis=1, keepdims=True) + EPSILON)).astype(BF)
+    xn_all[d] = xn
+    gd_all[d] = (cot_in[0].astype(F32) * scale_in[1:2, 0:1]).astype(BF)
+    wd[pl.ds(pl.multiple_of(s * ffr, 16), ffr), :] = down[...]
+    settle(net, att_land, wide, rows, 0)
+    own = pl.ds(pl.multiple_of(s * blk, 16), blk)
+    wa[d, own, :] = wide[:, :512].astype(BF)
+    wb[d, own, :] = wide[:, 512:768].astype(BF)
+    a.start()
+    a.spread(0)
+    exchange(net, gu_send, gu_land, 3)
+    dn.start()
+    b.start()
+    a.step(1)
+    a.spread(1)
+    a.pass_on(0)
+    b.spread(0)
+    a.step(2)
+    a.spread(2)
+    a.pass_on(1)
+    a.corner(0)
+    settle(net, gu_land, wide, rows, 3)
+    wgu[own, :] = wide[...].astype(BF)
+    gu.start()
+    a.step(3)
+    a.spread(3)
+    a.pass_on(2)
+    a.corner(1)
+    b.step(1)
+    b.spread(1)
+    a.pass_on(3)
+    a.corner(2)
+    b.step(2)
+    b.spread(2)
+    a.corner(3)
+    a.take()
+
+    cosine, sine = cos_in[...], sin_in[...]
+    for j in range(4):
+        part = dot_nn(xn, wa[j])
+        for i in range(4):
+            t = 4 * j + i
+            if t == 15:
+                continue
+            tile = part[:, 128 * i : 128 * i + 128]
+            if t < 12:
+                tile = turned(tile, cosine, sine)
+            if t < 9:
+                tile = (tile * (1.0 / math.sqrt(HD))).astype(BF)
+                q_heads[2 * t] = tile[:, :HD]
+                q_heads[2 * t + 1] = tile[:, HD:]
+            else:
+                kv_all[s, :, pl.ds(128 * (t - 9), 128)] = tile.astype(BF)
+    kv.start()
+    share(net, gd_all, 8)
+    b.step(3)
+    b.spread(3)
+
+    position = s * tok + lax.broadcasted_iota(jnp.int32, (tok, 1), 0)
+    key = lax.broadcasted_iota(jnp.int32, bias.shape, 1)
+    bias[...] = jnp.where((key <= position) & (key >= first_in[:, 0:1]), 0.0, MASKED)
+
+    for k in range(3):
+        b.pass_on(k)
+    b.corner(0)
+    b.corner(1)
+    for k in (1, 2, 3):
+        kv.step(k)
+        kv.give(k)
+        if k == 1:
+            dn.step(1)
+            dn.give(1)
+            b.pass_on(3)
+        if k == 2:
+            gu.step(1)
+            gu.give(1)
+            b.corner(2)
+    kv.take()
+    share(net, xn_all, 11)
+    for j in range(8):
+        for k in range(KV):
+            k_heads[k, pl.ds(tok * j, tok), :] = kv_all[j, :, HD * k : HD * k + HD]
+            v_heads[k, pl.ds(tok * j, tok), :] = kv_all[j, :, HD * (KV + k) : HD * (KV + k) + HD]
+
+    def head(h, carry):
+        k = lax.div(h, H // KV)
+        score = dot_nt(q_heads[h], k_heads[k]) + bias[...]
+        expo = jnp.exp(score - jnp.max(score, axis=1, keepdims=True))
+        p = (expo / jnp.sum(expo, axis=1, keepdims=True)).astype(BF)
+        probs[h] = p
+        o_heads[h] = dot_nn(p, v_heads[k])
+        return carry
+
+    lax.fori_loop(0, 6, head, 0)
+    dn.step(2)
+    dn.give(2)
+    b.corner(3)
+    b.take()
+    lax.fori_loop(6, 12, head, 0)
+    gu.step(2)
+    gu.give(2)
+    lax.fori_loop(12, 18, head, 0)
+    for j in range(H // 2):
+        att[:, 128 * j : 128 * j + 128] = jnp.concatenate([o_heads[2 * j], o_heads[2 * j + 1]], axis=1).astype(BF)
+    full = att[...]
+    branch = [dot_nn(full, wb[j]) for j in range(4)] + [dot_nn(full, wa[3, :, 384:])]
+    mid = x_in[0].astype(F32) + scale_in[0:1, 0:1] * jnp.concatenate(branch, axis=1)
+    middle[...] = mid
+    mn_all[d] = (mid * lax.rsqrt(jnp.mean(mid * mid, axis=1, keepdims=True) + EPSILON)).astype(BF)
+    share(net, mn_all, 120)
+    dn.step(3)
+    dn.give(3)
+    gu.step(3)
+    gu.give(3)
+    shared(net, gd_all, 8)
+    shared(net, xn_all, 11)
+    dn.take()
+    gu.take()
+    shared(net, mn_all, 120)
+    net.finish()
+
+
+def front(x, cot, first, scale, cosine, sine, att_send, gu_send, down):
+    tok, dim = x.shape[1:]
+    ns = 8
+    length = tok * ns
+    hid = down.shape[0] * ns
+    vm = pl.BlockSpec(memory_space=pltpu.VMEM)
+    outs = [
+        ((4, dim, 512), BF),
+        ((4, dim, 256), BF),
+        ((dim, 2 * hid), BF),
+        ((hid, dim), BF),
+        ((4, tok, dim), BF),
+        ((4, tok, dim), BF),
+        ((4, tok, dim), BF),
+        ((H, tok, HD), BF),
+        ((KV, length, HD), BF),
+        ((KV, length, HD), BF),
+        ((H, tok, length), BF),
+        ((tok, H * HD), BF),
+        ((tok, dim), F32),
+    ]
+    return pl.pallas_call(
+        front_kernel,
+        out_shape=[jax.ShapeDtypeStruct(*o) for o in outs],
+        in_specs=[vm] * 9,
+        out_specs=[vm] * len(outs),
+        scratch_shapes=[
+            pltpu.VMEM(att_send.shape, BF),
+            pltpu.VMEM(gu_send.shape, BF),
+            pltpu.VMEM((dim // 8, 2 * hid), F32),
+            pltpu.VMEM((ns, tok, 2 * KV * HD), BF),
+            pltpu.VMEM((H, tok, HD), F32),
+            pltpu.VMEM((tok, length), F32),
+            pltpu.SemaphoreType.DMA((160,)),
+            pltpu.SemaphoreType.DMA((128,)),
+        ],
+        compiler_params=pltpu.CompilerParams(collective_id=0, has_side_effects=True, vmem_limit_bytes=LIMIT),
+        name="k_front",
+    )(x, cot, first, scale, cosine, sine, att_send, gu_send, down)
+
+
+def shards_by_kernels(
+    hidden_in,
+    attn_norm,
+    query_weight,
+    key_weight,
+    value_weight,
+    output_weight,
+    mlp_norm,
+    gate_weight,
+    up_weight,
+    down_weight,
+    cotangent,
+    doc_starts,
+    keep_mask,
+    keep_rate,
+    seq_order,
+):
+    tok = hidden_in.shape[1]
+    ns, nd = lax.axis_size("seq"), lax.axis_size("dp")
+    length = tok * ns
+    rows = query_weight.shape[0]
+    ffr = down_weight.shape[0]
+    dim = hidden_in.shape[2]
+    groups = H // KV
+    nq, nk = H * HD, KV * HD
+    score_scale = 1.0 / math.sqrt(HD)
+    me_s, me_d = lax.axis_index("seq"), lax.axis_index("dp")
+    sample = jnp.sum(jnp.where(jnp.arange(nd) == me_d, seq_order, 0))
+    pick = jnp.arange(nd) == sample
+    doc_begin = jnp.sum(jnp.where(pick[:, None], doc_starts, 0), axis=0)
+    keep_flags = jnp.sum(jnp.where(pick[:, None], keep_mask, 0), axis=0).astype(jnp.float32)
+    attn_scale = keep_flags[0] / keep_rate[0]
+    mlp_scale = keep_flags[1] / keep_rate[1]
+    positions = me_s * tok + jnp.arange(tok)
+    first = jnp.max(jnp.where(doc_begin[None, :] <= positions[:, None], doc_begin[None, :], 0), axis=1)
+    gain_one, gain_two = attn_norm[:, None], mlp_norm[:, None]
+
+    qkv_rows = low(jnp.concatenate([query_weight, key_weight, value_weight], axis=1).astype(jnp.float32) * gain_one)
+    def split_hidden(w):
+        w = low(w.astype(jnp.float32) * gain_two).reshape(rows, ns, nd, ffr)
+        w = jnp.transpose(w, (0, 2, 1, 3)).reshape(rows, nd * ns * ffr)
+        return w
+
+    gu = jnp.concatenate(
+        [split_hidden(gate_weight).reshape(rows, nd, -1), split_hidden(up_weight).reshape(rows, nd, -1)], axis=2
+    )
+    att_send = jnp.stack(
+        [jnp.concatenate([qkv_rows[:, 512 * j : 512 * j + 512], output_weight[:, 256 * j : 256 * j + 256]], axis=1) for j in range(3)]
+        + [jnp.concatenate([qkv_rows[:, 1536:], output_weight[:, 1024:], output_weight[:, 768:1024]], axis=1)]
+    )
+    pad = ((0, 0), (0, -rows % 16), (0, 0))
+    x = hidden_in[0].astype(jnp.float32)
+    r_one = lax.rsqrt(jnp.mean(x * x, axis=-1, keepdims=True) + EPSILON)
+    inverse_freq = ROPE_BASE ** (-2.0 * jnp.arange(HD // 2, dtype=jnp.float32) / HD)
+    angles = positions.astype(jnp.float32)[:, None] * inverse_freq[None, :]
+    cosine = jnp.tile(jnp.cos(angles), (1, 4))
+    sine = jnp.tile(jnp.concatenate([-jnp.sin(angles), jnp.sin(angles)], axis=1), (1, 2))
+    scale = jnp.broadcast_to(jnp.stack([attn_scale, mlp_scale])[:, None], (2, 128))
+    firsts = jnp.broadcast_to(first[:, None], (tok, 128))
+    wa, wb, w_gu, w_down, xn_all, gd_all, mn_all, queries, k_all, v_all, probs, att, middle = front(
+        hidden_in, cotangent, firsts, scale, cosine, sine, jnp.pad(att_send, pad), jnp.pad(jnp.transpose(gu, (1, 0, 2)), pad), down_weight
+    )
+    w_qkv = jnp.concatenate([wa[0], wa[1], wa[2], wa[3][:, :384]], axis=1)
+    w_out = jnp.concatenate([wb[0], wb[1], wb[2], wb[3], wa[3][:, 384:]], axis=1)
+    hid = w_down.shape[0]
+    r_two = lax.rsqrt(jnp.mean(middle * middle, axis=-1, keepdims=True) + EPSILON)
+    cosine, sine = cosine[:, None, :HD], sine[:, None, :HD]
+    queries = jnp.transpose(queries, (1, 0, 2)).reshape(tok, KV, groups, HD)
+    k_all, v_all = jnp.transpose(k_all, (1, 0, 2)), jnp.transpose(v_all, (1, 0, 2))
+    probs = probs.reshape(KV, groups, tok, length)
+    xn_all, gd_all, mn_all = xn_all.reshape(4 * tok, dim), gd_all.reshape(4 * tok, dim), mn_all.reshape(4 * tok, dim)
+
+    def turn_back(v):
+        return v * cosine - swap_halves(v) * sine
+
+    cot = cotangent[0].astype(jnp.float32)
+    att_all = lax.all_gather(att, "dp", axis=0, tiled=True)
+    gate, up = dot(mn_all, w_gu[:, :hid]), dot(mn_all, w_gu[:, hid:])
+    sig = jax.nn.sigmoid(gate)
+    act_gate = gate * sig
+    act = low(act_gate * up)
+    g_act = contract_cols(gd_all, w_down)
+    gg = low(g_act * up * (sig * (1.0 + gate * (1.0 - sig))))
+    gu_in = low(g_act * act_gate)
+    gboth = jnp.concatenate([gg, gu_in], axis=1)
+    g_mn = lax.psum_scatter(low(contract_cols(gboth, w_gu)), "dp", scatter_dimension=0, tiled=True).astype(jnp.float32)
+    branch = lax.psum_scatter(low(dot(act, w_down)), "dp", scatter_dimension=0, tiled=True).astype(jnp.float32)
+    block_output = low(middle + mlp_scale * branch)[None]
+    m_gu = lax.psum_scatter(low(contract_rows(mn_all, gboth)), "seq", scatter_dimension=0, tiled=True)
+    m_down = lax.psum_scatter(low(contract_rows(act, gd_all)), "seq", scatter_dimension=0, tiled=True)
+
+    def norm_back(e, v, r):
+        return r * e - v * (r * r * r) * jnp.mean(e * v, axis=-1, keepdims=True)
+
+    g_mid = cot + norm_back(g_mn, middle, r_two)
+    gba = low(attn_scale * g_mid)
+    g_att = low(contract_cols(gba, w_out)).reshape(tok, KV, groups, HD)
+    g_probs = jnp.einsum("tkgd,skd->kgts", g_att, v_all, preferred_element_type=jnp.float32)
+    delta = jnp.sum(probs.astype(jnp.float32) * g_probs, axis=-1)
+    g_scores = low(probs.astype(jnp.float32) * (g_probs - delta[..., None]))
+    g_q = jnp.einsum("kgts,skd->tkgd", g_scores, k_all, preferred_element_type=jnp.float32) * score_scale
+    g_k = jnp.einsum("kgts,tkgd->skd", g_scores, queries, preferred_element_type=jnp.float32)
+    g_v = jnp.einsum("kgts,tkgd->skd", probs, g_att, preferred_element_type=jnp.float32)
+    g_kv = low(jnp.concatenate([g_k.reshape(length, nk), g_v.reshape(length, nk)], axis=1))
+    g_kv = lax.psum_scatter(g_kv, "seq", scatter_dimension=0, tiled=True).astype(jnp.float32)
+    g_q_in = low(turn_back(g_q.reshape(tok, H, HD))).reshape(tok, nq)
+    g_k_in = low(turn_back(g_kv[:, :nk].reshape(tok, KV, HD))).reshape(tok, nk)
+    g_qkv = jnp.concatenate([g_q_in, g_k_in, low(g_kv[:, nk:])], axis=1)
+    g_xn = contract_cols(g_qkv, w_qkv)
+    input_grad = (g_mid + norm_back(g_xn, x, r_one))[None]
+
+    cut = jnp.concatenate([g_qkv.reshape(tok, nd, -1), gba.reshape(tok, nd, -1)], axis=2)
+    wq = g_qkv.shape[1] // nd
+    cut = lax.all_to_all(cut, "dp", split_axis=1, concat_axis=0, tiled=True).reshape(nd * tok, -1)
+    m_att = jnp.concatenate([contract_rows(xn_all, cut[:, :wq]), contract_rows(att_all, cut[:, wq:])], axis=1)
+    m_att = lax.psum_scatter(low(m_att), "seq", scatter_dimension=0, tiled=True)
+
+    back = jnp.concatenate([m_gu, m_att], axis=1)
+    back = lax.all_to_all(back.reshape(nd, rows, 1, -1), "dp", split_axis=0, concat_axis=2, tiled=True)
+    back = back.reshape(rows, nd, -1).astype(jnp.float32)
+
+    def whole_hidden(m):
+        return jnp.transpose(m.reshape(rows, nd, ns, ffr), (0, 2, 1, 3)).reshape(rows, -1)
+
+    m_gate, m_up = whole_hidden(back[:, :, :hid]), whole_hidden(back[:, :, hid : 2 * hid])
+    m_qkv = back[:, :, 2 * hid : 2 * hid + wq].reshape(rows, -1)
+    g_out = back[:, :, 2 * hid + wq :].reshape(rows, -1)
+
+    def weigh(w, m):
+        return jnp.sum(w.astype(jnp.float32) * m, axis=1)
+
+    m_q, m_k, m_v = m_qkv[:, :nq], m_qkv[:, nq : nq + nk], m_qkv[:, nq + nk :]
+    g_norm_one = weigh(query_weight, m_q) + weigh(key_weight, m_k) + weigh(value_weight, m_v)
+    g_norm_two = weigh(gate_weight, m_gate) + weigh(up_weight, m_up)
+    return (
+        block_output,
+        input_grad,
+        g_norm_one,
+        m_q * gain_one,
+        m_k * gain_one,
+        m_v * gain_one,
+        g_out,
+        g_norm_two,
+        m_gate * gain_two,
+        m_up * gain_two,
+        m_down.astype(jnp.float32),
+    )
+
+
 def solution(mesh):
     placed = (
         P("dp", "seq", None),
@@ -220,8 +746,9 @@
         P(),
         P(),
     )
+    fits = mesh.shape["seq"] == 8 and mesh.shape["dp"] == 4
     return jax.shard_map(
-        shards,
+        shards_by_kernels if fits else shards,
         mesh=mesh,
         in_specs=placed,
         out_specs=(

time: 573 us -> 442 us (0.77)
  waiting for transfers between devices: 386 us -> 172 us
  Pallas kernels: 0 us -> 121 us
  matrix products: 63.3 us -> 43.6 us
  blocking collectives: 23.2 us -> 15.1 us
    all_gather x7 -> x1, waiting for transfers between devices: 226 us -> 13.8 us  [shards_by_kernels(): att_all = lax.all_gather(att, 'dp', axis=0, tiled=True)]
    pallas_call x0 -> x1, Pallas kernels: none -> 121 us  [front(): pl.pallas_call(front_kernel, out_shape=[jax.ShapeDtypeStruct(*o) for o in...]
    dot_general x5 -> x3, matrix products: 15.4 us -> 6.16 us  [dot(): return jnp.dot(a, b, preferred_element_type=jnp.float32)]
    slice x17 -> x18, local copies, waits for them, and re-layouts: 13.1 us -> 4.2 us  [the longest x1 1.01 us: shards_by_kernels(): w_qkv = jnp.concatenate([wa[0], wa[1], wa[2], wa[3][:, :384]], axis=1)]
    all_to_all x2 -> x1, blocking collectives: 23.2 us -> 15.1 us  [shards_by_kernels(): lax.all_to_all(cut, 'dp', split_axis=1, concat_axis=0, tiled=True)]
    sub x1 -> x0, matrix products: 7.82 us -> none  [shards(): expo = jnp.exp(scores - jnp.max(scores, axis=-1, keepdims=True))]
    reshape x4, local copies, waits for them, and re-layouts: 2.96 us -> 9 us  [the longest x1 6.87 us: shards_by_kernels(): probs = probs.reshape(KV, groups, tok, length)]
    unnamed x104 -> x90, local copies, waits for them, and re-layouts: 23 us -> 17.4 us
  transfers between devices with their start and end apart: 14 -> 8, of which waited for: 13 -> 7; matrix products, arithmetic and copies ran while one was open for 17% -> 11% of each run, Pallas kernels for 0% -> 0%
where the time goes in v2:
time: 442 us; the launch traced here: 441 us
  waiting for transfers between devices  172 us (39%)
  Pallas kernels  121 us (27%)
  matrix products  43.6 us (10%)
  local copies, waits for them, and re-layouts  42.9 us (10%)
  other arithmetic  24.9 us (6%)
  between operations  17.6 us (4%)
  blocking collectives  15.1 us (3%)
    pallas_call x1, Pallas kernels, front(): pl.pallas_call(front_kernel, out_shape=[jax.ShapeDtypeStruct(*o) for o in...  121 us
    reduce_scatter x1, waiting for transfers between devices, shards_by_kernels(): lax.psum_scatter(low(contract_rows(mn_all, gboth)), 'seq', scatter_dimens...  38.5 us
    reduce_scatter x1, waiting for transfers between devices, shards_by_kernels(): m_att = lax.psum_scatter(low(m_att), 'seq', scatter_dimension=0, tiled=True)  35.7 us
    reduce_scatter x1, waiting for transfers between devices, shards_by_kernels(): lax.psum_scatter(low(dot(act, w_down)), 'dp', scatter_dimension=0, tiled=...  27 us
    reduce_scatter x1, waiting for transfers between devices, shards_by_kernels(): lax.psum_scatter(low(contract_rows(act, gd_all)), 'seq', scatter_dimensio...  25.6 us
    unnamed x8, waiting for transfers between devices  20.4 us
    unnamed x90, local copies, waits for them, and re-layouts  17.4 us
    all_to_all x1, blocking collectives, shards_by_kernels(): lax.all_to_all(cut, 'dp', split_axis=1, concat_axis=0, tiled=True)  15.1 us
  transfers between devices with their start and end apart: 8, of which 7 were waited for; matrix products, arithmetic and copies ran while one was open for 11% of the time, Pallas kernels for 0%

profile of v2, /device:TPU:0, one launch (start us, length us, event | category | flops | bytes accessed | tf_op | source)
XLA Modules:
  0.0 440.7 jit_solution(8517732310168266767)
XLA Ops:
  9.1 1.3 fusion.49
  23.4 120.6 %k_front.1 = (bf16[4,1152,512]{2,1,0:T(8,128)(2,1)}, bf16[4,1152,256]{2,1,0:T(8,128)(2,1)}, bf16[1152,1536]{1,0:T(8,128)(2,1)}, bf16[768,1152]{1,0:T(8,128)(2,1)...) custom-call(bf16[1,128,1152]{2,1,0:T(8,128)(2,1)} %x_in.1, ...), custom_call_target="tpu_custom_call" | custom-call | tf_op jit(solution)/shard_map/k_front/pallas_call | solution.py:562
  144.1 3.2 fusion.62
  148.5 2.7 multiply_convert_fusion.1
  152.4 3.3 convolution_convert_fusion.2
  157.9 6.9 %copy.166 = bf16[6,3,128,1024]{2,3,1,0:T(8,128)(2,1)} copy(bf16[6,3,128,1024]{3,2,1,0:T(8,128)(2,1)} %bitcast.161) | data formatting | bytes 9437184 | tf_op jit(solution)/shard_map/reshape | solution.py:651
  167.1 4.3 slice_bitcast_fusion.2
  172.5 10.9 %reduce-scatter.13.cloned.1.call-done = bf16[128,1152]{1,0:T(8,128)(2,1)} async-done(((bf16[512,1152]{1,0:T(8,128)(2,1)}), bf16[128,1152]{1,0:T(8,128)(2,1)}) %reduce-scatter.13.cloned.1.call-update) | async-done | bytes 294928 | tf_op jit(solution)/shard_map/reduce_scatter | solution.py:667
  187.6 4.3 bitcast_convert_fusion
  191.9 3.7 fusion
  195.6 6.0 %fusion.1 = bf16[6,3,128,1024]{2,3,1,0:T(8,128)(2,1)} fusion(bf16[6,3,128,1024]{2,3,1,0:T(8,128)(2,1)} %copy.166, f32[6,1024,128,3]{2,1,3,0:T(8,128)S(1)} %get-tuple-element.93, f32[6,3,128]{2,1,0:T(4,128)S(1)} %get-tuple-element.92), kind=kLoop, calls=%fused_computation.3 | loop fusion | flops 9437184 | bytes 18883584 | tf_op jit(solution)/shard_map/convert_element_type | solution.py:33
  201.7 4.2 bitcast_convert_fusion.1
  206.0 1.6 copy.194
  208.4 2.4 convolution_convert_fusion.1
  212.1 5.2 %convolution_convert_fusion = bf16[1152,1536]{1,0:T(8,128)(2,1)} fusion(bf16[512,1152]{1,0:T(8,128)(2,1)S(1)} %bitcast.186, bf16[512,768]{1,0:T(8,128)(2,1)} %copy-done.40, bf16[512,768]{1,0:T(8,128)(2,1)} %copy-done.39), kind=kOutput, calls=%fused_computation.5 | convolution fusion | flops 1816854528 | bytes 6291456 | tf_op jit(solution)/shard_map/dot_general | solution.py:21
  218.9 3.3 fusion.19
  222.4 19.6 %reduce-scatter.19.cloned.1.call-done = bf16[128,768]{1,0:T(8,128)(2,1)} async-done(((bf16[1024,768]{1,0:T(8,128)(2,1)}), bf16[128,768]{1,0:T(8,128)(2,1)}) %reduce-scatter.19.cloned.1.call-update) | async-done | bytes 196624
  244.1 15.1 %all_to_all.24 = bf16[128,4,768]{0,2,1:T(8,128)(2,1)S(1)} all-to-all(bf16[128,4,768]{0,2,1:T(8,128)(2,1)S(1)} %pad_maximum_fusion.5), channel_id=1, replica_groups=mesh['seq'=8,'dp'=4] {'dp'}, dimensions={1} | all-to-all | bytes 1572864 | tf_op jit(solution)/shard_map/all_to_all | solution.py:695
  259.5 13.8 %all-gather.2.cloned.1.call-done = bf16[512,1152]{1,0:T(8,128)(2,1)} async-done(((bf16[128,1152]{1,0:T(8,128)(2,1)}), bf16[512,1152]{1,0:T(8,128)(2,1)}) %all-gather.2.cloned.1.call-update) | async-done | bytes 1179664 | tf_op jit(solution)/shard_map/all_gather | solution.py:658
  273.2 2.0 convolution_convert_fusion.5
  276.3 2.3 copy.196
  278.7 1.4 copy-done.33
  280.1 2.3 convolution_convert_fusion.3
  282.4 1.2 copy-done.3
  284.7 25.6 %reduce-scatter.17.cloned.1.call-done = bf16[96,1152]{1,0:T(8,128)(2,1)} async-done(((bf16[768,1152]{1,0:T(8,128)(2,1)}), bf16[96,1152]{1,0:T(8,128)(2,1)}) %reduce-scatter.17.cloned.1.call-update) | async-done | bytes 221200 | tf_op jit(solution)/shard_map/reduce_scatter | solution.py:671
  310.3 1.7 convert_element_type.160
  312.0 4.0 fusion.25
  316.0 38.5 %reduce-scatter.15.cloned.1.call-done = bf16[144,1536]{1,0:T(8,128)(2,1)} async-done(((bf16[1152,1536]{1,0:T(8,128)(2,1)}), bf16[144,1536]{1,0:T(8,128)(2,1)}) %reduce-scatter.15.cloned.1.call-update) | async-done | bytes 442384 | tf_op jit(solution)/shard_map/reduce_scatter | solution.py:670
  354.5 35.7 %reduce-scatter.21.cloned.1.call-done = bf16[144,768]{1,0:T(8,128)(2,1)} async-done(((bf16[1152,768]{1,0:T(8,128)(2,1)}), bf16[144,768]{1,0:T(8,128)(2,1)}) %reduce-scatter.21.cloned.1.call-update) | async-done | bytes 221200 | tf_op jit(solution)/shard_map/reduce_scatter | solution.py:697
  392.5 3.7 all-to-all-start.1
  396.2 27.0 %reduce-scatter.11.cloned.1.call-done = bf16[128,1152]{1,0:T(8,128)(2,1)} async-done(((bf16[512,1152]{1,0:T(8,128)(2,1)}), bf16[128,1152]{1,0:T(8,128)(2,1)}) %reduce-scatter.11.cloned.1.call-update) | async-done | bytes 294928 | tf_op jit(solution)/shard_map/reduce_scatter | solution.py:668
  423.2 2.2 fusion.29
  (189 shorter events, 43.0 us)
Async XLA Ops:
  7.2 176.2 %reduce-scatter.13.cloned.1.call-start = ((), (), s32[]{:S(2)}) async-start(), calls=%async_computation.9 | async-start | bytes 1474560 | tf_op jit(solution)/shard_map/reduce_scatter | solution.py:667
  9.1 7.2 %copy-start.18 = (bf16[36,1920]{1,0:T(8,128)(2,1)}, bf16[36,1920]{1,0:T(8,128)(2,1)S(1)}, u32[]{:S(2)}) copy-start(bf16[36,1920]{1,0:T(8,128)(2,1)S(1)} %multiply_convert_fusion.4) | copy-start | bytes 414724
  12.8 2.7 copy-start.20
  13.6 2.0 copy-start.22
  16.6 4.7 %slice-start = ((bf16[36,1920]{1,0:T(8,128)(2,1)}), bf16[36,384]{1,0:T(8,128)(2,1)S(1)}, s32[]{:S(2)}) async-start(bf16[36,1920]{1,0:T(8,128)(2,1)} %copy-done.18), calls=%async_computation.15 | async-start | bytes 61440 | tf_op jit(solution)/shard_map/slice | solution.py:630
  16.6 4.7 %slice-start.1 = ((bf16[36,1152]{1,0:T(8,128)(2,1)}), bf16[36,128]{1,0:T(8,128)(2,1)S(1)}, s32[]{:S(2)}) async-start(bf16[36,1152]{1,0:T(8,128)(2,1)} %param.20), calls=%async_computation.16 | async-start | bytes 20480 | tf_op jit(solution)/shard_map/slice | solution.py:630
  144.1 3.2 copy-start.32
  144.1 3.2 copy-start.35
  155.7 86.4 %reduce-scatter.19.cloned.1.call-start = ((), (), s32[]{:S(2)}) async-start(), calls=%async_computation.13 | async-start | bytes 1769472
  167.0 16.3 %copy-start = (f32[128,1152]{1,0:T(8,128)S(1)}, f32[128,1152]{1,0:T(8,128)}, u32[]{:S(2)}) copy-start(f32[128,1152]{1,0:T(8,128)} %get-tuple-element.24) | copy-start | bytes 1769476
  167.1 17.5 %copy-start.7 = (bf16[1,128,1152]{2,1,0:T(8,128)(2,1)S(1)}, bf16[1,128,1152]{2,1,0:T(8,128)(2,1)}, u32[]{:S(2)}) copy-start(bf16[1,128,1152]{2,1,0:T(8,128)(2,1)} %cot_in.1) | copy-start | bytes 884740
  187.6 4.3 copy-start.5
  201.7 4.2 copy-start.6
  206.0 2.4 copy-start.37
  206.0 2.4 copy-start.38
  207.6 65.6 %all-gather.2.cloned.1.call-start = ((), (), s32[]{:S(2)}) async-start(), calls=%async_computation.11 | async-start | bytes 1474560 | tf_op jit(solution)/shard_map/all_gather | solution.py:658
  208.4 101.9 %reduce-scatter.17.cloned.1.call-start = ((), (), s32[]{:S(2)}) async-start(), calls=%async_computation.12 | async-start | bytes 1990656 | tf_op jit(solution)/shard_map/reduce_scatter | solution.py:671
  210.9 143.7 %reduce-scatter.15.cloned.1.call-start = ((), (), s32[]{:S(2)}) async-start(), calls=%async_computation.10 | async-start | bytes 3981312 | tf_op jit(solution)/shard_map/reduce_scatter | solution.py:670
  217.4 1.6 copy-start.4
  217.4 172.9 %reduce-scatter.21.cloned.1.call-start = ((), (), s32[]{:S(2)}) async-start(), calls=%async_computation.14 | async-start | bytes 1990656 | tf_op jit(solution)/shard_map/reduce_scatter | solution.py:697
  222.4 21.0 %copy-start.15 = (bf16[128,1152]{0,1:T(8,128)(2,1)}, bf16[128,1152]{0,1:T(8,128)(2,1)S(1)}, u32[]{:S(2)}) copy-start(bf16[128,1152]{0,1:T(8,128)(2,1)S(1)} %fusion.36) | copy-start | bytes 884740
  259.2 16.1 %copy-start.34 = (bf16[4,128,1152]{2,1,0:T(8,128)(2,1)S(1)}, bf16[4,128,1152]{2,1,0:T(8,128)(2,1)}, u32[]{:S(2)}) copy-start(bf16[4,128,1152]{2,1,0:T(8,128)(2,1)} %get-tuple-element.35) | copy-start | bytes 3538948
  278.6 144.6 %reduce-scatter.11.cloned.1.call-start = ((), (), s32[]{:S(2)}) async-start(), calls=%async_computation.8 | async-start | bytes 1474560 | tf_op jit(solution)/shard_map/reduce_scatter | solution.py:668
  282.4 29.7 %copy-start.12 = (bf16[1152,512]{1,0:T(8,128)(2,1)S(1)}, bf16[1152,512]{1,0:T(8,128)(2,1)}, u32[]{:S(2)}) copy-start(bf16[1152,512]{1,0:T(8,128)(2,1)} %get-tuple-element.43) | copy-start | bytes 3538948
  282.4 29.7 %copy-start.13 = (bf16[1152,512]{1,0:T(8,128)(2,1)S(1)}, bf16[1152,512]{1,0:T(8,128)(2,1)}, u32[]{:S(2)}) copy-start(bf16[1152,512]{1,0:T(8,128)(2,1)} %get-tuple-element.44) | copy-start | bytes 3538948
  391.4 31.8 %copy-start.1 = (f32[128,1152]{1,0:T(8,128)S(1)}, f32[128,1152]{1,0:T(8,128)}, u32[]{:S(2)}) copy-start(f32[128,1152]{1,0:T(8,128)} %get-tuple-element.24) | copy-start | bytes 1769476
  391.4 31.8 %copy-start.8 = (bf16[1,128,1152]{2,1,0:T(8,128)(2,1)S(1)}, bf16[1,128,1152]{2,1,0:T(8,128)(2,1)}, u32[]{:S(2)}) copy-start(bf16[1,128,1152]{2,1,0:T(8,128)(2,1)} %cot_in.1) | copy-start | bytes 884740
  391.5 31.8 %copy-start.11 = (bf16[128,1152]{1,0:T(8,128)(2,1)S(1)}, bf16[128,1152]{1,0:T(8,128)(2,1)}, u32[]{:S(2)}) copy-start(bf16[128,1152]{1,0:T(8,128)(2,1)} %reduce-scatter.13.cloned.1.call-done) | copy-start | bytes 884740
  391.5 31.7 %copy-start.14 = (bf16[1,128,1152]{2,1,0:T(8,128)(2,1)S(1)}, bf16[1,128,1152]{2,1,0:T(8,128)(2,1)}, u32[]{:S(2)}) copy-start(bf16[1,128,1152]{2,1,0:T(8,128)(2,1)} %x_in.1) | copy-start | bytes 884740
  391.5 31.7 %copy-start.19 = (f32[128,1152]{1,0:T(8,128)S(1)}, f32[128,1152]{1,0:T(8,128)}, u32[]{:S(2)}) copy-start(f32[128,1152]{1,0:T(8,128)} %get-tuple-element.94) | copy-start | bytes 1769476
  392.5 32.9 %all-to-all-start.1 = ((bf16[4,36,1,2304]{3,1,2,0:T(8,128)(2,1)}), bf16[4,36,1,2304]{3,1,2,0:T(8,128)(2,1)S(1)}, u32[]{:S(2)}, u32[]{:S(2)}) async-start(bf16[4,36,1,2304]{3,1,2,0:T(8,128)(2,1)} %bitcast.58), calls=%async_computation.4 | async-start | bytes 1474560 | tf_op jit(solution)/shard_map/all_to_all | solution.py:700
  425.7 1.5 copy-start.26
  (19 other events, 18.9 us)
Sparse Core Ops, SparseCore 0:
  155.8 27.5 reduce-scatter.12
  207.7 34.2 reduce-scatter.18
  243.9 29.3 all-gather.1
  275.4 34.8 reduce-scatter.16
  312.5 42.0 reduce-scatter.14
  356.8 33.3 reduce-scatter.20
  393.4 29.7 reduce-scatter.10

commit v3 on v2

--- a/solution.py
+++ b/solution.py
@@ -223,12 +223,17 @@
 
 class Net:
     def __init__(self, sends, recvs):
-        self.sends, self.recvs, self.count, self.open = sends, recvs, 0, []
+        self.sends, self.recvs, self.count, self.open, self.used = sends, recvs, 0, [], 0
         self.s, self.d = lax.axis_index("seq"), lax.axis_index("dp")
         self.z, self.c = lax.div(self.s, 2), lax.rem(self.s, 2)
         y, x = lax.div(self.d, 2), lax.rem(self.d, 2)
         self.plane = (y * 2 + 1 - x, (1 - y) * 2 + x, 3 - self.d)
         self.mate = self.at(self.z, 1 - self.c)
+
+    def room(self, count):
+        base = self.used
+        self.used += count
+        return base
 
     def at(self, z, core):
         return {"seq": z * 2 + core, "dp": self.d}
@@ -287,8 +292,8 @@
 
 
 class Chain:
-    def __init__(self, net, block, base):
-        self.net, self.block, self.base = net, block, base
+    def __init__(self, net, block, room=4):
+        self.net, self.block, self.base = net, block, net.room(room)
 
     def start(self):
         net = self.net
@@ -306,6 +311,9 @@
 
 
 class Lines(Chain):
+    def __init__(self, net, block):
+        super().__init__(net, block, 8)
+
     def start(self):
         super().start()
         self.give(0)
@@ -323,13 +331,17 @@
 
 
 class Slices(Chain):
-    def __init__(self, net, full, rows, base):
-        self.full, self.rows, self.half = full, rows, full.shape[2] // 2
-        super().__init__(net, lambda z, core: self.part(net.d, z, core), base)
-
-    def part(self, slot, z, core, cols=slice(None)):
+    def __init__(self, net, full, rows):
+        self.full, self.rows, self.half = full, rows, rows // 32 * 16
+        super().__init__(net, lambda z, core: self.part(net.d, z, core), 36)
+
+    def part(self, slot, z, core, half=None):
         first = pl.multiple_of((z * 2 + core) * self.rows, 16)
-        return self.full.at[slot, pl.ds(first, self.rows), cols]
+        if half is None:
+            return self.full.at[slot, pl.ds(first, self.rows)]
+        if half == 0:
+            return self.full.at[slot, pl.ds(first, self.half)]
+        return self.full.at[slot, pl.ds(pl.multiple_of(first + self.half, 16), self.rows - self.half)]
 
     def spread(self, k):
         net = self.net
@@ -345,7 +357,7 @@
         for kind in (0, 1):
             block = self.part(net.plane[kind], b, net.c)
             net.arrive(block, self.base + 4 + 4 * kind + b)
-            half = self.part(net.plane[kind], b, net.c, pl.ds(kind * self.half, self.half))
+            half = self.part(net.plane[kind], b, net.c, kind)
             net.push(half, half, self.base + 12 + 4 * kind + b, net.across(1 - kind))
             net.push(block, block, self.base + 24 + 4 * kind + b, net.mate)
 
@@ -353,7 +365,7 @@
         net = self.net
         b = net.order(k)
         for kind in (0, 1):
-            half = self.part(net.plane[2], b, net.c, pl.ds(kind * self.half, self.half))
+            half = self.part(net.plane[2], b, net.c, kind)
             net.arrive(half, self.base + 12 + 4 * kind + b)
         block = self.part(net.plane[2], b, net.c)
         net.push(block, block, self.base + 32 + b, net.mate)
@@ -366,27 +378,113 @@
                 net.arrive(self.part(net.plane[kind], b, 1 - net.c), self.base + 24 + 4 * kind + b)
 
 
-def exchange(net, send, land, base):
-    for kind in range(3):
-        net.push(send.at[net.plane[kind]], land.at[net.d], base + kind, net.across(kind))
-    land[net.d] = send[net.d]
-
-
-def settle(net, land, wide, rows, base):
-    for kind in range(3):
-        net.arrive(land.at[net.plane[kind]], base + kind)
+class Plane:
+    def __init__(self, net, full):
+        self.net, self.full, self.base = net, full, net.room(4)
+        self.half = full.shape[1] // 2
+
+    def start(self):
+        net = self.net
+        own = self.full.at[net.d]
+        for kind in (0, 1):
+            net.push(own, own, self.base + kind, net.across(kind))
+
+    def pass_on(self):
+        net = self.net
+        for kind in (0, 1):
+            net.arrive(self.full.at[net.plane[kind]], self.base + kind)
+            half = self.full.at[net.plane[kind], pl.ds(kind * self.half, self.half)]
+            net.push(half, half, self.base + 2 + kind, net.across(1 - kind))
+
+    def take(self):
+        net = self.net
+        for kind in (0, 1):
+            net.arrive(self.full.at[net.plane[2], pl.ds(kind * self.half, self.half)], self.base + 2 + kind)
+
+
+class Spread:
+    def __init__(self, net, send, land):
+        self.net, self.send, self.land, self.base = net, send, land, net.room(3)
+
+    def start(self):
+        net = self.net
+        for kind in (2, 0, 1):
+            net.push(self.send(net.plane[kind]), self.land(net.d), self.base + kind, net.across(kind))
+
+    def take(self):
+        for kind in range(3):
+            self.net.arrive(self.land(self.net.plane[kind]), self.base + kind)
+
+
+class ToMate:
+    def __init__(self, net, send, land):
+        self.net, self.send, self.land, self.base = net, send, land, net.room(1)
+
+    def start(self):
+        self.net.push(self.send, self.land, self.base, self.net.mate)
+
+    def take(self):
+        self.net.arrive(self.land, self.base)
+
+
+class ToOwners:
+    def __init__(self, net, part, land, down=False):
+        self.net, self.part, self.land, self.down, self.base = net, part, land, down, net.room(3)
+
+    def start(self):
+        net = self.net
+        for k in (3, 2, 1):
+            to = lax.rem(net.z - k + 4, 4)
+            net.push(self.part(to), self.land(k - 1), self.base + k - 1, net.at(to, net.c), (net.z >= k) if self.down else None)
+
+    def take(self):
+        net = self.net
+        for k in (1, 2, 3):
+            net.arrive(self.land(k - 1), self.base + k - 1, (net.z + k <= 3) if self.down else None)
+
+
+class ChainSum:
+    def __init__(self, net, part, land, add):
+        self.net, self.part, self.land, self.add, self.base = net, part, land, add, net.room(6)
+
+    def hop(self, i):
+        net, z = self.net, net_z(self.net)
+
+        @pl.when((i < z) & (z < 3))
+        def _():
+            net.arrive(self.land(i), self.base + i)
+            self.add(i, i)
+
+        net.push(self.part(i), self.land(i), self.base + i, net.at(z - 1, net.c), i < z)
+
+        @pl.when((3 - i > z) & (z > 0))
+        def _():
+            net.arrive(self.land(4 - i), self.base + 3 + i)
+            self.add(3 - i, 4 - i)
+
+        net.push(self.part(3 - i), self.land(4 - i), self.base + 3 + i, net.at(z + 1, net.c), 3 - i > z)
+
+    def own(self):
+        net, z = self.net, net_z(self.net)
+
+        @pl.when(z < 3)
+        def _():
+            net.arrive(self.land(z), self.base + z)
+            self.add(z, z)
+
+        @pl.when(z > 0)
+        def _():
+            net.arrive(self.land(1 + z), self.base + 6 - z)
+            self.add(z, 1 + z)
+
+
+def net_z(net):
+    return net.z
+
+
+def settle(land, wide, rows):
     for j in range(4):
         wide[pl.ds(j * rows, rows), : land.shape[2]] = land[j, :rows, :].astype(F32)
-
-
-def share(net, full, base):
-    for kind in range(3):
-        net.push(full.at[net.d], full.at[net.d], base + kind, net.across(kind))
-
-
-def shared(net, full, base):
-    for kind in range(3):
-        net.arrive(full.at[net.plane[kind]], base + kind)
 
 
 def turned(tile, cosine, sine):
@@ -395,191 +493,493 @@
     return tile * cosine + other * sine
 
 
-def front_kernel(
+def own_rows(index, rows):
+    return pl.ds(pl.multiple_of(index * rows, 16), rows)
+
+
+def norm_scale(v):
+    return lax.rsqrt(jnp.mean(v * v, axis=1, keepdims=True) + EPSILON)
+
+
+def norm_pull(e, v):
+    r = norm_scale(v)
+    return r * e - v * (r * r * r) * jnp.mean(e * v, axis=1, keepdims=True)
+
+
+def joined(heads, j, tok):
+    groups = H // KV
+    pair = [heads[h // groups, tok * (h % groups) : tok * (h % groups) + tok, :] for h in (2 * j, 2 * j + 1)]
+    return jnp.concatenate(pair, axis=1)
+
+
+def plane_sum(net, send, land):
+    total = send[net.d].astype(F32)
+    for kind in range(3):
+        total = total + land[net.plane[kind]].astype(F32)
+    return total
+
+
+def layer_kernel(
     x_in, cot_in, first_in, scale_in, cos_in, sin_in, att_send, gu_send, down,
-    wa, wb, wgu, wd, xn_all, gd_all, mn_all, q_heads, k_heads, v_heads, probs, att, middle,
-    att_land, gu_land, wide, kv_all, o_heads, bias, sends, recvs,
+    block_out, input_grad, back_gu, back_att, back_down,
+    att_land, gu_land, wide, qkv_land, kv_all, o_heads, bias, wa, wb, wgu, wd,
+    xn_all, gd_all, mn_all, att_all, q_heads, k_heads, v_heads, probs, middle, act, gboth, turn_x, turn_n, turn_a,
+    gn_send, gn_land, br_send, br_land, gu_mate, gu_zone, dn_mate, dn_zone, gmid, do_heads, dkv, kv_mate, kv_zone, kv_tot,
+    cut_land, ma_mate, ma_zone, gx_land, sends, recvs,
 ):
     net = Net(sends, recvs)
     tok, dim = x_in.shape[1], x_in.shape[2]
     rows = dim // 32
     blk = 4 * rows
     ffr = down.shape[0]
+    hid = 8 * ffr
     d, z, c, s = net.d, net.z, net.c, net.s
-
-    a = Slices(net, wa, blk, 16)
-    b = Slices(net, wb, blk, 56)
-    gu = Lines(net, lambda zz, core: wgu.at[pl.ds(pl.multiple_of((zz * 2 + core) * blk, 16), blk)], 96)
-    dn = Lines(net, lambda zz, core: wd.at[pl.ds(pl.multiple_of((zz * 2 + core) * ffr, 16), ffr)], 104)
-    kv = Lines(net, lambda zz, core: kv_all.at[zz * 2 + core], 112)
+    span, length = 4 * tok, 8 * tok
+    groups = H // KV
+    qkv_send = cut_send = act.reshape(4, tok, hid)
+    gx_send, gs_heads = gd_all, gboth
+    m_att = wb.reshape(4, 4, 2, blk, 384)
+
+    a2a_att = Spread(net, lambda j: att_send.at[j], lambda j: att_land.at[j])
+    a2a_gu = Spread(net, lambda j: gu_send.at[j], lambda j: gu_land.at[j])
+    a2a_qkv = Spread(net, lambda j: qkv_send.at[j, :, pl.ds(0, 512)], lambda j: qkv_land.at[j])
+    a = Lines(net, lambda zz, core: wa.at[own_rows(zz * 2 + core, blk)])
+    b = Slices(net, wb, blk)
+    gu = Lines(net, lambda zz, core: wgu.at[zz, core])
+    dn = Lines(net, lambda zz, core: wd.at[zz, core])
+    kv = Lines(net, lambda zz, core: kv_all.at[zz, core])
+    xs = Plane(net, xn_all)
+    gs = Plane(net, gd_all)
+    ms = Plane(net, mn_all)
+    ats = Plane(net, att_all)
 
     net.greet()
-    exchange(net, att_send, att_land, 0)
+    a2a_att.start()
+    att_land[d] = att_send[d]
     x = x_in[0].astype(F32)
-    xn = (x * lax.rsqrt(jnp.mean(x * x, axis=1, keepdims=True) + EPSILON)).astype(BF)
-    xn_all[d] = xn
+    xn_all[d] = (x * norm_scale(x)).astype(BF)
+    xs.start()
+    a2a_gu.start()
+    gu_land[d] = gu_send[d]
     gd_all[d] = (cot_in[0].astype(F32) * scale_in[1:2, 0:1]).astype(BF)
-    wd[pl.ds(pl.multiple_of(s * ffr, 16), ffr), :] = down[...]
-    settle(net, att_land, wide, rows, 0)
-    own = pl.ds(pl.multiple_of(s * blk, 16), blk)
-    wa[d, own, :] = wide[:, :512].astype(BF)
-    wb[d, own, :] = wide[:, 512:768].astype(BF)
+    wd[z, c] = down[...]
+    a2a_att.take()
+    settle(att_land, wide, rows)
+    own = own_rows(s, blk)
+    wa[own, :] = wide[:, :512].astype(BF)
+    wb[d, own, :] = wide[:, 384:768].astype(BF)
     a.start()
-    a.spread(0)
-    exchange(net, gu_send, gu_land, 3)
+    a.step(1)
+    a.give(1)
     dn.start()
+    xs.pass_on()
+    a.step(2)
+    a.give(2)
     b.start()
-    a.step(1)
-    a.spread(1)
-    a.pass_on(0)
+    a.step(3)
+    a.give(3)
+    a2a_gu.take()
+    settle(gu_land, wide, rows)
+    wgu[z, c] = wide[...].astype(BF)
+    gu.start()
+    xs.take()
+    a.take()
+
+    cosine, sine = cos_in[...], sin_in[...]
+    eighth = 1.0 / math.sqrt(HD)
+    for j in range(4):
+        part = dot_nn(xn_all[j], wa[...])
+        for i in range(4):
+            tile = part[:, 128 * i : 128 * i + 128]
+            spun = turned(tile, cosine, sine)
+            if i < 2:
+                tile = spun * eighth
+            elif i == 2:
+                tile = jnp.where(d < 2, spun, tile)
+            else:
+                tile = jnp.where(d == 0, spun, jnp.where(d == 2, spun * eighth, tile))
+            qkv_send[j, :, 128 * i : 128 * i + 128] = tile.astype(BF)
+    a2a_qkv.start()
+    qkv_land[d] = qkv_send[d, :, :512]
     b.spread(0)
-    a.step(2)
-    a.spread(2)
-    a.pass_on(1)
-    a.corner(0)
-    settle(net, gu_land, wide, rows, 3)
-    wgu[own, :] = wide[...].astype(BF)
-    gu.start()
-    a.step(3)
-    a.spread(3)
-    a.pass_on(2)
-    a.corner(1)
     b.step(1)
     b.spread(1)
-    a.pass_on(3)
-    a.corner(2)
-    b.step(2)
-    b.spread(2)
-    a.corner(3)
-    a.take()
-
-    cosine, sine = cos_in[...], sin_in[...]
-    for j in range(4):
-        part = dot_nn(xn, wa[j])
-        for i in range(4):
-            t = 4 * j + i
-            if t == 15:
-                continue
-            tile = part[:, 128 * i : 128 * i + 128]
-            if t < 12:
-                tile = turned(tile, cosine, sine)
-            if t < 9:
-                tile = (tile * (1.0 / math.sqrt(HD))).astype(BF)
-                q_heads[2 * t] = tile[:, :HD]
-                q_heads[2 * t + 1] = tile[:, HD:]
-            else:
-                kv_all[s, :, pl.ds(128 * (t - 9), 128)] = tile.astype(BF)
+    a2a_qkv.take()
+    places = [(0, 256), (0, 384), (1, 256), (1, 384), (2, 256), (3, 256)]
+    for i, (j, col) in enumerate(places):
+        kv_all[z, c, :, 128 * i : 128 * i + 128] = qkv_land[j, :, col : col + 128]
     kv.start()
-    share(net, gd_all, 8)
-    b.step(3)
-    b.spread(3)
-
+    gs.start()
+    for t in range(9):
+        j, col = (t // 2, (t % 2) * 128) if t < 8 else (2, 384)
+        for h in (2 * t, 2 * t + 1):
+            at = col + HD * (h % 2)
+            q_heads[h // groups, tok * (h % groups) : tok * (h % groups) + tok, :] = qkv_land[j, :, at : at + HD]
     position = s * tok + lax.broadcasted_iota(jnp.int32, (tok, 1), 0)
     key = lax.broadcasted_iota(jnp.int32, bias.shape, 1)
     bias[...] = jnp.where((key <= position) & (key >= first_in[:, 0:1]), 0.0, MASKED)
 
-    for k in range(3):
-        b.pass_on(k)
+    kv.step(1)
+    kv.give(1)
+    b.step(2)
+    b.spread(2)
+    kv.step(2)
+    kv.give(2)
+    b.step(3)
+    b.spread(3)
+    b.pass_on(0)
+    b.pass_on(1)
+    kv.step(3)
+    kv.give(3)
+    dn.step(1)
+    gu.step(1)
+    gs.pass_on()
+    b.pass_on(2)
     b.corner(0)
     b.corner(1)
-    for k in (1, 2, 3):
-        kv.step(k)
-        kv.give(k)
-        if k == 1:
-            dn.step(1)
-            dn.give(1)
-            b.pass_on(3)
-        if k == 2:
-            gu.step(1)
-            gu.give(1)
-            b.corner(2)
     kv.take()
-    share(net, xn_all, 11)
     for j in range(8):
         for k in range(KV):
-            k_heads[k, pl.ds(tok * j, tok), :] = kv_all[j, :, HD * k : HD * k + HD]
-            v_heads[k, pl.ds(tok * j, tok), :] = kv_all[j, :, HD * (KV + k) : HD * (KV + k) + HD]
+            k_heads[k, pl.ds(tok * j, tok), :] = kv_all[j // 2, j % 2, :, HD * k : HD * k + HD]
+            v_heads[k, pl.ds(tok * j, tok), :] = kv_all[j // 2, j % 2, :, HD * (KV + k) : HD * (KV + k) + HD]
 
     def head(h, carry):
-        k = lax.div(h, H // KV)
-        score = dot_nt(q_heads[h], k_heads[k]) + bias[...]
+        k = lax.div(h, groups)
+        mine = pl.ds(pl.multiple_of(lax.rem(h, groups) * tok, tok), tok)
+        score = dot_nt(q_heads[k, mine, :], k_heads[k]) + bias[...]
         expo = jnp.exp(score - jnp.max(score, axis=1, keepdims=True))
         p = (expo / jnp.sum(expo, axis=1, keepdims=True)).astype(BF)
-        probs[h] = p
-        o_heads[h] = dot_nn(p, v_heads[k])
+        probs[k, mine, :] = p
+        o_heads[k, mine, :] = dot_nn(p, v_heads[k])
         return carry
 
     lax.fori_loop(0, 6, head, 0)
+    b.pass_on(3)
+    b.corner(2)
+    lax.fori_loop(6, 12, head, 0)
+    b.corner(3)
     dn.step(2)
-    dn.give(2)
-    b.corner(3)
+    gu.step(2)
+    lax.fori_loop(12, 18, head, 0)
     b.take()
-    lax.fori_loop(6, 12, head, 0)
-    gu.step(2)
-    gu.give(2)
-    lax.fori_loop(12, 18, head, 0)
     for j in range(H // 2):
-        att[:, 128 * j : 128 * j + 128] = jnp.concatenate([o_heads[2 * j], o_heads[2 * j + 1]], axis=1).astype(BF)
-    full = att[...]
-    branch = [dot_nn(full, wb[j]) for j in range(4)] + [dot_nn(full, wa[3, :, 384:])]
+        att_all[d, :, 128 * j : 128 * j + 128] = joined(o_heads, j, tok).astype(BF)
+    full = att_all[d]
+    branch = [dot_nn(full, wb[j, :, 128:]) for j in range(4)] + [dot_nn(full, wb[3, :, :128])]
     mid = x_in[0].astype(F32) + scale_in[0:1, 0:1] * jnp.concatenate(branch, axis=1)
     middle[...] = mid
-    mn_all[d] = (mid * lax.rsqrt(jnp.mean(mid * mid, axis=1, keepdims=True) + EPSILON)).astype(BF)
-    share(net, mn_all, 120)
+    mn_all[d] = (mid * norm_scale(mid)).astype(BF)
+    gs.take()
+    ms.start()
+    for k in (1, 2):
+        dn.give(k)
+        gu.give(k)
     dn.step(3)
     dn.give(3)
+    ms.pass_on()
     gu.step(3)
     gu.give(3)
-    shared(net, gd_all, 8)
-    shared(net, xn_all, 11)
+    ms.take()
     dn.take()
     gu.take()
-    shared(net, mn_all, 120)
     net.finish()
-
-
-def front(x, cot, first, scale, cosine, sine, att_send, gu_send, down):
+    ats.start()
+
+    def by_cols(send, land, width):
+        return [
+            Spread(
+                net,
+                lambda j, n=n: send.at[j, :, pl.ds(width * n, width)],
+                lambda j, n=n: land.at[j, :, pl.ds(width * n, width)],
+            )
+            for n in range(dim // width)
+        ]
+
+    gn, br, gx = by_cols(gn_send, gn_land, 384), by_cols(br_send, br_land, dim), by_cols(gx_send, gx_land, 384)
+    wgu_flat, wd_flat = wgu.reshape(dim, 2 * hid), wd.reshape(hid, dim)
+    other = 1 - c
+    gu_pair = [
+        ToMate(net, wgu.at[:, other, :, pl.ds(256 * n, 256)], gu_mate.at[:, :, pl.ds(256 * n, 256)]) for n in range(2 * hid // 256)
+    ]
+    dn_pair = [ToMate(net, wd.at[:, other, :, pl.ds(384 * n, 384)], dn_mate.at[:, :, pl.ds(384 * n, 384)]) for n in range(3)]
+
+    for n in range(hid // 256):
+        cols, ups = pl.ds(256 * n, 256), pl.ds(hid + 256 * n, 256)
+        normed = mn_all[...].reshape(span, dim)
+        gate = dot_nn(normed, wgu_flat[:, cols])
+        up = dot_nn(normed, wgu_flat[:, ups])
+        g_act = dot_nt(gd_all[...].reshape(span, dim), wd_flat[cols, :])
+        sig = jax.nn.sigmoid(gate)
+        swish = gate * sig
+        act[:, cols] = (swish * up).astype(BF)
+        gboth[:, cols] = (g_act * up * (sig * (1.0 + gate * (1.0 - sig)))).astype(BF)
+        gboth[:, ups] = (g_act * swish).astype(BF)
+    for n in range(3):
+        part = dot_nt(gboth[...], wgu_flat[384 * n : 384 * n + 384, :]).astype(BF)
+        gn_send[:, :, 384 * n : 384 * n + 384] = part.reshape(4, tok, 384)
+        gn[n].start()
+    for n in range(3):
+        part = dot_nn(act[...], wd_flat[:, 384 * n : 384 * n + 384]).astype(BF)
+        br_send[:, :, 384 * n : 384 * n + 384] = part.reshape(4, tok, 384)
+    br[0].start()
+    turn_x[...] = mn_all[...].reshape(span, dim).T
+    turn_a[...] = act[...].T
+    for n in range(2 * hid // 256):
+        wgu_flat[:, 256 * n : 256 * n + 256] = dot_nn(turn_x[...], gboth[:, 256 * n : 256 * n + 256]).astype(BF)
+        gu_pair[n].start()
+    for n in range(3):
+        cols = pl.ds(384 * n, 384)
+        wd_flat[:, cols] = dot_nn(turn_a[...], gd_all[:, :, cols].reshape(span, 384)).astype(BF)
+        dn_pair[n].start()
+
+    def add_gu(block, slot):
+        wgu[block, c] = (wgu[block, c].astype(F32) + gu_zone[slot].astype(F32)).astype(BF)
+
+    def add_dn(block, slot):
+        wd[block, c] = (wd[block, c].astype(F32) + dn_zone[slot].astype(F32)).astype(BF)
+
+    gu_sum = ChainSum(net, lambda zz: wgu.at[zz, c], lambda k: gu_zone.at[k], add_gu)
+    dn_sum = ChainSum(net, lambda zz: wd.at[zz, c], lambda k: dn_zone.at[k], add_dn)
+    ats.pass_on()
+    for pair in gu_pair:
+        pair.take()
+    for k in range(4):
+        wgu[k, c] = (wgu[k, c].astype(F32) + gu_mate[k].astype(F32)).astype(BF)
+    for pair in dn_pair:
+        pair.take()
+    for k in range(4):
+        wd[k, c] = (wd[k, c].astype(F32) + dn_mate[k].astype(F32)).astype(BF)
+    gu_sum.hop(0)
+    dn_sum.hop(0)
+
+    for n in range(3):
+        gn[n].take()
+    mid = middle[...]
+    g_mid = cot_in[0].astype(F32) + norm_pull(plane_sum(net, gn_send, gn_land), mid)
+    gmid[...] = g_mid
+    gba = (scale_in[0:1, 0:1] * g_mid).astype(BF)
+    for j in range(4):
+        cut_send[j, :, 512:768] = gba[:, 256 * j : 256 * j + 256]
+    cut_send[3, :, 384:512] = gba[:, 1024:1152]
+    cut = lambda cols: Spread(net, lambda j: cut_send.at[j, :, cols], lambda j: cut_land.at[j, :, cols])
+    cut_o, cut_q, cut_l = cut(pl.ds(512, 256)), cut(pl.ds(0, 256)), cut(pl.ds(256, 256))
+    cut_o.start()
+    cut_land[d, :, 512:768] = cut_send[d, :, 512:768]
+    g_att = dot_nt(gba[:, 1024:1152], wb[3, :, :128])
+    for j in range(4):
+        g_att = g_att + dot_nt(gba[:, 256 * j : 256 * j + 256], wb[j, :, 128:])
+    for h in range(H):
+        do_heads[h // groups, tok * (h % groups) : tok * (h % groups) + tok, :] = g_att[:, HD * h : HD * h + HD].astype(BF)
+    gu_sum.hop(1)
+    dn_sum.hop(1)
+
+    kv_pair = [ToMate(net, dkv.at[n, :, other], kv_mate.at[n]) for n in range(2)]
+    kv_sum = [ToOwners(net, lambda zz, n=n: dkv.at[n, zz, c], lambda k, n=n: kv_zone.at[n, k], True) for n in range(2)]
+
+    def pull(k, carry):
+        for g in range(groups):
+            mine = pl.ds(tok * g, tok)
+            p = probs[k, mine, :].astype(F32)
+            t = p * dot_nt(do_heads[k, mine, :], v_heads[k])
+            ds = (t - p * jnp.sum(t, axis=1, keepdims=True)).astype(BF)
+            gs_heads[mine, :length] = ds
+            o_heads[k, mine, :] = dot_nn(ds, k_heads[k]) * eighth
+        half, kk = lax.div(k, 3), lax.rem(k, 3)
+        for i, (left, right) in enumerate(((q_heads[k], gs_heads[: groups * tok, :length]), (do_heads[k], probs[k]))):
+            turned_grad = dot_tn(left, right).astype(BF)
+            at = pl.ds(pl.multiple_of(192 * i + HD * kk, HD), HD)
+            for j in range(8):
+                dkv[half, j // 2, j % 2, at, :] = turned_grad[:, tok * j : tok * j + tok]
+        return carry
+
+    def pair_sum(n):
+        kv_pair[n].take()
+        for k in range(4):
+            dkv[n, k, c] = (dkv[n, k, c].astype(F32) + kv_mate[n, k].astype(F32)).astype(BF)
+        kv_sum[n].start()
+
+    def grads(p, parts):
+        at = 0
+        for part in parts:
+            wb[p, :, at : at + part.shape[1]] = part.astype(BF)
+            at += part.shape[1]
+        pair = ToMate(net, m_att.at[p, :, other, :, quarter], ma_mate.at[p])
+        pair.start()
+        return pair
+
+    def grads_sum(p, pair):
+        pair.take()
+        for k in range(4):
+            m_att[p, k, c, :, quarter] = (m_att[p, k, c, :, quarter].astype(F32) + ma_mate[p, k].astype(F32)).astype(BF)
+        out = ToOwners(net, lambda zz: m_att.at[p, zz, c, :, quarter], lambda k: ma_zone.at[p, k])
+        out.start()
+        return out
+
+    def grads_back(p, out):
+        cols = pl.ds(256 * p, 256)
+        out.take()
+        total = m_att[p, z, c, :, quarter].astype(F32)
+        for k in range(3):
+            total = total + ma_zone[p, k].astype(F32)
+        wide[:, : total.shape[1]] = total
+        for j in range(4):
+            att_land[j, :rows, cols] = wide[pl.ds(j * rows, rows), : total.shape[1]].astype(BF)
+        spread = Spread(net, lambda j: att_land.at[j, :, cols], lambda j: back_att.at[j, :, cols])
+        spread.start()
+        back_att[d, :, cols] = att_land[d, :, cols]
+        return spread
+
+    q_cols, l_cols, o_cols = pl.ds(0, 256), pl.ds(256, 256), pl.ds(512, 256)
+    quarter = pl.ds(0, 256)
+    lax.fori_loop(0, 3, pull, 0)
+    kv_pair[0].start()
+    ats.take()
+    cut_o.take()
+    turn_x[...] = att_all[...].reshape(span, dim).T
+    pair_o = grads(2, [dot_nn(turn_x[...], cut_land[:, :, o_cols].reshape(span, 256))])
+    pair_sum(0)
+    lax.fori_loop(3, 6, pull, 0)
+    kv_pair[1].start()
+    for t in range(9):
+        j, col = (t // 2, (t % 2) * 128) if t < 8 else (2, 384)
+        cut_send[j, :, col : col + 128] = turned(joined(o_heads, t, tok), cosine, -sine).astype(BF)
+    cut_q.start()
+    cut_land[d, :, q_cols] = cut_send[d, :, q_cols]
+    pair_sum(1)
+    gu_sum.hop(2)
+    dn_sum.hop(2)
+    sum_o = grads_sum(2, pair_o)
+    turn_n[...] = xn_all[...].reshape(span, dim).T
+    cut_q.take()
+    pair_q = grads(0, [dot_nn(turn_n[...], cut_land[:, :, q_cols].reshape(span, 256))])
+    br[0].take()
+    block_out[0] = (middle[...] + scale_in[1:2, 0:1] * plane_sum(net, br_send, br_land)).astype(BF)
+    sum_q = grads_sum(0, pair_q)
+
+    for n in range(2):
+        kv_sum[n].take()
+        kv_tot[n] = dkv[n, z, c].astype(F32)
+        for k in (1, 2, 3):
+
+            @pl.when(z + k <= 3)
+            def _(n=n, k=k):
+                kv_tot[n] += kv_zone[n, k - 1].astype(F32)
+
+    keys = jnp.concatenate([kv_tot[0, :192, :], kv_tot[1, :192, :]], axis=0).T
+    vals = jnp.concatenate([kv_tot[0, 192:, :], kv_tot[1, 192:, :]], axis=0).T
+    late = [turned(keys[:, 128 * i : 128 * i + 128], cosine, -sine) for i in range(3)] + [vals[:, 128 * i : 128 * i + 128] for i in range(3)]
+    for tile, (j, col) in zip(late, places):
+        cut_send[j, :, col : col + 128] = tile.astype(BF)
+    cut_l.start()
+    cut_land[d, :, l_cols] = cut_send[d, :, l_cols]
+    cut_l.take()
+    last = cut_land[:, :, 384:512].reshape(span, 128)
+    cuts = cut_land[:, :, :512].reshape(span, 512)
+    lane = lax.broadcasted_iota(jnp.int32, cuts.shape, 1)
+    cuts = jnp.where((d == 3) & (lane >= 384), jnp.zeros_like(cuts), cuts)
+    for n in range(3):
+        part = dot_nt(cuts, wa[384 * n : 384 * n + 384, :]).astype(BF)
+        gx_send[:, :, 384 * n : 384 * n + 384] = part.reshape(4, tok, 384)
+        gx[n].start()
+    second = jnp.where(d == 3, dot_nn(turn_x[...], last), dot_nn(turn_n[...], last))
+    pair_l = grads(1, [dot_nn(turn_n[...], cut_land[:, :, 256:384].reshape(span, 128)), second])
+    sum_l = grads_sum(1, pair_l)
+    back_o = grads_back(2, sum_o)
+    back_q = grads_back(0, sum_q)
+    gu_sum.own()
+    dn_sum.own()
+    back_down[...] = wd[z, c]
+    wide[...] = wgu[z, c].astype(F32)
+    for j in range(4):
+        gu_land[j, :rows, :] = wide[pl.ds(j * rows, rows), :].astype(BF)
+    back_g = Spread(net, lambda j: gu_land.at[j], lambda j: back_gu.at[j])
+    back_g.start()
+    back_gu[d] = gu_land[d]
+    back_l = grads_back(1, sum_l)
+    for n in range(3):
+        gx[n].take()
+    input_grad[0] = gmid[...] + norm_pull(plane_sum(net, gx_send, gx_land), x_in[0].astype(F32))
+    for spread in (back_o, back_q, back_g, back_l):
+        spread.take()
+    net.finish()
+
+
+def layer(x, cot, first, scale, cosine, sine, att_send, gu_send, down):
     tok, dim = x.shape[1:]
     ns = 8
     length = tok * ns
-    hid = down.shape[0] * ns
+    ffr = down.shape[0]
+    hid = ffr * ns
+    blk = dim // ns
+    span = 4 * tok
     vm = pl.BlockSpec(memory_space=pltpu.VMEM)
     outs = [
-        ((4, dim, 512), BF),
-        ((4, dim, 256), BF),
-        ((dim, 2 * hid), BF),
-        ((hid, dim), BF),
-        ((4, tok, dim), BF),
-        ((4, tok, dim), BF),
-        ((4, tok, dim), BF),
-        ((H, tok, HD), BF),
+        ((1, tok, dim), BF),
+        ((1, tok, dim), F32),
+        (gu_send.shape, BF),
+        (att_send.shape, BF),
+        (down.shape, BF),
+    ]
+    plane = ((4, tok, dim), BF)
+    wide_cut = ((4, tok, 512), BF)
+    three = ((KV, 3 * tok, HD), BF)
+    scratch = [
+        (att_send.shape, BF),
+        (gu_send.shape, BF),
+        ((blk, 2 * hid), F32),
+        wide_cut,
+        ((4, 2, tok, 2 * KV * HD), BF),
+        ((KV, 3 * tok, HD), F32),
+        ((tok, length), F32),
+        ((dim, 512), BF),
+        ((4, dim, 384), BF),
+        ((4, 2, blk, 2 * hid), BF),
+        ((4, 2, ffr, dim), BF),
+        plane,
+        plane,
+        plane,
+        plane,
+        three,
         ((KV, length, HD), BF),
         ((KV, length, HD), BF),
-        ((H, tok, length), BF),
-        ((tok, H * HD), BF),
+        ((KV, 3 * tok, length), BF),
         ((tok, dim), F32),
+        ((span, hid), BF),
+        ((span, 2 * hid), BF),
+        ((dim, span), BF),
+        ((dim, span), BF),
+        ((hid, span), BF),
+        plane,
+        plane,
+        plane,
+        plane,
+        ((4, blk, 2 * hid), BF),
+        ((5, blk, 2 * hid), BF),
+        ((4, ffr, dim), BF),
+        ((5, ffr, dim), BF),
+        ((tok, dim), F32),
+        three,
+        ((2, 4, 2, 384, tok), BF),
+        ((2, 4, 384, tok), BF),
+        ((2, 3, 384, tok), BF),
+        ((2, 384, tok), F32),
+        ((4, tok, 768), BF),
+        ((3, 4, blk, 256), BF),
+        ((3, 3, blk, 256), BF),
+        plane,
     ]
     return pl.pallas_call(
-        front_kernel,
+        layer_kernel,
         out_shape=[jax.ShapeDtypeStruct(*o) for o in outs],
         in_specs=[vm] * 9,
         out_specs=[vm] * len(outs),
-        scratch_shapes=[
-            pltpu.VMEM(att_send.shape, BF),
-            pltpu.VMEM(gu_send.shape, BF),
-            pltpu.VMEM((dim // 8, 2 * hid), F32),
-            pltpu.VMEM((ns, tok, 2 * KV * HD), BF),
-            pltpu.VMEM((H, tok, HD), F32),
-            pltpu.VMEM((tok, length), F32),
-            pltpu.SemaphoreType.DMA((160,)),
-            pltpu.SemaphoreType.DMA((128,)),
-        ],
+        scratch_shapes=[pltpu.VMEM(*t) for t in scratch] + [pltpu.SemaphoreType.DMA((320,)), pltpu.SemaphoreType.DMA((256,))],
         compiler_params=pltpu.CompilerParams(collective_id=0, has_side_effects=True, vmem_limit_bytes=LIMIT),
-        name="k_front",
+        name="k_layer",
     )(x, cot, first, scale, cosine, sine, att_send, gu_send, down)
 
 
-def shards_by_kernels(
+def shards_by_kernel(
     hidden_in,
     attn_norm,
     query_weight,
@@ -625,87 +1025,44 @@
     gu = jnp.concatenate(
         [split_hidden(gate_weight).reshape(rows, nd, -1), split_hidden(up_weight).reshape(rows, nd, -1)], axis=2
     )
-    att_send = jnp.stack(
-        [jnp.concatenate([qkv_rows[:, 512 * j : 512 * j + 512], output_weight[:, 256 * j : 256 * j + 256]], axis=1) for j in range(3)]
-        + [jnp.concatenate([qkv_rows[:, 1536:], output_weight[:, 1024:], output_weight[:, 768:1024]], axis=1)]
-    )
+    late = [(9, 10), (11, 12), (13, 8), (14, None)]
+    tiles = []
+    for j in range(4):
+        first_late, second_late = late[j]
+        qkv_tile = lambda t: qkv_rows[:, 128 * t : 128 * t + 128]
+        second = output_weight[:, 1024:] if second_late is None else qkv_tile(second_late)
+        tiles.append(
+            jnp.concatenate(
+                [qkv_rows[:, 256 * j : 256 * j + 256], qkv_tile(first_late), second, output_weight[:, 256 * j : 256 * j + 256]], axis=1
+            )
+        )
+    att_send = jnp.stack(tiles)
     pad = ((0, 0), (0, -rows % 16), (0, 0))
-    x = hidden_in[0].astype(jnp.float32)
-    r_one = lax.rsqrt(jnp.mean(x * x, axis=-1, keepdims=True) + EPSILON)
     inverse_freq = ROPE_BASE ** (-2.0 * jnp.arange(HD // 2, dtype=jnp.float32) / HD)
     angles = positions.astype(jnp.float32)[:, None] * inverse_freq[None, :]
     cosine = jnp.tile(jnp.cos(angles), (1, 4))
     sine = jnp.tile(jnp.concatenate([-jnp.sin(angles), jnp.sin(angles)], axis=1), (1, 2))
     scale = jnp.broadcast_to(jnp.stack([attn_scale, mlp_scale])[:, None], (2, 128))
     firsts = jnp.broadcast_to(first[:, None], (tok, 128))
-    wa, wb, w_gu, w_down, xn_all, gd_all, mn_all, queries, k_all, v_all, probs, att, middle = front(
+    block_output, input_grad, back_gu, back_att, m_down = layer(
         hidden_in, cotangent, firsts, scale, cosine, sine, jnp.pad(att_send, pad), jnp.pad(jnp.transpose(gu, (1, 0, 2)), pad), down_weight
     )
-    w_qkv = jnp.concatenate([wa[0], wa[1], wa[2], wa[3][:, :384]], axis=1)
-    w_out = jnp.concatenate([wb[0], wb[1], wb[2], wb[3], wa[3][:, 384:]], axis=1)
-    hid = w_down.shape[0]
-    r_two = lax.rsqrt(jnp.mean(middle * middle, axis=-1, keepdims=True) + EPSILON)
-    cosine, sine = cosine[:, None, :HD], sine[:, None, :HD]
-    queries = jnp.transpose(queries, (1, 0, 2)).reshape(tok, KV, groups, HD)
-    k_all, v_all = jnp.transpose(k_all, (1, 0, 2)), jnp.transpose(v_all, (1, 0, 2))
-    probs = probs.reshape(KV, groups, tok, length)
-    xn_all, gd_all, mn_all = xn_all.reshape(4 * tok, dim), gd_all.reshape(4 * tok, dim), mn_all.reshape(4 * tok, dim)
-
-    def turn_back(v):
-        return v * cosine - swap_halves(v) * sine
-
-    cot = cotangent[0].astype(jnp.float32)
-    att_all = lax.all_gather(att, "dp", axis=0, tiled=True)
-    gate, up = dot(mn_all, w_gu[:, :hid]), dot(mn_all, w_gu[:, hid:])
-    sig = jax.nn.sigmoid(gate)
-    act_gate = gate * sig
-    act = low(act_gate * up)
-    g_act = contract_cols(gd_all, w_down)
-    gg = low(g_act * up * (sig * (1.0 + gate * (1.0 - sig))))
-    gu_in = low(g_act * act_gate)
-    gboth = jnp.concatenate([gg, gu_in], axis=1)
-    g_mn = lax.psum_scatter(low(contract_cols(gboth, w_gu)), "dp", scatter_dimension=0, tiled=True).astype(jnp.float32)
-    branch = lax.psum_scatter(low(dot(act, w_down)), "dp", scatter_dimension=0, tiled=True).astype(jnp.float32)
-    block_output = low(middle + mlp_scale * branch)[None]
-    m_gu = lax.psum_scatter(low(contract_rows(mn_all, gboth)), "seq", scatter_dimension=0, tiled=True)
-    m_down = lax.psum_scatter(low(contract_rows(act, gd_all)), "seq", scatter_dimension=0, tiled=True)
-
-    def norm_back(e, v, r):
-        return r * e - v * (r * r * r) * jnp.mean(e * v, axis=-1, keepdims=True)
-
-    g_mid = cot + norm_back(g_mn, middle, r_two)
-    gba = low(attn_scale * g_mid)
-    g_att = low(contract_cols(gba, w_out)).reshape(tok, KV, groups, HD)
-    g_probs = jnp.einsum("tkgd,skd->kgts", g_att, v_all, preferred_element_type=jnp.float32)
-    delta = jnp.sum(probs.astype(jnp.float32) * g_probs, axis=-1)
-    g_scores = low(probs.astype(jnp.float32) * (g_probs - delta[..., None]))
-    g_q = jnp.einsum("kgts,skd->tkgd", g_scores, k_all, preferred_element_type=jnp.float32) * score_scale
-    g_k = jnp.einsum("kgts,tkgd->skd", g_scores, queries, preferred_element_type=jnp.float32)
-    g_v = jnp.einsum("kgts,tkgd->skd", probs, g_att, preferred_element_type=jnp.float32)
-    g_kv = low(jnp.concatenate([g_k.reshape(length, nk), g_v.reshape(length, nk)], axis=1))
-    g_kv = lax.psum_scatter(g_kv, "seq", scatter_dimension=0, tiled=True).astype(jnp.float32)
-    g_q_in = low(turn_back(g_q.reshape(tok, H, HD))).reshape(tok, nq)
-    g_k_in = low(turn_back(g_kv[:, :nk].reshape(tok, KV, HD))).reshape(tok, nk)
-    g_qkv = jnp.concatenate([g_q_in, g_k_in, low(g_kv[:, nk:])], axis=1)
-    g_xn = contract_cols(g_qkv, w_qkv)
-    input_grad = (g_mid + norm_back(g_xn, x, r_one))[None]
-
-    cut = jnp.concatenate([g_qkv.reshape(tok, nd, -1), gba.reshape(tok, nd, -1)], axis=2)
-    wq = g_qkv.shape[1] // nd
-    cut = lax.all_to_all(cut, "dp", split_axis=1, concat_axis=0, tiled=True).reshape(nd * tok, -1)
-    m_att = jnp.concatenate([contract_rows(xn_all, cut[:, :wq]), contract_rows(att_all, cut[:, wq:])], axis=1)
-    m_att = lax.psum_scatter(low(m_att), "seq", scatter_dimension=0, tiled=True)
-
-    back = jnp.concatenate([m_gu, m_att], axis=1)
-    back = lax.all_to_all(back.reshape(nd, rows, 1, -1), "dp", split_axis=0, concat_axis=2, tiled=True)
-    back = back.reshape(rows, nd, -1).astype(jnp.float32)
+    hid = ns * ffr
+    back_gu = jnp.transpose(back_gu[:, :rows].astype(jnp.float32), (1, 0, 2))
+    m_att = jnp.transpose(back_att[:, :rows].astype(jnp.float32), (1, 0, 2))
 
     def whole_hidden(m):
         return jnp.transpose(m.reshape(rows, nd, ns, ffr), (0, 2, 1, 3)).reshape(rows, -1)
 
-    m_gate, m_up = whole_hidden(back[:, :, :hid]), whole_hidden(back[:, :, hid : 2 * hid])
-    m_qkv = back[:, :, 2 * hid : 2 * hid + wq].reshape(rows, -1)
-    g_out = back[:, :, 2 * hid + wq :].reshape(rows, -1)
+    m_gate, m_up = whole_hidden(back_gu[:, :, :hid]), whole_hidden(back_gu[:, :, hid:])
+    tiles = [None] * 15
+    for j in range(4):
+        tiles[2 * j], tiles[2 * j + 1] = m_att[:, j, :128], m_att[:, j, 128:256]
+        tiles[late[j][0]] = m_att[:, j, 256:384]
+        if late[j][1] is not None:
+            tiles[late[j][1]] = m_att[:, j, 384:512]
+    m_qkv = jnp.concatenate(tiles, axis=1)
+    g_out = jnp.concatenate([m_att[:, j, 512:] for j in range(4)] + [m_att[:, 3, 384:512]], axis=1)
 
     def weigh(w, m):
         return jnp.sum(w.astype(jnp.float32) * m, axis=1)
@@ -748,7 +1105,7 @@
     )
     fits = mesh.shape["seq"] == 8 and mesh.shape["dp"] == 4
     return jax.shard_map(
-        shards_by_kernels if fits else shards,
+        shards_by_kernel if fits else shards,
         mesh=mesh,
         in_specs=placed,
         out_specs=(

time: 442 us -> 269 us (0.61)
  waiting for transfers between devices: 172 us -> 0 us
  Pallas kernels: 121 us -> 241 us
  matrix products: 43.6 us -> 0 us
  local copies, waits for them, and re-layouts: 42.9 us -> 14.2 us
  other arithmetic: 24.9 us -> 9.7 us
  blocking collectives: 15.1 us -> 0 us
  between operations: 17.6 us -> 3.76 us
    reduce_scatter x5 -> x0, waiting for transfers between devices: 138 us -> none  [the longest x1 38.5 us: shards_by_kernels(): lax.psum_scatter(low(contract_rows(mn_all, gboth)), 'seq', scatter_dimens...]
    pallas_call x1, Pallas kernels: 121 us -> 241 us  [layer(): pl.pallas_call(layer_kernel, out_shape=[jax.ShapeDtypeStruct(*o) for o in...]
    dot_general x15 -> x0, matrix products: 43.6 us -> none  [the longest x4 11.4 us: contract_cols(): lax.dot_general(left_mat, right_mat, (((1,), (1,)), ((), ())), preferred_...]
    unnamed x8 -> x0, waiting for transfers between devices: 20.4 us -> none
    all_to_all x1 -> x0, blocking collectives: 15.1 us -> none  [shards_by_kernels(): lax.all_to_all(cut, 'dp', split_axis=1, concat_axis=0, tiled=True)]
    all_gather x1 -> x0, waiting for transfers between devices: 13.8 us -> none  [shards_by_kernels(): att_all = lax.all_gather(att, 'dp', axis=0, tiled=True)]
    unnamed x90 -> x48, local copies, waits for them, and re-layouts: 17.4 us -> 5.37 us
    reshape x4 -> x0, local copies, waits for them, and re-layouts: 9 us -> none  [the longest x1 6.87 us: shards_by_kernels(): probs = probs.reshape(KV, groups, tok, length)]
  transfers between devices with their start and end apart: 8 -> 0, of which waited for: 7 -> 0; matrix products, arithmetic and copies ran while one was open for 11% -> 0% of each run, Pallas kernels for 0% -> 0%
where the time goes in v3:
time: 269 us
  Pallas kernels  241 us (90%)
  local copies, waits for them, and re-layouts  14.2 us (5%)
  other arithmetic  9.7 us (4%)
  between operations  3.76 us (1%)
    pallas_call x1, Pallas kernels, layer(): pl.pallas_call(layer_kernel, out_shape=[jax.ShapeDtypeStruct(*o) for o in...  241 us

profile of v3, /device:TPU:0, one launch (start us, length us, event | category | flops | bytes accessed | tf_op | source)
XLA Modules:
  0.0 268.5 jit_solution(16731531035826927330)
XLA Ops:
  0.6 1.0 multiply_convert_fusion
  1.7 0.9 copy-done.9
  2.6 0.7 slice-done
  3.3 0.7 fusion.10.att_send
  4.1 0.7 copy-done.16
  4.7 0.6 fusion.18
  5.4 0.7 iota_compare_fusion.1
  6.2 0.6 copy-done.14
  6.8 0.6 fusion.24
  10.1 0.6 broadcast_in_dim.66.scale_in
  11.0 0.7 copy.53.sin_in
  11.7 0.7 copy.52.cos_in
  12.7 0.7 broadcast_in_dim.63.first_in
  13.9 0.3 reshape_reshape.6
  14.6 0.3 reshape_reshape.7
  14.9 0.9 pad.9.gu_send
  15.8 240.8 %k_layer.1 = (bf16[1,128,1152]{2,1,0:T(8,128)(2,1)}, f32[1,128,1152]{2,1,0:T(8,128)}, bf16[4,48,1536]{2,1,0:T(8,128)(2,1)}, bf16[4,48,768]{2,1,0:T(8,128)(2,1)}, bf16[96,1152]{1,0:T(8,128)(2,1)}) custom-call(bf16[1,128,1152]{2,1,0:T(8,128)(2,1)} %x_in.1, bf16[1,128,1152]{2,1,0:T(8,128)(2,1)} %cot_in.1, s32[128,128]{1,0:T(8,128)} %broadcast_in_dim.63.first_in, ...), custom_call_target="tpu_custom_call" | custom-call | tf_op jit(solution)/shard_map/k_layer/pallas_call | solution.py:971
  256.7 1.1 convert_bitcast_fusion
  258.1 0.4 reshape.101
  258.6 0.5 reshape.102
  259.3 0.4 reshape.103
  259.8 0.5 reshape.104
  260.4 1.2 broadcast_multiply_fusion
  261.6 0.5 add.30
  262.4 0.8 copy-done.3
  263.2 0.9 broadcast_multiply_fusion.2
  264.1 0.7 copy-done.7
  264.8 0.8 fusion.11
  265.7 0.5 add_add_fusion
  266.2 0.8 convert_element_type.59
  267.0 0.7 copy.76
  267.7 0.8 copy.77
  (74 shorter events, 2.4 us)
Async XLA Ops:
  1.7 0.9 copy-start.9
  2.6 0.7 slice-start
  4.1 0.7 copy-start.16
  5.4 0.7 copy-start.15
  6.2 0.7 copy-start.14
  10.9 1.5 copy-start.13
  11.0 2.4 copy-start
  11.0 2.4 copy-start.1
  12.7 0.7 copy-start.12
  260.4 1.7 copy-start.6
  262.3 0.9 copy-start.3
  262.3 1.7 copy-start.10
  262.4 0.8 copy-start.11
  264.1 0.8 copy-start.7
  264.1 0.8 copy-start.8
  264.1 2.1 copy-start.5
  264.8 2.2 copy-start.4
  266.2 1.5 copy-start.2

commit v4 on v3

--- a/solution.py
+++ b/solution.py
@@ -275,13 +275,14 @@
         else:
             pl.when(when)(copy.wait_recv)
 
-    def finish(self):
-        for copy, when in self.open:
+    def finish(self, upto=None):
+        upto = len(self.open) if upto is None else upto
+        for copy, when in self.open[:upto]:
             if when is None:
                 copy.wait_send()
             else:
                 pl.when(when)(copy.wait_send)
-        self.open = []
+        self.open = self.open[upto:]
 
     def order(self, step):
         if step == 0:
@@ -447,25 +448,31 @@
     def __init__(self, net, part, land, add):
         self.net, self.part, self.land, self.add, self.base = net, part, land, add, net.room(6)
 
-    def hop(self, i):
-        net, z = self.net, net_z(self.net)
-
-        @pl.when((i < z) & (z < 3))
+    def stage(self, k):
+        net, z = self.net, self.net.z
+        i = k - 3 + z
+        valid = (i >= 0) & (i < z)
+        i = jnp.clip(i, 0, 3)
+
+        @pl.when(valid & (z < 3))
         def _():
             net.arrive(self.land(i), self.base + i)
             self.add(i, i)
 
-        net.push(self.part(i), self.land(i), self.base + i, net.at(z - 1, net.c), i < z)
-
-        @pl.when((3 - i > z) & (z > 0))
+        net.push(self.part(i), self.land(i), self.base + i, net.at(z - 1, net.c), valid)
+        j = k - z
+        valid = (j >= 0) & (3 - j > z)
+        j = jnp.clip(j, 0, 3)
+
+        @pl.when(valid & (z > 0))
         def _():
-            net.arrive(self.land(4 - i), self.base + 3 + i)
-            self.add(3 - i, 4 - i)
-
-        net.push(self.part(3 - i), self.land(4 - i), self.base + 3 + i, net.at(z + 1, net.c), 3 - i > z)
+            net.arrive(self.land(4 - j), self.base + 3 + j)
+            self.add(3 - j, 4 - j)
+
+        net.push(self.part(3 - j), self.land(4 - j), self.base + 3 + j, net.at(z + 1, net.c), valid)
 
     def own(self):
-        net, z = self.net, net_z(self.net)
+        net, z = self.net, self.net.z
 
         @pl.when(z < 3)
         def _():
@@ -476,10 +483,6 @@
         def _():
             net.arrive(self.land(1 + z), self.base + 6 - z)
             self.add(z, 1 + z)
-
-
-def net_z(net):
-    return net.z
 
 
 def settle(land, wide, rows):
@@ -600,6 +603,7 @@
                 tile = jnp.where(d == 0, spun, jnp.where(d == 2, spun * eighth, tile))
             qkv_send[j, :, 128 * i : 128 * i + 128] = tile.astype(BF)
     a2a_qkv.start()
+    early = len(net.open)
     qkv_land[d] = qkv_send[d, :, :512]
     b.spread(0)
     b.step(1)
@@ -682,7 +686,8 @@
     ms.take()
     dn.take()
     gu.take()
-    net.finish()
+    net.finish(early)
+    sent = len(net.open)
     ats.start()
 
     def by_cols(send, land, width):
@@ -721,9 +726,9 @@
     for n in range(3):
         part = dot_nn(act[...], wd_flat[:, 384 * n : 384 * n + 384]).astype(BF)
         br_send[:, :, 384 * n : 384 * n + 384] = part.reshape(4, tok, 384)
-    br[0].start()
     turn_x[...] = mn_all[...].reshape(span, dim).T
     turn_a[...] = act[...].T
+    net.finish(sent)
     for n in range(2 * hid // 256):
         wgu_flat[:, 256 * n : 256 * n + 256] = dot_nn(turn_x[...], gboth[:, 256 * n : 256 * n + 256]).astype(BF)
         gu_pair[n].start()
@@ -731,6 +736,7 @@
         cols = pl.ds(384 * n, 384)
         wd_flat[:, cols] = dot_nn(turn_a[...], gd_all[:, :, cols].reshape(span, 384)).astype(BF)
         dn_pair[n].start()
+    br[0].start()
 
     def add_gu(block, slot):
         wgu[block, c] = (wgu[block, c].astype(F32) + gu_zone[slot].astype(F32)).astype(BF)
@@ -745,12 +751,12 @@
         pair.take()
     for k in range(4):
         wgu[k, c] = (wgu[k, c].astype(F32) + gu_mate[k].astype(F32)).astype(BF)
+    gu_sum.stage(0)
     for pair in dn_pair:
         pair.take()
     for k in range(4):
         wd[k, c] = (wd[k, c].astype(F32) + dn_mate[k].astype(F32)).astype(BF)
-    gu_sum.hop(0)
-    dn_sum.hop(0)
+    dn_sum.stage(0)
 
     for n in range(3):
         gn[n].take()
@@ -770,8 +776,7 @@
         g_att = g_att + dot_nt(gba[:, 256 * j : 256 * j + 256], wb[j, :, 128:])
     for h in range(H):
         do_heads[h // groups, tok * (h % groups) : tok * (h % groups) + tok, :] = g_att[:, HD * h : HD * h + HD].astype(BF)
-    gu_sum.hop(1)
-    dn_sum.hop(1)
+    gu_sum.stage(1)
 
     kv_pair = [ToMate(net, dkv.at[n, :, other], kv_mate.at[n]) for n in range(2)]
     kv_sum = [ToOwners(net, lambda zz, n=n: dkv.at[n, zz, c], lambda k, n=n: kv_zone.at[n, k], True) for n in range(2)]
@@ -836,7 +841,6 @@
     ats.take()
     cut_o.take()
     turn_x[...] = att_all[...].reshape(span, dim).T
-    pair_o = grads(2, [dot_nn(turn_x[...], cut_land[:, :, o_cols].reshape(span, 256))])
     pair_sum(0)
     lax.fori_loop(3, 6, pull, 0)
     kv_pair[1].start()
@@ -846,15 +850,13 @@
     cut_q.start()
     cut_land[d, :, q_cols] = cut_send[d, :, q_cols]
     pair_sum(1)
-    gu_sum.hop(2)
-    dn_sum.hop(2)
-    sum_o = grads_sum(2, pair_o)
+    pair_o = grads(2, [dot_nn(turn_x[...], cut_land[:, :, o_cols].reshape(span, 256))])
     turn_n[...] = xn_all[...].reshape(span, dim).T
+    br[0].take()
+    block_out[0] = (middle[...] + scale_in[1:2, 0:1] * plane_sum(net, br_send, br_land)).astype(BF)
     cut_q.take()
     pair_q = grads(0, [dot_nn(turn_n[...], cut_land[:, :, q_cols].reshape(span, 256))])
-    br[0].take()
-    block_out[0] = (middle[...] + scale_in[1:2, 0:1] * plane_sum(net, br_send, br_land)).astype(BF)
-    sum_q = grads_sum(0, pair_q)
+    dn_sum.stage(1)
 
     for n in range(2):
         kv_sum[n].take()
@@ -872,6 +874,8 @@
         cut_send[j, :, col : col + 128] = tile.astype(BF)
     cut_l.start()
     cut_land[d, :, l_cols] = cut_send[d, :, l_cols]
+    gu_sum.stage(2)
+    sum_o = grads_sum(2, pair_o)
     cut_l.take()
     last = cut_land[:, :, 384:512].reshape(span, 128)
     cuts = cut_land[:, :, :512].reshape(span, 512)
@@ -884,11 +888,10 @@
     second = jnp.where(d == 3, dot_nn(turn_x[...], last), dot_nn(turn_n[...], last))
     pair_l = grads(1, [dot_nn(turn_n[...], cut_land[:, :, 256:384].reshape(span, 128)), second])
     sum_l = grads_sum(1, pair_l)
+    sum_q = grads_sum(0, pair_q)
+    dn_sum.stage(2)
     back_o = grads_back(2, sum_o)
-    back_q = grads_back(0, sum_q)
     gu_sum.own()
-    dn_sum.own()
-    back_down[...] = wd[z, c]
     wide[...] = wgu[z, c].astype(F32)
     for j in range(4):
         gu_land[j, :rows, :] = wide[pl.ds(j * rows, rows), :].astype(BF)
@@ -896,9 +899,12 @@
     back_g.start()
     back_gu[d] = gu_land[d]
     back_l = grads_back(1, sum_l)
+    back_q = grads_back(0, sum_q)
     for n in range(3):
         gx[n].take()
     input_grad[0] = gmid[...] + norm_pull(plane_sum(net, gx_send, gx_land), x_in[0].astype(F32))
+    dn_sum.own()
+    back_down[...] = wd[z, c]
     for spread in (back_o, back_q, back_g, back_l):
         spread.take()
     net.finish()

time: 269 us -> 227 us (0.84)
  Pallas kernels: 241 us -> 199 us
    pallas_call x1, Pallas kernels: 241 us -> 199 us  [layer(): pl.pallas_call(layer_kernel, out_shape=[jax.ShapeDtypeStruct(*o) for o in...]
where the time goes in v4:
time: 227 us; the launch traced here: 226 us
  Pallas kernels  199 us (88%)
  local copies, waits for them, and re-layouts  14.2 us (6%)
  other arithmetic  9.7 us (4%)
  between operations  3.76 us (2%)
    pallas_call x1, Pallas kernels, layer(): pl.pallas_call(layer_kernel, out_shape=[jax.ShapeDtypeStruct(*o) for o in...  199 us
    unnamed x48, local copies, waits for them, and re-layouts  5.37 us

profile of v4, /device:TPU:0, one launch (start us, length us, event | category | flops | bytes accessed | tf_op | source)
XLA Modules:
  0.0 226.4 jit_solution(16408187010577275761)
XLA Ops:
  0.6 1.0 multiply_convert_fusion
  1.7 0.9 copy-done.9
  2.6 0.7 slice-done
  3.3 0.7 fusion.10.att_send
  4.1 0.7 copy-done.16
  4.7 0.6 fusion.18
  5.4 0.7 iota_compare_fusion.1
  6.2 0.6 copy-done.14
  6.8 0.6 fusion.24
  10.1 0.6 broadcast_in_dim.66.scale_in
  11.0 0.7 copy.53.sin_in
  11.7 0.7 copy.52.cos_in
  12.7 0.7 broadcast_in_dim.63.first_in
  13.9 0.3 reshape_reshape.6
  14.6 0.3 reshape_reshape.7
  14.9 0.9 pad.9.gu_send
  15.8 198.7 %k_layer.1 = (bf16[1,128,1152]{2,1,0:T(8,128)(2,1)}, f32[1,128,1152]{2,1,0:T(8,128)}, bf16[4,48,1536]{2,1,0:T(8,128)(2,1)}, bf16[4,48,768]{2,1,0:T(8,128)(2,1)}, bf16[96,1152]{1,0:T(8,128)(2,1)}) custom-call(bf16[1,128,1152]{2,1,0:T(8,128)(2,1)} %x_in.1, bf16[1,128,1152]{2,1,0:T(8,128)(2,1)} %cot_in.1, s32[128,128]{1,0:T(8,128)} %broadcast_in_dim.63.first_in, ...), custom_call_target="tpu_custom_call" | custom-call | tf_op jit(solution)/shard_map/k_layer/pallas_call | solution.py:977
  214.5 1.1 convert_bitcast_fusion
  215.9 0.4 reshape.101
  216.4 0.5 reshape.102
  217.2 0.4 reshape.103
  217.7 0.5 reshape.104
  218.2 1.2 broadcast_multiply_fusion
  219.4 0.5 add.30
  220.2 0.8 copy-done.3
  221.0 0.9 broadcast_multiply_fusion.2
  222.0 0.7 copy-done.7
  222.7 0.8 fusion.11
  223.5 0.5 add_add_fusion
  224.0 0.8 convert_element_type.59
  224.8 0.7 copy.76
  225.6 0.8 copy.77
  (74 shorter events, 2.4 us)
Async XLA Ops:
  1.7 0.9 copy-start.9
  2.6 0.7 slice-start
  4.1 0.7 copy-start.16
  5.4 0.7 copy-start.15
  6.2 0.7 copy-start.14
  10.9 1.5 copy-start.13
  11.0 2.4 %copy-start = (bf16[36,3072]{1,0:T(8,128)(2,1)S(1)}, bf16[36,3072]{1,0:T(8,128)(2,1)}, u32[]{:S(2)}) copy-start(bf16[36,3072]{1,0:T(8,128)(2,1)} %param.22) | copy-start | bytes 663556
  11.0 2.4 %copy-start.1 = (bf16[36,3072]{1,0:T(8,128)(2,1)S(1)}, bf16[36,3072]{1,0:T(8,128)(2,1)}, u32[]{:S(2)}) copy-start(bf16[36,3072]{1,0:T(8,128)(2,1)} %param.23) | copy-start | bytes 663556
  12.7 0.7 copy-start.12
  218.2 1.7 copy-start.6
  220.1 0.9 copy-start.3
  220.2 1.7 copy-start.10
  220.2 0.8 copy-start.11
  221.9 0.8 copy-start.7
  221.9 0.8 copy-start.8
  222.0 2.1 copy-start.5
  222.7 2.2 copy-start.4
  224.0 1.5 copy-start.2

commit v5 on v4

--- a/solution.py
+++ b/solution.py
@@ -247,7 +247,9 @@
         peers += [self.at(lax.rem(self.z + k, 4), self.c) for k in (1, 2, 3)]
         for peer in peers:
             pl.semaphore_signal(barrier, inc=1, device_id=peer, device_id_type=MESH)
-        pl.semaphore_wait(barrier, len(peers))
+
+    def greeted(self):
+        pl.semaphore_wait(pltpu.get_barrier_semaphore(), 7)
 
     def copy(self, src, dst, send, recv, peer):
         return pltpu.make_async_remote_copy(
@@ -522,10 +524,26 @@
     return total
 
 
+LATE = ((9, 10), (11, 12), (13, 8), (14, None))
+
+
+def column(row):
+    n = row.shape[1]
+    same = lax.broadcasted_iota(jnp.int32, (n, n), 0) == lax.broadcasted_iota(jnp.int32, (n, n), 1)
+    return jnp.sum(jnp.where(same, row, 0.0), axis=1, keepdims=True)
+
+
+def row_of(col):
+    n = col.shape[0]
+    same = lax.broadcasted_iota(jnp.int32, (n, n), 0) == lax.broadcasted_iota(jnp.int32, (n, n), 1)
+    return jnp.sum(jnp.where(same, col, 0.0), axis=0, keepdims=True)
+
+
 def layer_kernel(
-    x_in, cot_in, first_in, scale_in, cos_in, sin_in, att_send, gu_send, down,
+    x_in, cot_in, query, key_w, value, output, gate_w, up_w, down, gain_one, gain_two, freq,
+    doc_starts, keep_mask, keep_rate, seq_order,
     block_out, input_grad, back_gu, back_att, back_down,
-    att_land, gu_land, wide, qkv_land, kv_all, o_heads, bias, wa, wb, wgu, wd,
+    att_send, gu_send, att_land, gu_land, wide, qkv_land, kv_all, o_heads, bias, wa, wb, wgu, wd,
     xn_all, gd_all, mn_all, att_all, q_heads, k_heads, v_heads, probs, middle, act, gboth, turn_x, turn_n, turn_a,
     gn_send, gn_land, br_send, br_land, gu_mate, gu_zone, dn_mate, dn_zone, gmid, do_heads, dkv, kv_mate, kv_zone, kv_tot,
     cut_land, ma_mate, ma_zone, gx_land, sends, recvs,
@@ -557,15 +575,46 @@
     ats = Plane(net, att_all)
 
     net.greet()
+    first_gain = column(gain_one[...])
+    zero = jnp.zeros((att_send.shape[1] - rows, 128), BF)
+    weights = (query, key_w, value)
+
+    def qkv_tile(t):
+        ref, t = (query, t) if t < 9 else (key_w, t - 9) if t < 12 else (value, t - 12)
+        return (ref[:, 128 * t : 128 * t + 128].astype(F32) * first_gain).astype(BF)
+
+    for j in range(4):
+        tiles = [qkv_tile(2 * j), qkv_tile(2 * j + 1), qkv_tile(LATE[j][0])]
+        tiles.append(output[:, 1024:1152] if LATE[j][1] is None else qkv_tile(LATE[j][1]))
+        tiles += [output[:, 256 * j : 256 * j + 128], output[:, 256 * j + 128 : 256 * j + 256]]
+        for i, tile in enumerate(tiles):
+            att_send[j, :rows, 128 * i : 128 * i + 128] = tile
+            att_send[j, rows:, 128 * i : 128 * i + 128] = zero
+    net.greeted()
     a2a_att.start()
     att_land[d] = att_send[d]
     x = x_in[0].astype(F32)
     xn_all[d] = (x * norm_scale(x)).astype(BF)
     xs.start()
+    second_gain = column(gain_two[...])
+    for i, ref in enumerate((gate_w, up_w)):
+        scaled = ref[...].astype(F32) * second_gain
+        for j in range(4):
+            part = [scaled[:, ffr * (4 * k + j) : ffr * (4 * k + j) + ffr] for k in range(8)]
+            gu_send[j, :rows, hid * i : hid * i + hid] = jnp.concatenate(part, axis=1).astype(BF)
+            gu_send[j, rows:, hid * i : hid * i + hid] = jnp.zeros((gu_send.shape[1] - rows, hid), BF)
     a2a_gu.start()
     gu_land[d] = gu_send[d]
-    gd_all[d] = (cot_in[0].astype(F32) * scale_in[1:2, 0:1]).astype(BF)
+    sample = seq_order[d]
+    scale_attn, scale_mlp = [
+        jnp.full((1, 1), keep_mask[sample, i].astype(F32), F32) / jnp.full((1, 1), keep_rate[i], F32) for i in range(2)
+    ]
+    gd_all[d] = (cot_in[0].astype(F32) * scale_mlp).astype(BF)
     wd[z, c] = down[...]
+    position = s * tok + lax.broadcasted_iota(jnp.int32, (tok, 1), 0)
+    angle = position.astype(F32) * freq[...]
+    lane = lax.broadcasted_iota(jnp.int32, angle.shape, 1)
+    cosine, sine = jnp.cos(angle), jnp.where(lax.rem(lane, HD) < HD // 2, -jnp.sin(angle), jnp.sin(angle))
     a2a_att.take()
     settle(att_land, wide, rows)
     own = own_rows(s, blk)
@@ -588,7 +637,6 @@
     xs.take()
     a.take()
 
-    cosine, sine = cos_in[...], sin_in[...]
     eighth = 1.0 / math.sqrt(HD)
     for j in range(4):
         part = dot_nn(xn_all[j], wa[...])
@@ -619,9 +667,12 @@
         for h in (2 * t, 2 * t + 1):
             at = col + HD * (h % 2)
             q_heads[h // groups, tok * (h % groups) : tok * (h % groups) + tok, :] = qkv_land[j, :, at : at + HD]
-    position = s * tok + lax.broadcasted_iota(jnp.int32, (tok, 1), 0)
+    first = jnp.zeros((tok, 1), jnp.int32)
+    for j in range(doc_starts.shape[1]):
+        start = doc_starts[sample, j]
+        first = jnp.where(position >= start, jnp.maximum(first, start), first)
     key = lax.broadcasted_iota(jnp.int32, bias.shape, 1)
-    bias[...] = jnp.where((key <= position) & (key >= first_in[:, 0:1]), 0.0, MASKED)
+    bias[...] = jnp.where((key <= position) & (key >= first), 0.0, MASKED)
 
     kv.step(1)
     kv.give(1)
@@ -670,7 +721,7 @@
         att_all[d, :, 128 * j : 128 * j + 128] = joined(o_heads, j, tok).astype(BF)
     full = att_all[d]
     branch = [dot_nn(full, wb[j, :, 128:]) for j in range(4)] + [dot_nn(full, wb[3, :, :128])]
-    mid = x_in[0].astype(F32) + scale_in[0:1, 0:1] * jnp.concatenate(branch, axis=1)
+    mid = x_in[0].astype(F32) + scale_attn * jnp.concatenate(branch, axis=1)
     middle[...] = mid
     mn_all[d] = (mid * norm_scale(mid)).astype(BF)
     gs.take()
@@ -763,7 +814,7 @@
     mid = middle[...]
     g_mid = cot_in[0].astype(F32) + norm_pull(plane_sum(net, gn_send, gn_land), mid)
     gmid[...] = g_mid
-    gba = (scale_in[0:1, 0:1] * g_mid).astype(BF)
+    gba = (scale_attn * g_mid).astype(BF)
     for j in range(4):
         cut_send[j, :, 512:768] = gba[:, 256 * j : 256 * j + 256]
     cut_send[3, :, 384:512] = gba[:, 1024:1152]
@@ -853,7 +904,7 @@
     pair_o = grads(2, [dot_nn(turn_x[...], cut_land[:, :, o_cols].reshape(span, 256))])
     turn_n[...] = xn_all[...].reshape(span, dim).T
     br[0].take()
-    block_out[0] = (middle[...] + scale_in[1:2, 0:1] * plane_sum(net, br_send, br_land)).astype(BF)
+    block_out[0] = (middle[...] + scale_mlp * plane_sum(net, br_send, br_land)).astype(BF)
     cut_q.take()
     pair_q = grads(0, [dot_nn(turn_n[...], cut_land[:, :, q_cols].reshape(span, 256))])
     dn_sum.stage(1)
@@ -910,7 +961,7 @@
     net.finish()
 
 
-def layer(x, cot, first, scale, cosine, sine, att_send, gu_send, down):
+def layer(x, cot, weights, down, gains, freq, doc_starts, keep_mask, keep_rate, seq_order):
     tok, dim = x.shape[1:]
     ns = 8
     length = tok * ns
@@ -919,19 +970,18 @@
     blk = dim // ns
     span = 4 * tok
     vm = pl.BlockSpec(memory_space=pltpu.VMEM)
-    outs = [
-        ((1, tok, dim), BF),
-        ((1, tok, dim), F32),
-        (gu_send.shape, BF),
-        (att_send.shape, BF),
-        (down.shape, BF),
-    ]
+    sm = pl.BlockSpec(memory_space=pltpu.SMEM)
+    padded = blk // 4 + -(blk // 4) % 16
+    att_pack, gu_pack = ((4, padded, 768), BF), ((4, padded, 2 * hid), BF)
+    outs = [((1, tok, dim), BF), ((1, tok, dim), F32), gu_pack, att_pack, (down.shape, BF)]
     plane = ((4, tok, dim), BF)
     wide_cut = ((4, tok, 512), BF)
     three = ((KV, 3 * tok, HD), BF)
     scratch = [
-        (att_send.shape, BF),
-        (gu_send.shape, BF),
+        att_pack,
+        gu_pack,
+        att_pack,
+        gu_pack,
         ((blk, 2 * hid), F32),
         wide_cut,
         ((4, 2, tok, 2 * KV * HD), BF),
@@ -977,12 +1027,61 @@
     return pl.pallas_call(
         layer_kernel,
         out_shape=[jax.ShapeDtypeStruct(*o) for o in outs],
-        in_specs=[vm] * 9,
+        in_specs=[vm] * 12 + [sm] * 4,
         out_specs=[vm] * len(outs),
         scratch_shapes=[pltpu.VMEM(*t) for t in scratch] + [pltpu.SemaphoreType.DMA((320,)), pltpu.SemaphoreType.DMA((256,))],
         compiler_params=pltpu.CompilerParams(collective_id=0, has_side_effects=True, vmem_limit_bytes=LIMIT),
         name="k_layer",
-    )(x, cot, first, scale, cosine, sine, att_send, gu_send, down)
+    )(x, cot, *weights, down, *gains, freq, doc_starts, keep_mask, keep_rate, seq_order)
+
+
+def grads_kernel(
+    query, key_w, value, gate_w, up_w, gain_one, gain_two, block_in, input_in, back_gu, back_att, back_down,
+    block_out, input_out, norm_one, g_query, g_key, g_value, g_output, norm_two, g_gate, g_up, g_down,
+):
+    rows, ffr = query.shape[0], back_down.shape[0]
+    hid = 8 * ffr
+    block_out[...] = block_in[...]
+    input_out[...] = input_in[...]
+    g_down[...] = back_down[...].astype(F32)
+    gain = column(gain_one[...])
+    total = jnp.zeros((rows, 128), F32)
+    for j in range(4):
+        for i, t in enumerate((2 * j, 2 * j + 1, LATE[j][0], LATE[j][1])):
+            m = back_att[j, :rows, 128 * i : 128 * i + 128].astype(F32)
+            if t is None:
+                g_output[:, 1024:1152] = m
+                continue
+            w, g, t = (query, g_query, t) if t < 9 else (key_w, g_key, t - 9) if t < 12 else (value, g_value, t - 12)
+            cols = slice(128 * t, 128 * t + 128)
+            total = total + w[:, cols].astype(F32) * m
+            g[:, cols] = m * gain
+        g_output[:, 256 * j : 256 * j + 256] = back_att[j, :rows, 512:768].astype(F32)
+    norm_one[...] = row_of(jnp.sum(total, axis=1, keepdims=True))
+    gain = column(gain_two[...])
+    total = jnp.zeros((rows, 4 * ffr), F32)
+    for i, (w, g) in enumerate(((gate_w, g_gate), (up_w, g_up))):
+        parts = [back_gu[j, :rows, hid * i : hid * i + hid].astype(F32) for j in range(4)]
+        for k in range(8):
+            m = jnp.concatenate([part[:, ffr * k : ffr * k + ffr] for part in parts], axis=1)
+            cols = slice(4 * ffr * k, 4 * ffr * k + 4 * ffr)
+            total = total + w[:, cols].astype(F32) * m
+            g[:, cols] = m * gain
+    norm_two[...] = row_of(jnp.sum(total, axis=1, keepdims=True))
+
+
+def gradients(query, key_w, value, output, gate_w, up_w, gains, results):
+    block, grad, back_gu, back_att, back_down = results
+    shapes = [grad.shape, gains[0].shape] + [w.shape for w in (query, key_w, value, output)]
+    shapes += [gains[1].shape, gate_w.shape, up_w.shape, back_down.shape]
+    vm = pl.BlockSpec(memory_space=pltpu.VMEM)
+    return pl.pallas_call(
+        grads_kernel,
+        out_shape=[jax.ShapeDtypeStruct(block.shape, BF)] + [jax.ShapeDtypeStruct(t, F32) for t in shapes],
+        in_specs=[vm] * 12,
+        out_specs=[vm] * 11,
+        name="k_grads",
+    )(query, key_w, value, gate_w, up_w, *gains, block, grad, back_gu, back_att, back_down)
 
 
 def shards_by_kernel(
@@ -1002,93 +1101,17 @@
     keep_rate,
     seq_order,
 ):
-    tok = hidden_in.shape[1]
-    ns, nd = lax.axis_size("seq"), lax.axis_size("dp")
-    length = tok * ns
     rows = query_weight.shape[0]
-    ffr = down_weight.shape[0]
-    dim = hidden_in.shape[2]
-    groups = H // KV
-    nq, nk = H * HD, KV * HD
-    score_scale = 1.0 / math.sqrt(HD)
-    me_s, me_d = lax.axis_index("seq"), lax.axis_index("dp")
-    sample = jnp.sum(jnp.where(jnp.arange(nd) == me_d, seq_order, 0))
-    pick = jnp.arange(nd) == sample
-    doc_begin = jnp.sum(jnp.where(pick[:, None], doc_starts, 0), axis=0)
-    keep_flags = jnp.sum(jnp.where(pick[:, None], keep_mask, 0), axis=0).astype(jnp.float32)
-    attn_scale = keep_flags[0] / keep_rate[0]
-    mlp_scale = keep_flags[1] / keep_rate[1]
-    positions = me_s * tok + jnp.arange(tok)
-    first = jnp.max(jnp.where(doc_begin[None, :] <= positions[:, None], doc_begin[None, :], 0), axis=1)
-    gain_one, gain_two = attn_norm[:, None], mlp_norm[:, None]
-
-    qkv_rows = low(jnp.concatenate([query_weight, key_weight, value_weight], axis=1).astype(jnp.float32) * gain_one)
-    def split_hidden(w):
-        w = low(w.astype(jnp.float32) * gain_two).reshape(rows, ns, nd, ffr)
-        w = jnp.transpose(w, (0, 2, 1, 3)).reshape(rows, nd * ns * ffr)
-        return w
-
-    gu = jnp.concatenate(
-        [split_hidden(gate_weight).reshape(rows, nd, -1), split_hidden(up_weight).reshape(rows, nd, -1)], axis=2
+    freq = ROPE_BASE ** (-2.0 * jnp.arange(HD // 2, dtype=F32) / HD)
+    freq = jnp.tile(freq, 128 // freq.shape[0])[None]
+    gains = (attn_norm.reshape(1, rows), mlp_norm.reshape(1, rows))
+    weights = (query_weight, key_weight, value_weight, output_weight, gate_weight, up_weight)
+    results = layer(
+        hidden_in, cotangent, weights, down_weight, gains, freq, doc_starts, keep_mask, keep_rate, seq_order
     )
-    late = [(9, 10), (11, 12), (13, 8), (14, None)]
-    tiles = []
-    for j in range(4):
-        first_late, second_late = late[j]
-        qkv_tile = lambda t: qkv_rows[:, 128 * t : 128 * t + 128]
-        second = output_weight[:, 1024:] if second_late is None else qkv_tile(second_late)
-        tiles.append(
-            jnp.concatenate(
-                [qkv_rows[:, 256 * j : 256 * j + 256], qkv_tile(first_late), second, output_weight[:, 256 * j : 256 * j + 256]], axis=1
-            )
-        )
-    att_send = jnp.stack(tiles)
-    pad = ((0, 0), (0, -rows % 16), (0, 0))
-    inverse_freq = ROPE_BASE ** (-2.0 * jnp.arange(HD // 2, dtype=jnp.float32) / HD)
-    angles = positions.astype(jnp.float32)[:, None] * inverse_freq[None, :]
-    cosine = jnp.tile(jnp.cos(angles), (1, 4))
-    sine = jnp.tile(jnp.concatenate([-jnp.sin(angles), jnp.sin(angles)], axis=1), (1, 2))
-    scale = jnp.broadcast_to(jnp.stack([attn_scale, mlp_scale])[:, None], (2, 128))
-    firsts = jnp.broadcast_to(first[:, None], (tok, 128))
-    block_output, input_grad, back_gu, back_att, m_down = layer(
-        hidden_in, cotangent, firsts, scale, cosine, sine, jnp.pad(att_send, pad), jnp.pad(jnp.transpose(gu, (1, 0, 2)), pad), down_weight
-    )
-    hid = ns * ffr
-    back_gu = jnp.transpose(back_gu[:, :rows].astype(jnp.float32), (1, 0, 2))
-    m_att = jnp.transpose(back_att[:, :rows].astype(jnp.float32), (1, 0, 2))
-
-    def whole_hidden(m):
-        return jnp.transpose(m.reshape(rows, nd, ns, ffr), (0, 2, 1, 3)).reshape(rows, -1)
-
-    m_gate, m_up = whole_hidden(back_gu[:, :, :hid]), whole_hidden(back_gu[:, :, hid:])
-    tiles = [None] * 15
-    for j in range(4):
-        tiles[2 * j], tiles[2 * j + 1] = m_att[:, j, :128], m_att[:, j, 128:256]
-        tiles[late[j][0]] = m_att[:, j, 256:384]
-        if late[j][1] is not None:
-            tiles[late[j][1]] = m_att[:, j, 384:512]
-    m_qkv = jnp.concatenate(tiles, axis=1)
-    g_out = jnp.concatenate([m_att[:, j, 512:] for j in range(4)] + [m_att[:, 3, 384:512]], axis=1)
-
-    def weigh(w, m):
-        return jnp.sum(w.astype(jnp.float32) * m, axis=1)
-
-    m_q, m_k, m_v = m_qkv[:, :nq], m_qkv[:, nq : nq + nk], m_qkv[:, nq + nk :]
-    g_norm_one = weigh(query_weight, m_q) + weigh(key_weight, m_k) + weigh(value_weight, m_v)
-    g_norm_two = weigh(gate_weight, m_gate) + weigh(up_weight, m_up)
-    return (
-        block_output,
-        input_grad,
-        g_norm_one,
-        m_q * gain_one,
-        m_k * gain_one,
-        m_v * gain_one,
-        g_out,
-        g_norm_two,
-        m_gate * gain_two,
-        m_up * gain_two,
-        m_down.astype(jnp.float32),
-    )
+    outs = list(gradients(*weights, gains, results))
+    outs[2], outs[7] = outs[2].reshape(rows), outs[7].reshape(rows)
+    return tuple(outs)
 
 
 def solution(mesh):

time: 227 us -> 205 us (0.903)
  local copies, waits for them, and re-layouts: 14.2 us -> 1.34 us
  other arithmetic: 9.7 us -> 0.01 us
  between operations: 3.76 us -> 0.67 us
  Pallas kernels: 199 us -> 202 us
    unnamed x48 -> x3, local copies, waits for them, and re-layouts: 5.37 us -> 0.74 us
    pallas_call x0 -> x1, Pallas kernels: none -> 3.67 us  [gradients(): pl.pallas_call(grads_kernel, out_shape=[jax.ShapeDtypeStruct(block.shape,...]
    mul x3 -> x0, other arithmetic: 2.89 us -> none  [the longest x1 1.2 us: shards_by_kernel(): m_up * gain_two]
    reshape x8 -> x0, local copies, waits for them, and re-layouts: 2.47 us -> none  [the longest x2 1.1 us: whole_hidden(): jnp.transpose(m.reshape(rows, nd, ns, ffr), (0, 2, 1, 3)).reshape(rows, -1)]
where the time goes in v5:
time: 205 us; the launch traced here: 204 us
  Pallas kernels  202 us (99%)
    pallas_call x1, Pallas kernels, layer(): pl.pallas_call(layer_kernel, out_shape=[jax.ShapeDtypeStruct(*o) for o in...  199 us

profile of v5, /device:TPU:0, one launch (start us, length us, event | category | flops | bytes accessed | tf_op | source)
XLA Modules:
  0.0 204.4 jit_solution(16632648941832208595)
XLA Ops:
  0.7 0.0 copy-start
  0.7 0.6 broadcast_in_dim_tile.3.freq
  1.3 0.1 copy-done
  1.3 0.7 copy.26.keep_mask
  2.0 198.7 %k_layer.1 = (bf16[1,128,1152]{2,1,0:T(8,128)(2,1)}, f32[1,128,1152]{2,1,0:T(8,128)}, bf16[4,48,1536]{2,1,0:T(8,128)(2,1)}, bf16[4,48,768]{2,1,0:T(8,128)(2,1)}, bf16[96,1152]{1,0:T(8,128)(2,1)}) custom-call(bf16[1,128,1152]{2,1,0:T(8,128)(2,1)} %x_in.1, bf16[1,128,1152]{2,1,0:T(8,128)(2,1)} %cot_in.1, bf16[36,1152]{1,0:T(8,128)(2,1)} %query.3, ...), custom_call_target="tpu_custom_call" | custom-call | tf_op jit(solution)/shard_map/k_layer/pallas_call | solution.py:1027
  200.7 3.7 %k_grads.1 = (bf16[1,128,1152]{2,1,0:T(8,128)(2,1)}, f32[1,128,1152]{2,1,0:T(8,128)}, f32[1,36]{1,0:T(1,128)}, f32[36,1152]{1,0:T(8,128)}, f32[36,384]{1,0:T(8,1...) custom-call(bf16[36,1152]{1,0:T(8,128)(2,1)} %query.3, ...), custom_call_target="tpu_custom_call" | custom-call | tf_op jit(solution)/shard_map/k_grads/pallas_call | solution.py:1078
  (2 shorter events, 0.0 us)
Async XLA Ops:
  0.7 0.7 copy-start

commit v6 on v5

--- a/solution.py
+++ b/solution.py
@@ -261,14 +261,14 @@
             device_id_type=MESH,
         )
 
-    def push(self, src, dst, recv, peer, when=None):
+    def push(self, owner, src, dst, recv, peer, when=None):
         copy = self.copy(src, dst, self.count, recv, peer)
         self.count += 1
         if when is None:
             copy.start()
         else:
             pl.when(when)(copy.start)
-        self.open.append((copy, when))
+        self.open.append((copy, when, owner))
 
     def arrive(self, dst, recv, when=None):
         copy = self.copy(dst, dst, 0, recv, self.mate)
@@ -277,14 +277,16 @@
         else:
             pl.when(when)(copy.wait_recv)
 
-    def finish(self, upto=None):
-        upto = len(self.open) if upto is None else upto
-        for copy, when in self.open[:upto]:
-            if when is None:
+    def finish(self, *owners):
+        kept = []
+        for copy, when, owner in self.open:
+            if owners and owner not in owners:
+                kept.append((copy, when, owner))
+            elif when is None:
                 copy.wait_send()
             else:
                 pl.when(when)(copy.wait_send)
-        self.open = self.open[upto:]
+        self.open = kept
 
     def order(self, step):
         if step == 0:
@@ -301,8 +303,8 @@
     def start(self):
         net = self.net
         own = self.block(net.z, net.c)
-        net.push(own, own, self.base + net.z, net.at(net.z + 1, net.c), net.z < 3)
-        net.push(own, own, self.base + net.z, net.at(net.z - 1, net.c), net.z > 0)
+        net.push(self, own, own, self.base + net.z, net.at(net.z + 1, net.c), net.z < 3)
+        net.push(self, own, own, self.base + net.z, net.at(net.z - 1, net.c), net.z > 0)
 
     def step(self, k):
         net = self.net
@@ -310,7 +312,7 @@
         block = self.block(b, net.c)
         net.arrive(block, self.base + b)
         to = jnp.where(b < net.z, net.z + 1, net.z - 1)
-        net.push(block, block, self.base + b, net.at(to, net.c), (to >= 0) & (to <= 3))
+        net.push(self, block, block, self.base + b, net.at(to, net.c), (to >= 0) & (to <= 3))
 
 
 class Lines(Chain):
@@ -321,16 +323,51 @@
         super().start()
         self.give(0)
 
-    def give(self, k):
+    def onward(self, b):
+        to = jnp.where(b < self.net.z, self.net.z + 1, self.net.z - 1)
+        return to, (to >= 0) & (to <= 3)
+
+    def step(self, k):
         net = self.net
         b = net.order(k)
         block = self.block(b, net.c)
-        net.push(block, block, self.base + 4 + b, net.mate)
+        to, on = self.onward(b)
+        net.arrive(block, self.base + b, on)
+        net.push(self, block, block, self.base + b, net.at(to, net.c), on)
+
+    def give(self, k):
+        net = self.net
+        b = net.order(k)
+        block = self.block(b, net.c)
+        if k:
+            net.arrive(block, self.base + b, jnp.logical_not(self.onward(b)[1]))
+        net.push(self, block, block, self.base + 4 + b, net.mate)
 
     def take(self):
         net = self.net
         for b in range(4):
             net.arrive(self.block(b, 1 - net.c), self.base + 4 + b)
+
+
+class Rising(Lines):
+    def start(self):
+        net = self.net
+        own = self.block(net.z, net.c)
+        net.push(self, own, own, self.base + net.z, net.at(net.z + 1, net.c), net.z < 3)
+        net.push(self, own, own, self.base + 4 + net.z, net.mate)
+
+    def step(self, k):
+        net = self.net
+        b = jnp.maximum(net.z - k, 0)
+        block = self.block(b, net.c)
+        net.arrive(block, self.base + b, net.z >= k)
+        net.push(self, block, block, self.base + b, net.at(net.z + 1, net.c), (net.z >= k) & (net.z < 3))
+        net.push(self, block, block, self.base + 4 + b, net.mate, net.z >= k)
+
+    def take(self):
+        net = self.net
+        for b in range(4):
+            net.arrive(self.block(b, 1 - net.c), self.base + 4 + b, net.z >= b)
 
 
 class Slices(Chain):
@@ -350,9 +387,9 @@
         net = self.net
         b = net.order(k)
         block = self.part(net.d, b, net.c)
-        net.push(block, block, self.base + 4 + b, net.across(0))
-        net.push(block, block, self.base + 8 + b, net.across(1))
-        net.push(block, block, self.base + 20 + b, net.mate)
+        net.push(self, block, block, self.base + 4 + b, net.across(0))
+        net.push(self, block, block, self.base + 8 + b, net.across(1))
+        net.push(self, block, block, self.base + 20 + b, net.mate)
 
     def pass_on(self, k):
         net = self.net
@@ -361,8 +398,8 @@
             block = self.part(net.plane[kind], b, net.c)
             net.arrive(block, self.base + 4 + 4 * kind + b)
             half = self.part(net.plane[kind], b, net.c, kind)
-            net.push(half, half, self.base + 12 + 4 * kind + b, net.across(1 - kind))
-            net.push(block, block, self.base + 24 + 4 * kind + b, net.mate)
+            net.push(self, half, half, self.base + 12 + 4 * kind + b, net.across(1 - kind))
+            net.push(self, block, block, self.base + 24 + 4 * kind + b, net.mate)
 
     def corner(self, k):
         net = self.net
@@ -371,7 +408,7 @@
             half = self.part(net.plane[2], b, net.c, kind)
             net.arrive(half, self.base + 12 + 4 * kind + b)
         block = self.part(net.plane[2], b, net.c)
-        net.push(block, block, self.base + 32 + b, net.mate)
+        net.push(self, block, block, self.base + 32 + b, net.mate)
 
     def take(self):
         net = self.net
@@ -390,14 +427,14 @@
         net = self.net
         own = self.full.at[net.d]
         for kind in (0, 1):
-            net.push(own, own, self.base + kind, net.across(kind))
+            net.push(self, own, own, self.base + kind, net.across(kind))
 
     def pass_on(self):
         net = self.net
         for kind in (0, 1):
             net.arrive(self.full.at[net.plane[kind]], self.base + kind)
             half = self.full.at[net.plane[kind], pl.ds(kind * self.half, self.half)]
-            net.push(half, half, self.base + 2 + kind, net.across(1 - kind))
+            net.push(self, half, half, self.base + 2 + kind, net.across(1 - kind))
 
     def take(self):
         net = self.net
@@ -412,7 +449,7 @@
     def start(self):
         net = self.net
         for kind in (2, 0, 1):
-            net.push(self.send(net.plane[kind]), self.land(net.d), self.base + kind, net.across(kind))
+            net.push(self, self.send(net.plane[kind]), self.land(net.d), self.base + kind, net.across(kind))
 
     def take(self):
         for kind in range(3):
@@ -424,7 +461,7 @@
         self.net, self.send, self.land, self.base = net, send, land, net.room(1)
 
     def start(self):
-        self.net.push(self.send, self.land, self.base, self.net.mate)
+        self.net.push(self, self.send, self.land, self.base, self.net.mate)
 
     def take(self):
         self.net.arrive(self.land, self.base)
@@ -438,7 +475,7 @@
         net = self.net
         for k in (3, 2, 1):
             to = lax.rem(net.z - k + 4, 4)
-            net.push(self.part(to), self.land(k - 1), self.base + k - 1, net.at(to, net.c), (net.z >= k) if self.down else None)
+            net.push(self, self.part(to), self.land(k - 1), self.base + k - 1, net.at(to, net.c), (net.z >= k) if self.down else None)
 
     def take(self):
         net = self.net
@@ -461,7 +498,7 @@
             net.arrive(self.land(i), self.base + i)
             self.add(i, i)
 
-        net.push(self.part(i), self.land(i), self.base + i, net.at(z - 1, net.c), valid)
+        net.push(self, self.part(i), self.land(i), self.base + i, net.at(z - 1, net.c), valid)
         j = k - z
         valid = (j >= 0) & (3 - j > z)
         j = jnp.clip(j, 0, 3)
@@ -471,7 +508,7 @@
             net.arrive(self.land(4 - j), self.base + 3 + j)
             self.add(3 - j, 4 - j)
 
-        net.push(self.part(3 - j), self.land(4 - j), self.base + 3 + j, net.at(z + 1, net.c), valid)
+        net.push(self, self.part(3 - j), self.land(4 - j), self.base + 3 + j, net.at(z + 1, net.c), valid)
 
     def own(self):
         net, z = self.net, self.net.z
@@ -487,9 +524,16 @@
             self.add(z, 1 + z)
 
 
-def settle(land, wide, rows):
+def settle(land, wide, rows, cols=slice(None)):
     for j in range(4):
-        wide[pl.ds(j * rows, rows), : land.shape[2]] = land[j, :rows, :].astype(F32)
+        wide[pl.ds(j * rows, rows), :] = land[j, :rows, cols].astype(F32)
+    return wide[...].astype(BF)
+
+
+def unsettle(block, wide, land, rows, cols):
+    wide[:, : block.shape[1]] = block
+    for j in range(4):
+        land[j, :rows, cols] = wide[pl.ds(j * rows, rows), : block.shape[1]].astype(BF)
 
 
 def turned(tile, cosine, sine):
@@ -543,7 +587,7 @@
     x_in, cot_in, query, key_w, value, output, gate_w, up_w, down, gain_one, gain_two, freq,
     doc_starts, keep_mask, keep_rate, seq_order,
     block_out, input_grad, back_gu, back_att, back_down,
-    att_send, gu_send, att_land, gu_land, wide, qkv_land, kv_all, o_heads, bias, wa, wb, wgu, wd,
+    att_land, gu_land, wide, qkv_land, kv_all, o_heads, bias, wa, wb, wgu, wd,
     xn_all, gd_all, mn_all, att_all, q_heads, k_heads, v_heads, probs, middle, act, gboth, turn_x, turn_n, turn_a,
     gn_send, gn_land, br_send, br_land, gu_mate, gu_zone, dn_mate, dn_zone, gmid, do_heads, dkv, kv_mate, kv_zone, kv_tot,
     cut_land, ma_mate, ma_zone, gx_land, sends, recvs,
@@ -553,30 +597,37 @@
     rows = dim // 32
     blk = 4 * rows
     ffr = down.shape[0]
-    hid = 8 * ffr
+    hid, quad = 8 * ffr, 4 * ffr
     d, z, c, s = net.d, net.z, net.c, net.s
     span, length = 4 * tok, 8 * tok
     groups = H // KV
-    qkv_send = cut_send = act.reshape(4, tok, hid)
+    padded = att_land.shape[1]
+    att_send = qkv_send = cut_send = act.reshape(4, tok, hid)
+    gu_send = gboth.reshape(4, tok, 2 * hid)
     gx_send, gs_heads = gd_all, gboth
     m_att = wb.reshape(4, 4, 2, blk, 384)
 
-    a2a_att = Spread(net, lambda j: att_send.at[j], lambda j: att_land.at[j])
-    a2a_gu = Spread(net, lambda j: gu_send.at[j], lambda j: gu_land.at[j])
-    a2a_qkv = Spread(net, lambda j: qkv_send.at[j, :, pl.ds(0, 512)], lambda j: qkv_land.at[j])
-    a = Lines(net, lambda zz, core: wa.at[own_rows(zz * 2 + core, blk)])
+    first_cols, late_cols = pl.ds(0, 256), pl.ds(256, 256)
+    a2a_att = Spread(net, lambda j: att_send.at[j, pl.ds(0, padded)], lambda j: att_land.at[j])
+    a2a_gu = Spread(net, lambda j: gu_send.at[j, pl.ds(0, padded)], lambda j: gu_land.at[j])
+    a2a_qkv = [
+        Spread(net, lambda j, cols=cols: qkv_send.at[j, :, cols], lambda j, cols=cols: qkv_land.at[j, :, cols])
+        for cols in (late_cols, first_cols)
+    ]
+    a = [Lines(net, lambda zz, core, cols=cols: wa.at[own_rows(zz * 2 + core, blk), cols]) for cols in (late_cols, first_cols)]
     b = Slices(net, wb, blk)
-    gu = Lines(net, lambda zz, core: wgu.at[zz, core])
+    gu = [Lines(net, lambda zz, core, h=h: wgu.at[zz, core, :, pl.ds(hid * h, hid)]) for h in range(2)]
     dn = Lines(net, lambda zz, core: wd.at[zz, core])
-    kv = Lines(net, lambda zz, core: kv_all.at[zz, core])
+    kv = Rising(net, lambda zz, core: kv_all.at[zz, core])
     xs = Plane(net, xn_all)
     gs = Plane(net, gd_all)
     ms = Plane(net, mn_all)
     ats = Plane(net, att_all)
 
+    kv_all[...] = jnp.zeros_like(kv_all)
     net.greet()
     first_gain = column(gain_one[...])
-    zero = jnp.zeros((att_send.shape[1] - rows, 128), BF)
+    zero = jnp.zeros((padded - rows, 128), BF)
     weights = (query, key_w, value)
 
     def qkv_tile(t):
@@ -589,10 +640,10 @@
         tiles += [output[:, 256 * j : 256 * j + 128], output[:, 256 * j + 128 : 256 * j + 256]]
         for i, tile in enumerate(tiles):
             att_send[j, :rows, 128 * i : 128 * i + 128] = tile
-            att_send[j, rows:, 128 * i : 128 * i + 128] = zero
+            att_send[j, rows:padded, 128 * i : 128 * i + 128] = zero
     net.greeted()
     a2a_att.start()
-    att_land[d] = att_send[d]
+    att_land[d] = att_send[d, :padded, :]
     x = x_in[0].astype(F32)
     xn_all[d] = (x * norm_scale(x)).astype(BF)
     xs.start()
@@ -600,11 +651,12 @@
     for i, ref in enumerate((gate_w, up_w)):
         scaled = ref[...].astype(F32) * second_gain
         for j in range(4):
-            part = [scaled[:, ffr * (4 * k + j) : ffr * (4 * k + j) + ffr] for k in range(8)]
-            gu_send[j, :rows, hid * i : hid * i + hid] = jnp.concatenate(part, axis=1).astype(BF)
-            gu_send[j, rows:, hid * i : hid * i + hid] = jnp.zeros((gu_send.shape[1] - rows, hid), BF)
-    a2a_gu.start()
-    gu_land[d] = gu_send[d]
+            for h in range(2):
+                part = [scaled[:, ffr * (4 * k + j) : ffr * (4 * k + j) + ffr] for k in range(4 * h, 4 * h + 4)]
+                cols = slice(hid * h + quad * i, hid * h + quad * i + quad)
+                gu_send[j, :rows, cols] = jnp.concatenate(part, axis=1).astype(BF)
+                gu_send[j, rows:padded, cols] = jnp.zeros((padded - rows, quad), BF)
+    gu_land[d] = gu_send[d, :padded, :]
     sample = seq_order[d]
     scale_attn, scale_mlp = [
         jnp.full((1, 1), keep_mask[sample, i].astype(F32), F32) / jnp.full((1, 1), keep_rate[i], F32) for i in range(2)
@@ -616,51 +668,67 @@
     lane = lax.broadcasted_iota(jnp.int32, angle.shape, 1)
     cosine, sine = jnp.cos(angle), jnp.where(lax.rem(lane, HD) < HD // 2, -jnp.sin(angle), jnp.sin(angle))
     a2a_att.take()
-    settle(att_land, wide, rows)
     own = own_rows(s, blk)
-    wa[own, :] = wide[:, :512].astype(BF)
-    wb[d, own, :] = wide[:, 384:768].astype(BF)
-    a.start()
-    a.step(1)
-    a.give(1)
+    packed = settle(att_land, wide, rows)
+    wa[own, :] = packed[:, :512]
+    wb[d, own, :] = packed[:, 384:]
+    for line in a:
+        line.start()
+    for k in (1, 2, 3):
+        for line in a:
+            line.step(k)
+        for line in a:
+            line.give(k)
+        if k == 1:
+            xs.pass_on()
+            a2a_gu.start()
+    b.start()
     dn.start()
-    xs.pass_on()
-    a.step(2)
-    a.give(2)
-    b.start()
-    a.step(3)
-    a.give(3)
-    a2a_gu.take()
-    settle(gu_land, wide, rows)
-    wgu[z, c] = wide[...].astype(BF)
-    gu.start()
     xs.take()
-    a.take()
+    a[0].take()
 
     eighth = 1.0 / math.sqrt(HD)
-    for j in range(4):
-        part = dot_nn(xn_all[j], wa[...])
-        for i in range(4):
-            tile = part[:, 128 * i : 128 * i + 128]
-            spun = turned(tile, cosine, sine)
-            if i < 2:
-                tile = spun * eighth
-            elif i == 2:
-                tile = jnp.where(d < 2, spun, tile)
-            else:
-                tile = jnp.where(d == 0, spun, jnp.where(d == 2, spun * eighth, tile))
-            qkv_send[j, :, 128 * i : 128 * i + 128] = tile.astype(BF)
-    a2a_qkv.start()
-    early = len(net.open)
+
+    def project(cols, kinds):
+        part = dot_nn(xn_all[...].reshape(span, dim), wa[:, cols])
+        for j in range(4):
+            for i, kind in enumerate(kinds):
+                tile = part[tok * j : tok * j + tok, 128 * i : 128 * i + 128]
+                spun = turned(tile, cosine, sine)
+                if kind == 1:
+                    tile = jnp.where(d < 2, spun, tile)
+                elif kind == 2:
+                    tile = jnp.where(d == 0, spun, jnp.where(d == 2, spun * eighth, tile))
+                else:
+                    tile = spun * eighth
+                qkv_send[j, :, pl.ds(cols.start + 128 * i, 128)] = tile.astype(BF)
+
+    net.finish(a2a_att)
+    project(late_cols, (1, 2))
+    a2a_qkv[0].start()
+    a[1].take()
+    project(first_cols, (0, 0))
+    a2a_qkv[1].start()
     qkv_land[d] = qkv_send[d, :, :512]
     b.spread(0)
     b.step(1)
     b.spread(1)
-    a2a_qkv.take()
+    a2a_qkv[0].take()
     places = [(0, 256), (0, 384), (1, 256), (1, 384), (2, 256), (3, 256)]
     for i, (j, col) in enumerate(places):
         kv_all[z, c, :, 128 * i : 128 * i + 128] = qkv_land[j, :, col : col + 128]
     kv.start()
+    b.step(2)
+    b.spread(2)
+    a2a_gu.take()
+    for h in range(2):
+        wgu[z, c, :, hid * h : hid * h + hid] = settle(gu_land, wide, rows, slice(hid * h, hid * h + hid))
+    b.step(3)
+    b.spread(3)
+    gu[0].start()
+    b.pass_on(0)
+    b.pass_on(1)
+    a2a_qkv[1].take()
     gs.start()
     for t in range(9):
         j, col = (t // 2, (t % 2) * 128) if t < 8 else (2, 384)
@@ -675,23 +743,13 @@
     bias[...] = jnp.where((key <= position) & (key >= first), 0.0, MASKED)
 
     kv.step(1)
-    kv.give(1)
-    b.step(2)
-    b.spread(2)
     kv.step(2)
-    kv.give(2)
-    b.step(3)
-    b.spread(3)
-    b.pass_on(0)
-    b.pass_on(1)
-    kv.step(3)
-    kv.give(3)
-    dn.step(1)
-    gu.step(1)
-    gs.pass_on()
     b.pass_on(2)
+    b.pass_on(3)
     b.corner(0)
     b.corner(1)
+    kv.step(3)
+    dn.step(1)
     kv.take()
     for j in range(8):
         for k in range(KV):
@@ -703,19 +761,21 @@
         mine = pl.ds(pl.multiple_of(lax.rem(h, groups) * tok, tok), tok)
         score = dot_nt(q_heads[k, mine, :], k_heads[k]) + bias[...]
         expo = jnp.exp(score - jnp.max(score, axis=1, keepdims=True))
-        p = (expo / jnp.sum(expo, axis=1, keepdims=True)).astype(BF)
+        p = (expo * (1.0 / jnp.sum(expo, axis=1, keepdims=True))).astype(BF)
         probs[k, mine, :] = p
         o_heads[k, mine, :] = dot_nn(p, v_heads[k])
         return carry
 
     lax.fori_loop(0, 6, head, 0)
-    b.pass_on(3)
+    dn.step(2)
+    gu[0].step(1)
+    gs.pass_on()
     b.corner(2)
     lax.fori_loop(6, 12, head, 0)
+    dn.step(3)
+    gu[0].step(2)
+    lax.fori_loop(12, 18, head, 0)
     b.corner(3)
-    dn.step(2)
-    gu.step(2)
-    lax.fori_loop(12, 18, head, 0)
     b.take()
     for j in range(H // 2):
         att_all[d, :, 128 * j : 128 * j + 128] = joined(o_heads, j, tok).astype(BF)
@@ -724,22 +784,24 @@
     mid = x_in[0].astype(F32) + scale_attn * jnp.concatenate(branch, axis=1)
     middle[...] = mid
     mn_all[d] = (mid * norm_scale(mid)).astype(BF)
+    ms.start()
+    gu[0].step(3)
+    gu[1].start()
     gs.take()
-    ms.start()
-    for k in (1, 2):
-        dn.give(k)
-        gu.give(k)
-    dn.step(3)
+    dn.give(1)
+    gu[0].give(1)
+    dn.give(2)
+    ms.pass_on()
+    gu[1].step(1)
+    gu[0].give(2)
     dn.give(3)
-    ms.pass_on()
-    gu.step(3)
-    gu.give(3)
+    gu[0].give(3)
+    gu[1].give(1)
     ms.take()
     dn.take()
-    gu.take()
-    net.finish(early)
-    sent = len(net.open)
+    gu[0].take()
     ats.start()
+    net.finish(a2a_gu, *a2a_qkv)
 
     def by_cols(send, land, width):
         return [
@@ -754,60 +816,86 @@
     gn, br, gx = by_cols(gn_send, gn_land, 384), by_cols(br_send, br_land, dim), by_cols(gx_send, gx_land, 384)
     wgu_flat, wd_flat = wgu.reshape(dim, 2 * hid), wd.reshape(hid, dim)
     other = 1 - c
-    gu_pair = [
-        ToMate(net, wgu.at[:, other, :, pl.ds(256 * n, 256)], gu_mate.at[:, :, pl.ds(256 * n, 256)]) for n in range(2 * hid // 256)
-    ]
-    dn_pair = [ToMate(net, wd.at[:, other, :, pl.ds(384 * n, 384)], dn_mate.at[:, :, pl.ds(384 * n, 384)]) for n in range(3)]
-
-    for n in range(hid // 256):
-        cols, ups = pl.ds(256 * n, 256), pl.ds(hid + 256 * n, 256)
-        normed = mn_all[...].reshape(span, dim)
-        gate = dot_nn(normed, wgu_flat[:, cols])
-        up = dot_nn(normed, wgu_flat[:, ups])
-        g_act = dot_nt(gd_all[...].reshape(span, dim), wd_flat[cols, :])
-        sig = jax.nn.sigmoid(gate)
-        swish = gate * sig
-        act[:, cols] = (swish * up).astype(BF)
-        gboth[:, cols] = (g_act * up * (sig * (1.0 + gate * (1.0 - sig)))).astype(BF)
-        gboth[:, ups] = (g_act * swish).astype(BF)
-    for n in range(3):
-        part = dot_nt(gboth[...], wgu_flat[384 * n : 384 * n + 384, :]).astype(BF)
-        gn_send[:, :, 384 * n : 384 * n + 384] = part.reshape(4, tok, 384)
-        gn[n].start()
-    for n in range(3):
-        part = dot_nn(act[...], wd_flat[:, 384 * n : 384 * n + 384]).astype(BF)
-        br_send[:, :, 384 * n : 384 * n + 384] = part.reshape(4, tok, 384)
-    turn_x[...] = mn_all[...].reshape(span, dim).T
-    turn_a[...] = act[...].T
-    net.finish(sent)
-    for n in range(2 * hid // 256):
-        wgu_flat[:, 256 * n : 256 * n + 256] = dot_nn(turn_x[...], gboth[:, 256 * n : 256 * n + 256]).astype(BF)
-        gu_pair[n].start()
-    for n in range(3):
-        cols = pl.ds(384 * n, 384)
-        wd_flat[:, cols] = dot_nn(turn_a[...], gd_all[:, :, cols].reshape(span, 384)).astype(BF)
-        dn_pair[n].start()
-    br[0].start()
-
-    def add_gu(block, slot):
-        wgu[block, c] = (wgu[block, c].astype(F32) + gu_zone[slot].astype(F32)).astype(BF)
+    halves = [pl.ds(hid * h, hid) for h in range(2)]
+    gu_pair = [ToMate(net, wgu.at[:, other, :, cols], gu_mate.at[:, :, cols]) for cols in halves]
+    dn_pair = [ToMate(net, wd.at[2 * h : 2 * h + 2, other], dn_mate.at[2 * h : 2 * h + 2]) for h in range(2)]
 
     def add_dn(block, slot):
         wd[block, c] = (wd[block, c].astype(F32) + dn_zone[slot].astype(F32)).astype(BF)
 
-    gu_sum = ChainSum(net, lambda zz: wgu.at[zz, c], lambda k: gu_zone.at[k], add_gu)
+    def half_sum(cols):
+        def add(block, slot):
+            wgu[block, c, :, cols] = (wgu[block, c, :, cols].astype(F32) + gu_zone[slot, :, cols].astype(F32)).astype(BF)
+
+        return ChainSum(net, lambda zz: wgu.at[zz, c, :, cols], lambda k: gu_zone.at[k, :, cols], add)
+
+    gu_sum = [half_sum(cols) for cols in halves]
     dn_sum = ChainSum(net, lambda zz: wd.at[zz, c], lambda k: dn_zone.at[k], add_dn)
-    ats.pass_on()
-    for pair in gu_pair:
-        pair.take()
-    for k in range(4):
-        wgu[k, c] = (wgu[k, c].astype(F32) + gu_mate[k].astype(F32)).astype(BF)
-    gu_sum.stage(0)
-    for pair in dn_pair:
-        pair.take()
-    for k in range(4):
-        wd[k, c] = (wd[k, c].astype(F32) + dn_mate[k].astype(F32)).astype(BF)
+
+    def pair_gu(h):
+        gu_pair[h].take()
+        cols = halves[h]
+        for k in range(4):
+            wgu[k, c, :, cols] = (wgu[k, c, :, cols].astype(F32) + gu_mate[k, :, cols].astype(F32)).astype(BF)
+        gu_sum[h].stage(0)
+
+    turn_x[...] = mn_all[...].reshape(span, dim).T
+    for h in range(2):
+        base = hid * h
+        gates, ups, downs = pl.ds(base, quad), pl.ds(base + quad, quad), pl.ds(quad * h, quad)
+        if h == 1:
+            gu[1].step(3)
+            gu[1].give(3)
+            gu[1].take()
+        for pair in range(2):
+            lines, two = pl.ds(2 * tok * pair, 2 * tok), slice(2 * pair, 2 * pair + 2)
+            normed = mn_all[two].reshape(2 * tok, dim)
+            gate = dot_nn(normed, wgu_flat[:, gates])
+            up = dot_nn(normed, wgu_flat[:, ups])
+            g_act = dot_nt(gd_all[two].reshape(2 * tok, dim), wd_flat[downs, :])
+            sig = jax.nn.sigmoid(gate)
+            swish = gate * sig
+            act[lines, downs] = (swish * up).astype(BF)
+            gboth[lines, gates] = (g_act * up * (sig * (1.0 + gate * (1.0 - sig)))).astype(BF)
+            gboth[lines, ups] = (g_act * swish).astype(BF)
+        for n in range(3):
+            cols = pl.ds(384 * n, 384)
+            part = dot_nt(gboth[:, halves[h]], wgu_flat[cols, halves[h]]).reshape(4, tok, 384)
+            if h == 0:
+                gn_send[:, :, cols] = part.astype(BF)
+            else:
+                gn_send[:, :, cols] = (gn_send[:, :, cols].astype(F32) + part).astype(BF)
+                gn[n].start()
+        if h == 0:
+            gu[1].step(2)
+            gu[1].give(2)
+        net.finish(gu[h])
+        for span_cols in (gates, ups):
+            wgu_flat[:, span_cols] = dot_nn(turn_x[...], gboth[:, span_cols]).astype(BF)
+        gu_pair[h].start()
+        for n in range(3):
+            cols = pl.ds(384 * n, 384)
+            part = dot_nn(act[:, downs], wd_flat[downs, cols]).reshape(4, tok, 384)
+            if h == 0:
+                br_send[:, :, cols] = part.astype(BF)
+            else:
+                br_send[:, :, cols] = (br_send[:, :, cols].astype(F32) + part).astype(BF)
+        turn_a[downs, :] = act[:, downs].T
+        if h == 0:
+            net.finish(dn)
+        for n in range(3):
+            cols = pl.ds(384 * n, 384)
+            wd_flat[downs, cols] = dot_nn(turn_a[downs, :], gd_all[:, :, cols].reshape(span, 384)).astype(BF)
+        dn_pair[h].start()
+        if h == 0:
+            pair_gu(0)
+    pair_gu(1)
+    for h in range(2):
+        dn_pair[h].take()
+        for k in (2 * h, 2 * h + 1):
+            wd[k, c] = (wd[k, c].astype(F32) + dn_mate[k].astype(F32)).astype(BF)
     dn_sum.stage(0)
+    gu_sum[0].stage(1)
 
     for n in range(3):
         gn[n].take()
@@ -821,13 +909,14 @@
     cut = lambda cols: Spread(net, lambda j: cut_send.at[j, :, cols], lambda j: cut_land.at[j, :, cols])
     cut_o, cut_q, cut_l = cut(pl.ds(512, 256)), cut(pl.ds(0, 256)), cut(pl.ds(256, 256))
     cut_o.start()
+    ats.pass_on()
     cut_land[d, :, 512:768] = cut_send[d, :, 512:768]
     g_att = dot_nt(gba[:, 1024:1152], wb[3, :, :128])
     for j in range(4):
         g_att = g_att + dot_nt(gba[:, 256 * j : 256 * j + 256], wb[j, :, 128:])
     for h in range(H):
         do_heads[h // groups, tok * (h % groups) : tok * (h % groups) + tok, :] = g_att[:, HD * h : HD * h + HD].astype(BF)
-    gu_sum.stage(1)
+    net.finish(b, gs)
 
     kv_pair = [ToMate(net, dkv.at[n, :, other], kv_mate.at[n]) for n in range(2)]
     kv_sum = [ToOwners(net, lambda zz, n=n: dkv.at[n, zz, c], lambda k, n=n: kv_zone.at[n, k], True) for n in range(2)]
@@ -863,23 +952,39 @@
         pair.start()
         return pair
 
-    def grads_sum(p, pair):
+    def grads_pair(p, pair):
         pair.take()
         for k in range(4):
             m_att[p, k, c, :, quarter] = (m_att[p, k, c, :, quarter].astype(F32) + ma_mate[p, k].astype(F32)).astype(BF)
+
+    def grads_chain(p, pair):
+        def add(block, slot):
+            m_att[p, block, c, :, quarter] = (
+                m_att[p, block, c, :, quarter].astype(F32) + ma_zone[p, slot].astype(F32)
+            ).astype(BF)
+
+        grads_pair(p, pair)
+        out = ChainSum(net, lambda zz: m_att.at[p, zz, c, :, quarter], lambda k: ma_zone.at[p, k], add)
+        out.stage(0)
+        return out
+
+    def grads_straight(p, pair):
+        grads_pair(p, pair)
         out = ToOwners(net, lambda zz: m_att.at[p, zz, c, :, quarter], lambda k: ma_zone.at[p, k])
         out.start()
         return out
 
     def grads_back(p, out):
         cols = pl.ds(256 * p, 256)
-        out.take()
-        total = m_att[p, z, c, :, quarter].astype(F32)
-        for k in range(3):
-            total = total + ma_zone[p, k].astype(F32)
-        wide[:, : total.shape[1]] = total
-        for j in range(4):
-            att_land[j, :rows, cols] = wide[pl.ds(j * rows, rows), : total.shape[1]].astype(BF)
+        if isinstance(out, ChainSum):
+            out.own()
+            total = m_att[p, z, c, :, quarter].astype(F32)
+        else:
+            out.take()
+            total = m_att[p, z, c, :, quarter].astype(F32)
+            for k in range(3):
+                total = total + ma_zone[p, k].astype(F32)
+        unsettle(total, wide, att_land, rows, cols)
         spread = Spread(net, lambda j: att_land.at[j, :, cols], lambda j: back_att.at[j, :, cols])
         spread.start()
         back_att[d, :, cols] = att_land[d, :, cols]
@@ -889,9 +994,7 @@
     quarter = pl.ds(0, 256)
     lax.fori_loop(0, 3, pull, 0)
     kv_pair[0].start()
-    ats.take()
-    cut_o.take()
-    turn_x[...] = att_all[...].reshape(span, dim).T
+    gu_sum[0].stage(2)
     pair_sum(0)
     lax.fori_loop(3, 6, pull, 0)
     kv_pair[1].start()
@@ -899,15 +1002,22 @@
         j, col = (t // 2, (t % 2) * 128) if t < 8 else (2, 384)
         cut_send[j, :, col : col + 128] = turned(joined(o_heads, t, tok), cosine, -sine).astype(BF)
     cut_q.start()
+    br[0].start()
     cut_land[d, :, q_cols] = cut_send[d, :, q_cols]
     pair_sum(1)
+    gu_sum[1].stage(1)
+    ats.take()
+    cut_o.take()
+    turn_x[...] = att_all[...].reshape(span, dim).T
     pair_o = grads(2, [dot_nn(turn_x[...], cut_land[:, :, o_cols].reshape(span, 256))])
     turn_n[...] = xn_all[...].reshape(span, dim).T
-    br[0].take()
-    block_out[0] = (middle[...] + scale_mlp * plane_sum(net, br_send, br_land)).astype(BF)
     cut_q.take()
     pair_q = grads(0, [dot_nn(turn_n[...], cut_land[:, :, q_cols].reshape(span, 256))])
     dn_sum.stage(1)
+    gu_sum[1].stage(2)
+    br[0].take()
+    block_out[0] = (middle[...] + scale_mlp * plane_sum(net, br_send, br_land)).astype(BF)
+    sum_o = grads_chain(2, pair_o)
 
     for n in range(2):
         kv_sum[n].take()
@@ -925,8 +1035,9 @@
         cut_send[j, :, col : col + 128] = tile.astype(BF)
     cut_l.start()
     cut_land[d, :, l_cols] = cut_send[d, :, l_cols]
-    gu_sum.stage(2)
-    sum_o = grads_sum(2, pair_o)
+    sum_q = grads_chain(0, pair_q)
+    sum_o.stage(1)
+    dn_sum.stage(2)
     cut_l.take()
     last = cut_land[:, :, 384:512].reshape(span, 128)
     cuts = cut_land[:, :, :512].reshape(span, 512)
@@ -938,24 +1049,24 @@
         gx[n].start()
     second = jnp.where(d == 3, dot_nn(turn_x[...], last), dot_nn(turn_n[...], last))
     pair_l = grads(1, [dot_nn(turn_n[...], cut_land[:, :, 256:384].reshape(span, 128)), second])
-    sum_l = grads_sum(1, pair_l)
-    sum_q = grads_sum(0, pair_q)
-    dn_sum.stage(2)
-    back_o = grads_back(2, sum_o)
-    gu_sum.own()
-    wide[...] = wgu[z, c].astype(F32)
-    for j in range(4):
-        gu_land[j, :rows, :] = wide[pl.ds(j * rows, rows), :].astype(BF)
+    sum_l = grads_straight(1, pair_l)
+    sum_q.stage(1)
+    sum_o.stage(2)
+    for k in range(2):
+        gu_sum[k].own()
+        unsettle(wgu[z, c, :, halves[k]].astype(F32), wide, gu_land, rows, halves[k])
     back_g = Spread(net, lambda j: gu_land.at[j], lambda j: back_gu.at[j])
     back_g.start()
     back_gu[d] = gu_land[d]
+    sum_q.stage(2)
+    dn_sum.own()
+    back_down[...] = wd[z, c]
+    back_o = grads_back(2, sum_o)
     back_l = grads_back(1, sum_l)
     back_q = grads_back(0, sum_q)
     for n in range(3):
         gx[n].take()
     input_grad[0] = gmid[...] + norm_pull(plane_sum(net, gx_send, gx_land), x_in[0].astype(F32))
-    dn_sum.own()
-    back_down[...] = wd[z, c]
     for spread in (back_o, back_q, back_g, back_l):
         spread.take()
     net.finish()
@@ -980,9 +1091,7 @@
     scratch = [
         att_pack,
         gu_pack,
-        att_pack,
-        gu_pack,
-        ((blk, 2 * hid), F32),
+        ((blk, hid), F32),
         wide_cut,
         ((4, 2, tok, 2 * KV * HD), BF),
         ((KV, 3 * tok, HD), F32),
@@ -1021,7 +1130,7 @@
         ((2, 384, tok), F32),
         ((4, tok, 768), BF),
         ((3, 4, blk, 256), BF),
-        ((3, 3, blk, 256), BF),
+        ((3, 5, blk, 256), BF),
         plane,
     ]
     return pl.pallas_call(
@@ -1061,9 +1170,9 @@
     gain = column(gain_two[...])
     total = jnp.zeros((rows, 4 * ffr), F32)
     for i, (w, g) in enumerate(((gate_w, g_gate), (up_w, g_up))):
-        parts = [back_gu[j, :rows, hid * i : hid * i + hid].astype(F32) for j in range(4)]
         for k in range(8):
-            m = jnp.concatenate([part[:, ffr * k : ffr * k + ffr] for part in parts], axis=1)
+            at = hid * (k // 4) + 4 * ffr * i + ffr * (k % 4)
+            m = jnp.concatenate([back_gu[j, :rows, at : at + ffr].astype(F32) for j in range(4)], axis=1)
             cols = slice(4 * ffr * k, 4 * ffr * k + 4 * ffr)
             total = total + w[:, cols].astype(F32) * m
             g[:, cols] = m * gain

time: 205 us -> 188 us (0.917)
  Pallas kernels: 202 us -> 186 us
    pallas_call x1, Pallas kernels: 199 us -> 182 us  [layer(): pl.pallas_call(layer_kernel, out_shape=[jax.ShapeDtypeStruct(*o) for o in...]
where the time goes in v6:
time: 188 us
  Pallas kernels  186 us (99%)
    pallas_call x1, Pallas kernels, layer(): pl.pallas_call(layer_kernel, out_shape=[jax.ShapeDtypeStruct(*o) for o in...  182 us

profile of v6, /device:TPU:0, one launch (start us, length us, event | category | flops | bytes accessed | tf_op | source)
XLA Modules:
  0.0 187.8 jit_solution(10002230384759222252)
XLA Ops:
  0.7 0.0 copy-start
  0.7 0.6 broadcast_in_dim_tile.3.freq
  1.3 0.1 copy-done
  1.3 0.7 copy.26.keep_mask
  2.0 182.1 %k_layer.1 = (bf16[1,128,1152]{2,1,0:T(8,128)(2,1)}, f32[1,128,1152]{2,1,0:T(8,128)}, bf16[4,48,1536]{2,1,0:T(8,128)(2,1)}, bf16[4,48,768]{2,1,0:T(8,128)(2,1)}, bf16[96,1152]{1,0:T(8,128)(2,1)}) custom-call(bf16[1,128,1152]{2,1,0:T(8,128)(2,1)} %x_in.1, bf16[1,128,1152]{2,1,0:T(8,128)(2,1)} %cot_in.1, bf16[36,1152]{1,0:T(8,128)(2,1)} %query.3, ...), custom_call_target="tpu_custom_call" | custom-call | tf_op jit(solution)/shard_map/k_layer/pallas_call | solution.py:1136
  184.1 3.7 %k_grads.1 = (bf16[1,128,1152]{2,1,0:T(8,128)(2,1)}, f32[1,128,1152]{2,1,0:T(8,128)}, f32[1,36]{1,0:T(1,128)}, f32[36,1152]{1,0:T(8,128)}, f32[36,384]{1,0:T(8,1...) custom-call(bf16[36,1152]{1,0:T(8,128)(2,1)} %query.3, ...), custom_call_target="tpu_custom_call" | custom-call | tf_op jit(solution)/shard_map/k_grads/pallas_call | solution.py:1187
  (2 shorter events, 0.0 us)
Async XLA Ops:
  0.7 0.7 copy-start

commit v7 on v6

--- a/solution.py
+++ b/solution.py
@@ -206,6 +206,7 @@
 
 MESH = pl.DeviceIdType.MESH
 LIMIT = 60 * 2**20
+SENDS, RECVS = 120, 202
 BF, F32 = jnp.bfloat16, jnp.float32
 
 
@@ -223,7 +224,8 @@
 
 class Net:
     def __init__(self, sends, recvs):
-        self.sends, self.recvs, self.count, self.open, self.used = sends, recvs, 0, [], 0
+        self.sends, self.recvs, self.open, self.used = sends, recvs, [], 0
+        self.free = list(range(sends.shape[0]))
         self.s, self.d = lax.axis_index("seq"), lax.axis_index("dp")
         self.z, self.c = lax.div(self.s, 2), lax.rem(self.s, 2)
         y, x = lax.div(self.d, 2), lax.rem(self.d, 2)
@@ -262,13 +264,13 @@
         )
 
     def push(self, owner, src, dst, recv, peer, when=None):
-        copy = self.copy(src, dst, self.count, recv, peer)
-        self.count += 1
+        send = self.free.pop(0)
+        copy = self.copy(src, dst, send, recv, peer)
         if when is None:
             copy.start()
         else:
             pl.when(when)(copy.start)
-        self.open.append((copy, when, owner))
+        self.open.append((copy, when, owner, send))
 
     def arrive(self, dst, recv, when=None):
         copy = self.copy(dst, dst, 0, recv, self.mate)
@@ -279,13 +281,16 @@
 
     def finish(self, *owners):
         kept = []
-        for copy, when, owner in self.open:
+        for entry in self.open:
+            copy, when, owner, send = entry
             if owners and owner not in owners:
-                kept.append((copy, when, owner))
-            elif when is None:
+                kept.append(entry)
+                continue
+            if when is None:
                 copy.wait_send()
             else:
                 pl.when(when)(copy.wait_send)
+            self.free.append(send)
         self.open = kept
 
     def order(self, step):
@@ -319,9 +324,17 @@
     def __init__(self, net, block):
         super().__init__(net, block, 8)
 
-    def start(self):
-        super().start()
-        self.give(0)
+    def start(self, ends=None):
+        net = self.net
+        own = self.block(net.z, net.c)
+        up, down, any_z = net.z < 3, net.z > 0, None
+        if ends is not None:
+            any_z = (net.z == 0) | (net.z == 3)
+            any_z = any_z if ends else jnp.logical_not(any_z)
+            up, down = up & any_z, down & any_z
+        net.push(self, own, own, self.base + net.z, net.at(net.z + 1, net.c), up)
+        net.push(self, own, own, self.base + net.z, net.at(net.z - 1, net.c), down)
+        net.push(self, own, own, self.base + 4 + net.z, net.mate, any_z)
 
     def onward(self, b):
         to = jnp.where(b < self.net.z, self.net.z + 1, self.net.z - 1)
@@ -483,11 +496,48 @@
             net.arrive(self.land(k - 1), self.base + k - 1, (net.z + k <= 3) if self.down else None)
 
 
+class DownSum:
+    def __init__(self, net, part, land, add):
+        self.net, self.part, self.land, self.add, self.base = net, part, land, add, net.room(3)
+
+    def send(self, b, when):
+        net = self.net
+        net.push(self, self.part(b), self.land(b), self.base + b, net.at(net.z - 1, net.c), when)
+
+    def start(self):
+        for b in range(3):
+            self.send(b, self.net.z == 3)
+
+    def relay(self, b):
+        net = self.net
+        on = (net.z > b) & (net.z < 3)
+
+        @pl.when(on)
+        def _():
+            net.arrive(self.land(b), self.base + b)
+            self.add(b)
+
+        self.send(b, on)
+
+    def own(self):
+        net = self.net
+        for b in range(3):
+
+            @pl.when(net.z == b)
+            def _(b=b):
+                net.arrive(self.land(b), self.base + b)
+                self.add(b)
+
+
 class ChainSum:
     def __init__(self, net, part, land, add):
         self.net, self.part, self.land, self.add, self.base = net, part, land, add, net.room(6)
 
     def stage(self, k):
+        self.falling(k)
+        self.rising(k)
+
+    def falling(self, k):
         net, z = self.net, self.net.z
         i = k - 3 + z
         valid = (i >= 0) & (i < z)
@@ -499,6 +549,9 @@
             self.add(i, i)
 
         net.push(self, self.part(i), self.land(i), self.base + i, net.at(z - 1, net.c), valid)
+
+    def rising(self, k):
+        net, z = self.net, self.net.z
         j = k - z
         valid = (j >= 0) & (3 - j > z)
         j = jnp.clip(j, 0, 3)
@@ -584,7 +637,7 @@
 
 
 def layer_kernel(
-    x_in, cot_in, query, key_w, value, output, gate_w, up_w, down, gain_one, gain_two, freq,
+    x_in, cot_in, query, key_w, value, output, gate_w, up_w, down, gain_one, gain_two,
     doc_starts, keep_mask, keep_rate, seq_order,
     block_out, input_grad, back_gu, back_att, back_down,
     att_land, gu_land, wide, qkv_land, kv_all, o_heads, bias, wa, wb, wgu, wd,
@@ -659,13 +712,14 @@
     gu_land[d] = gu_send[d, :padded, :]
     sample = seq_order[d]
     scale_attn, scale_mlp = [
-        jnp.full((1, 1), keep_mask[sample, i].astype(F32), F32) / jnp.full((1, 1), keep_rate[i], F32) for i in range(2)
+        jnp.full((1, 1), keep_mask[2 * sample + i].astype(F32), F32) / jnp.full((1, 1), keep_rate[i], F32) for i in range(2)
     ]
     gd_all[d] = (cot_in[0].astype(F32) * scale_mlp).astype(BF)
     wd[z, c] = down[...]
     position = s * tok + lax.broadcasted_iota(jnp.int32, (tok, 1), 0)
-    angle = position.astype(F32) * freq[...]
-    lane = lax.broadcasted_iota(jnp.int32, angle.shape, 1)
+    lane = lax.broadcasted_iota(jnp.int32, (tok, 128), 1)
+    power = lax.rem(lane, HD // 2).astype(F32) * (-2.0 * math.log(ROPE_BASE) / HD)
+    angle = position.astype(F32) * jnp.exp(power)
     cosine, sine = jnp.cos(angle), jnp.where(lax.rem(lane, HD) < HD // 2, -jnp.sin(angle), jnp.sin(angle))
     a2a_att.take()
     own = own_rows(s, blk)
@@ -725,7 +779,8 @@
         wgu[z, c, :, hid * h : hid * h + hid] = settle(gu_land, wide, rows, slice(hid * h, hid * h + hid))
     b.step(3)
     b.spread(3)
-    gu[0].start()
+    for half in gu:
+        half.start(True)
     b.pass_on(0)
     b.pass_on(1)
     a2a_qkv[1].take()
@@ -744,6 +799,7 @@
 
     kv.step(1)
     kv.step(2)
+    gu[0].start(False)
     b.pass_on(2)
     b.pass_on(3)
     b.corner(0)
@@ -766,6 +822,7 @@
         o_heads[k, mine, :] = dot_nn(p, v_heads[k])
         return carry
 
+    net.finish(xs, *a, a2a_gu)
     lax.fori_loop(0, 6, head, 0)
     dn.step(2)
     gu[0].step(1)
@@ -774,6 +831,7 @@
     lax.fori_loop(6, 12, head, 0)
     dn.step(3)
     gu[0].step(2)
+    gu[1].step(1)
     lax.fori_loop(12, 18, head, 0)
     b.corner(3)
     b.take()
@@ -786,22 +844,22 @@
     mn_all[d] = (mid * norm_scale(mid)).astype(BF)
     ms.start()
     gu[0].step(3)
-    gu[1].start()
+    gu[1].start(False)
     gs.take()
     dn.give(1)
     gu[0].give(1)
     dn.give(2)
     ms.pass_on()
-    gu[1].step(1)
+    gu[1].step(2)
     gu[0].give(2)
     dn.give(3)
     gu[0].give(3)
-    gu[1].give(1)
     ms.take()
+    gu[1].step(3)
     dn.take()
     gu[0].take()
     ats.start()
-    net.finish(a2a_gu, *a2a_qkv)
+    net.finish(b, kv, gs, *a2a_qkv)
 
     def by_cols(send, land, width):
         return [
@@ -839,40 +897,7 @@
             wgu[k, c, :, cols] = (wgu[k, c, :, cols].astype(F32) + gu_mate[k, :, cols].astype(F32)).astype(BF)
         gu_sum[h].stage(0)
 
-    turn_x[...] = mn_all[...].reshape(span, dim).T
-    for h in range(2):
-        base = hid * h
-        gates, ups, downs = pl.ds(base, quad), pl.ds(base + quad, quad), pl.ds(quad * h, quad)
-        if h == 1:
-            gu[1].step(3)
-            gu[1].give(3)
-            gu[1].take()
-        for pair in range(2):
-            lines, two = pl.ds(2 * tok * pair, 2 * tok), slice(2 * pair, 2 * pair + 2)
-            normed = mn_all[two].reshape(2 * tok, dim)
-            gate = dot_nn(normed, wgu_flat[:, gates])
-            up = dot_nn(normed, wgu_flat[:, ups])
-            g_act = dot_nt(gd_all[two].reshape(2 * tok, dim), wd_flat[downs, :])
-            sig = jax.nn.sigmoid(gate)
-            swish = gate * sig
-            act[lines, downs] = (swish * up).astype(BF)
-            gboth[lines, gates] = (g_act * up * (sig * (1.0 + gate * (1.0 - sig)))).astype(BF)
-            gboth[lines, ups] = (g_act * swish).astype(BF)
-        for n in range(3):
-            cols = pl.ds(384 * n, 384)
-            part = dot_nt(gboth[:, halves[h]], wgu_flat[cols, halves[h]]).reshape(4, tok, 384)
-            if h == 0:
-                gn_send[:, :, cols] = part.astype(BF)
-            else:
-                gn_send[:, :, cols] = (gn_send[:, :, cols].astype(F32) + part).astype(BF)
-                gn[n].start()
-        if h == 0:
-            gu[1].step(2)
-            gu[1].give(2)
-        net.finish(gu[h])
-        for span_cols in (gates, ups):
-            wgu_flat[:, span_cols] = dot_nn(turn_x[...], gboth[:, span_cols]).astype(BF)
-        gu_pair[h].start()
+    def branch_rows(h, downs):
         for n in range(3):
             cols = pl.ds(384 * n, 384)
             part = dot_nn(act[:, downs], wd_flat[downs, cols]).reshape(4, tok, 384)
@@ -887,14 +912,54 @@
             cols = pl.ds(384 * n, 384)
             wd_flat[downs, cols] = dot_nn(turn_a[downs, :], gd_all[:, :, cols].reshape(span, 384)).astype(BF)
         dn_pair[h].start()
-        if h == 0:
-            pair_gu(0)
-    pair_gu(1)
-    for h in range(2):
+
+    def pair_dn(h):
         dn_pair[h].take()
         for k in (2 * h, 2 * h + 1):
             wd[k, c] = (wd[k, c].astype(F32) + dn_mate[k].astype(F32)).astype(BF)
-    dn_sum.stage(0)
+
+    turn_x[...] = mn_all[...].reshape(span, dim).T
+    for h in range(2):
+        base = hid * h
+        gates, ups, downs = pl.ds(base, quad), pl.ds(base + quad, quad), pl.ds(quad * h, quad)
+        if h == 1:
+            for k in (1, 2, 3):
+                gu[1].give(k)
+            gu[1].take()
+            pair_gu(0)
+        for pair in range(2):
+            lines, two = pl.ds(2 * tok * pair, 2 * tok), slice(2 * pair, 2 * pair + 2)
+            normed = mn_all[two].reshape(2 * tok, dim)
+            gate = dot_nn(normed, wgu_flat[:, gates])
+            up = dot_nn(normed, wgu_flat[:, ups])
+            g_act = dot_nt(gd_all[two].reshape(2 * tok, dim), wd_flat[downs, :])
+            sig = jax.nn.sigmoid(gate)
+            swish = gate * sig
+            act[lines, downs] = (swish * up).astype(BF)
+            gboth[lines, gates] = (g_act * up * (sig * (1.0 + gate * (1.0 - sig)))).astype(BF)
+            gboth[lines, ups] = (g_act * swish).astype(BF)
+        if h == 0:
+            branch_rows(h, downs)
+        for n in range(3):
+            cols = pl.ds(384 * n, 384)
+            part = dot_nt(gboth[:, halves[h]], wgu_flat[cols, halves[h]]).reshape(4, tok, 384)
+            if h == 0:
+                gn_send[:, :, cols] = part.astype(BF)
+            else:
+                gn_send[:, :, cols] = (gn_send[:, :, cols].astype(F32) + part).astype(BF)
+                gn[n].start()
+        if h == 1:
+            branch_rows(h, downs)
+        net.finish(gu[h])
+        for span_cols in (gates, ups):
+            wgu_flat[:, span_cols] = dot_nn(turn_x[...], gboth[:, span_cols]).astype(BF)
+        gu_pair[h].start()
+        pair_dn(h)
+        if h == 0:
+            dn_sum.falling(0)
+    dn_sum.rising(0)
+    dn_sum.falling(1)
+    pair_gu(1)
     gu_sum[0].stage(1)
 
     for n in range(3):
@@ -916,10 +981,19 @@
         g_att = g_att + dot_nt(gba[:, 256 * j : 256 * j + 256], wb[j, :, 128:])
     for h in range(H):
         do_heads[h // groups, tok * (h % groups) : tok * (h % groups) + tok, :] = g_att[:, HD * h : HD * h + HD].astype(BF)
-    net.finish(b, gs)
+
+    dn_sum.falling(2)
+    dn_sum.rising(1)
 
     kv_pair = [ToMate(net, dkv.at[n, :, other], kv_mate.at[n]) for n in range(2)]
-    kv_sum = [ToOwners(net, lambda zz, n=n: dkv.at[n, zz, c], lambda k, n=n: kv_zone.at[n, k], True) for n in range(2)]
+
+    def kv_total(n):
+        def add(block):
+            dkv[n, block, c] = (dkv[n, block, c].astype(F32) + kv_zone[n, block].astype(F32)).astype(BF)
+
+        return DownSum(net, lambda zz: dkv.at[n, zz, c], lambda k: kv_zone.at[n, k], add)
+
+    kv_sum = [kv_total(n) for n in range(2)]
 
     def pull(k, carry):
         for g in range(groups):
@@ -994,9 +1068,9 @@
     quarter = pl.ds(0, 256)
     lax.fori_loop(0, 3, pull, 0)
     kv_pair[0].start()
-    gu_sum[0].stage(2)
+    lax.fori_loop(3, 4, pull, 0)
     pair_sum(0)
-    lax.fori_loop(3, 6, pull, 0)
+    lax.fori_loop(4, 6, pull, 0)
     kv_pair[1].start()
     for t in range(9):
         j, col = (t // 2, (t % 2) * 128) if t < 8 else (2, 384)
@@ -1005,29 +1079,25 @@
     br[0].start()
     cut_land[d, :, q_cols] = cut_send[d, :, q_cols]
     pair_sum(1)
-    gu_sum[1].stage(1)
     ats.take()
     cut_o.take()
     turn_x[...] = att_all[...].reshape(span, dim).T
     pair_o = grads(2, [dot_nn(turn_x[...], cut_land[:, :, o_cols].reshape(span, 256))])
     turn_n[...] = xn_all[...].reshape(span, dim).T
+    for n in range(2):
+        kv_sum[n].relay(0)
+        kv_sum[n].relay(1)
+    gu_sum[0].stage(2)
+    gu_sum[1].stage(1)
     cut_q.take()
     pair_q = grads(0, [dot_nn(turn_n[...], cut_land[:, :, q_cols].reshape(span, 256))])
-    dn_sum.stage(1)
+    sum_o = grads_chain(2, pair_o)
     gu_sum[1].stage(2)
-    br[0].take()
-    block_out[0] = (middle[...] + scale_mlp * plane_sum(net, br_send, br_land)).astype(BF)
-    sum_o = grads_chain(2, pair_o)
+    dn_sum.rising(2)
 
     for n in range(2):
-        kv_sum[n].take()
+        kv_sum[n].own()
         kv_tot[n] = dkv[n, z, c].astype(F32)
-        for k in (1, 2, 3):
-
-            @pl.when(z + k <= 3)
-            def _(n=n, k=k):
-                kv_tot[n] += kv_zone[n, k - 1].astype(F32)
-
     keys = jnp.concatenate([kv_tot[0, :192, :], kv_tot[1, :192, :]], axis=0).T
     vals = jnp.concatenate([kv_tot[0, 192:, :], kv_tot[1, 192:, :]], axis=0).T
     late = [turned(keys[:, 128 * i : 128 * i + 128], cosine, -sine) for i in range(3)] + [vals[:, 128 * i : 128 * i + 128] for i in range(3)]
@@ -1037,7 +1107,6 @@
     cut_land[d, :, l_cols] = cut_send[d, :, l_cols]
     sum_q = grads_chain(0, pair_q)
     sum_o.stage(1)
-    dn_sum.stage(2)
     cut_l.take()
     last = cut_land[:, :, 384:512].reshape(span, 128)
     cuts = cut_land[:, :, :512].reshape(span, 512)
@@ -1050,6 +1119,8 @@
     second = jnp.where(d == 3, dot_nn(turn_x[...], last), dot_nn(turn_n[...], last))
     pair_l = grads(1, [dot_nn(turn_n[...], cut_land[:, :, 256:384].reshape(span, 128)), second])
     sum_l = grads_straight(1, pair_l)
+    br[0].take()
+    block_out[0] = (middle[...] + scale_mlp * plane_sum(net, br_send, br_land)).astype(BF)
     sum_q.stage(1)
     sum_o.stage(2)
     for k in range(2):
@@ -1059,11 +1130,11 @@
     back_g.start()
     back_gu[d] = gu_land[d]
     sum_q.stage(2)
-    dn_sum.own()
-    back_down[...] = wd[z, c]
     back_o = grads_back(2, sum_o)
     back_l = grads_back(1, sum_l)
     back_q = grads_back(0, sum_q)
+    dn_sum.own()
+    back_down[...] = wd[z, c]
     for n in range(3):
         gx[n].take()
     input_grad[0] = gmid[...] + norm_pull(plane_sum(net, gx_send, gx_land), x_in[0].astype(F32))
@@ -1072,7 +1143,7 @@
     net.finish()
 
 
-def layer(x, cot, weights, down, gains, freq, doc_starts, keep_mask, keep_rate, seq_order):
+def layer(x, cot, weights, down, gains, doc_starts, keep_mask, keep_rate, seq_order):
     tok, dim = x.shape[1:]
     ns = 8
     length = tok * ns
@@ -1136,12 +1207,12 @@
     return pl.pallas_call(
         layer_kernel,
         out_shape=[jax.ShapeDtypeStruct(*o) for o in outs],
-        in_specs=[vm] * 12 + [sm] * 4,
+        in_specs=[vm] * 11 + [sm] * 4,
         out_specs=[vm] * len(outs),
-        scratch_shapes=[pltpu.VMEM(*t) for t in scratch] + [pltpu.SemaphoreType.DMA((320,)), pltpu.SemaphoreType.DMA((256,))],
+        scratch_shapes=[pltpu.VMEM(*t) for t in scratch] + [pltpu.SemaphoreType.DMA((SENDS,)), pltpu.SemaphoreType.DMA((RECVS,))],
         compiler_params=pltpu.CompilerParams(collective_id=0, has_side_effects=True, vmem_limit_bytes=LIMIT),
         name="k_layer",
-    )(x, cot, *weights, down, *gains, freq, doc_starts, keep_mask, keep_rate, seq_order)
+    )(x, cot, *weights, down, *gains, doc_starts, keep_mask, keep_rate, seq_order)
 
 
 def grads_kernel(
@@ -1211,12 +1282,10 @@
     seq_order,
 ):
     rows = query_weight.shape[0]
-    freq = ROPE_BASE ** (-2.0 * jnp.arange(HD // 2, dtype=F32) / HD)
-    freq = jnp.tile(freq, 128 // freq.shape[0])[None]
     gains = (attn_norm.reshape(1, rows), mlp_norm.reshape(1, rows))
     weights = (query_weight, key_weight, value_weight, output_weight, gate_weight, up_weight)
     results = layer(
-        hidden_in, cotangent, weights, down_weight, gains, freq, doc_starts, keep_mask, keep_rate, seq_order
+        hidden_in, cotangent, weights, down_weight, gains, doc_starts, keep_mask.reshape(-1), keep_rate, seq_order
     )
     outs = list(gradients(*weights, gains, results))
     outs[2], outs[7] = outs[2].reshape(rows), outs[7].reshape(rows)

time: 188 us -> 178 us (0.947); the launches traced: 188 us -> 175 us
  Pallas kernels: 186 us -> 173 us
    pallas_call x1, Pallas kernels: 182 us -> 169 us  [layer(): pl.pallas_call(layer_kernel, out_shape=[jax.ShapeDtypeStruct(*o) for o in...]
where the time goes in v7:
time: 178 us; the launch traced here: 175 us
  Pallas kernels  173 us (97%)
    pallas_call x1, Pallas kernels, layer(): pl.pallas_call(layer_kernel, out_shape=[jax.ShapeDtypeStruct(*o) for o in...  169 us
    pallas_call x1, Pallas kernels, gradients(): pl.pallas_call(grads_kernel, out_shape=[jax.ShapeDtypeStruct(block.shape,...  3.66 us

profile of v7, /device:TPU:0, one launch (start us, length us, event | category | flops | bytes accessed | tf_op | source)
XLA Modules:
  0.0 174.8 jit_solution(9921722556229535394)
XLA Ops:
  0.6 0.0 copy-start
  0.7 0.7 copy-done
  1.3 0.1 copy.27
  1.4 0.6 reshape.39.keep_mask
  2.0 169.1 %k_layer.1 = (bf16[1,128,1152]{2,1,0:T(8,128)(2,1)}, f32[1,128,1152]{2,1,0:T(8,128)}, bf16[4,48,1536]{2,1,0:T(8,128)(2,1)}, bf16[4,48,768]{2,1,0:T(8,128)(2,1)}, bf16[96,1152]{1,0:T(8,128)(2,1)}) custom-call(bf16[1,128,1152]{2,1,0:T(8,128)(2,1)} %x_in.1, bf16[1,128,1152]{2,1,0:T(8,128)(2,1)} %cot_in.1, bf16[36,1152]{1,0:T(8,128)(2,1)} %query.3, ...), custom_call_target="tpu_custom_call" | custom-call | tf_op jit(solution)/shard_map/k_layer/pallas_call | solution.py:1207
  171.1 3.7 %k_grads.1 = (bf16[1,128,1152]{2,1,0:T(8,128)(2,1)}, f32[1,128,1152]{2,1,0:T(8,128)}, f32[1,36]{1,0:T(1,128)}, f32[36,1152]{1,0:T(8,128)}, f32[36,384]{1,0:T(8,1...) custom-call(bf16[36,1152]{1,0:T(8,128)(2,1)} %query.3, ...), custom_call_target="tpu_custom_call" | custom-call | tf_op jit(solution)/shard_map/k_grads/pallas_call | solution.py:1258
Async XLA Ops:
  0.6 0.7 copy-start

commit v8 on v7

--- a/solution.py
+++ b/solution.py
@@ -537,10 +537,12 @@
         self.falling(k)
         self.rising(k)
 
-    def falling(self, k):
+    def falling(self, k, top=None):
         net, z = self.net, self.net.z
         i = k - 3 + z
         valid = (i >= 0) & (i < z)
+        if top is not None:
+            valid = valid & ((z == 3) if top else (z < 3))
         i = jnp.clip(i, 0, 3)
 
         @pl.when(valid & (z < 3))
@@ -550,10 +552,20 @@
 
         net.push(self, self.part(i), self.land(i), self.base + i, net.at(z - 1, net.c), valid)
 
-    def rising(self, k):
+    def last(self):
+        self.falling(2, True)
+        self.rising(2, True)
+
+    def between(self, k):
+        self.falling(k, False)
+        self.rising(k, False)
+
+    def rising(self, k, end=None):
         net, z = self.net, self.net.z
         j = k - z
         valid = (j >= 0) & (3 - j > z)
+        if end is not None:
+            valid = valid & ((z == 0) if end else (z > 0))
         j = jnp.clip(j, 0, 3)
 
         @pl.when(valid & (z > 0))
@@ -781,6 +793,7 @@
     b.spread(3)
     for half in gu:
         half.start(True)
+    kv.step(1)
     b.pass_on(0)
     b.pass_on(1)
     a2a_qkv[1].take()
@@ -797,7 +810,6 @@
     key = lax.broadcasted_iota(jnp.int32, bias.shape, 1)
     bias[...] = jnp.where((key <= position) & (key >= first), 0.0, MASKED)
 
-    kv.step(1)
     kv.step(2)
     gu[0].start(False)
     b.pass_on(2)
@@ -812,27 +824,27 @@
             k_heads[k, pl.ds(tok * j, tok), :] = kv_all[j // 2, j % 2, :, HD * k : HD * k + HD]
             v_heads[k, pl.ds(tok * j, tok), :] = kv_all[j // 2, j % 2, :, HD * (KV + k) : HD * (KV + k) + HD]
 
-    def head(h, carry):
-        k = lax.div(h, groups)
-        mine = pl.ds(pl.multiple_of(lax.rem(h, groups) * tok, tok), tok)
-        score = dot_nt(q_heads[k, mine, :], k_heads[k]) + bias[...]
-        expo = jnp.exp(score - jnp.max(score, axis=1, keepdims=True))
-        p = (expo * (1.0 / jnp.sum(expo, axis=1, keepdims=True))).astype(BF)
-        probs[k, mine, :] = p
-        o_heads[k, mine, :] = dot_nn(p, v_heads[k])
+    def attend(k, carry):
+        for g in range(groups):
+            mine = pl.ds(tok * g, tok)
+            score = dot_nt(q_heads[k, mine, :], k_heads[k]) + bias[...]
+            expo = jnp.exp(score - jnp.max(score, axis=1, keepdims=True))
+            p = (expo * (1.0 / jnp.sum(expo, axis=1, keepdims=True))).astype(BF)
+            probs[k, mine, :] = p
+            o_heads[k, mine, :] = dot_nn(p, v_heads[k])
         return carry
 
     net.finish(xs, *a, a2a_gu)
-    lax.fori_loop(0, 6, head, 0)
+    lax.fori_loop(0, 2, attend, 0)
     dn.step(2)
     gu[0].step(1)
     gs.pass_on()
     b.corner(2)
-    lax.fori_loop(6, 12, head, 0)
+    lax.fori_loop(2, 4, attend, 0)
     dn.step(3)
     gu[0].step(2)
     gu[1].step(1)
-    lax.fori_loop(12, 18, head, 0)
+    lax.fori_loop(4, 6, attend, 0)
     b.corner(3)
     b.take()
     for j in range(H // 2):
@@ -926,7 +938,6 @@
             for k in (1, 2, 3):
                 gu[1].give(k)
             gu[1].take()
-            pair_gu(0)
         for pair in range(2):
             lines, two = pl.ds(2 * tok * pair, 2 * tok), slice(2 * pair, 2 * pair + 2)
             normed = mn_all[two].reshape(2 * tok, dim)
@@ -948,17 +959,25 @@
             else:
                 gn_send[:, :, cols] = (gn_send[:, :, cols].astype(F32) + part).astype(BF)
                 gn[n].start()
-        if h == 1:
-            branch_rows(h, downs)
+        if h == 0:
+            pair_dn(h)
+            dn_sum.falling(0)
+            dn_sum.falling(1, True)
+
+    def grads_gu(h):
         net.finish(gu[h])
-        for span_cols in (gates, ups):
-            wgu_flat[:, span_cols] = dot_nn(turn_x[...], gboth[:, span_cols]).astype(BF)
+        for base in (hid * h, hid * h + quad):
+            cols = pl.ds(base, quad)
+            wgu_flat[:, cols] = dot_nn(turn_x[...], gboth[:, cols]).astype(BF)
         gu_pair[h].start()
-        pair_dn(h)
-        if h == 0:
-            dn_sum.falling(0)
+
+    grads_gu(0)
+    branch_rows(1, pl.ds(quad, quad))
+    pair_gu(0)
+    grads_gu(1)
+    pair_dn(1)
     dn_sum.rising(0)
-    dn_sum.falling(1)
+    dn_sum.falling(1, False)
     pair_gu(1)
     gu_sum[0].stage(1)
 
@@ -982,7 +1001,7 @@
     for h in range(H):
         do_heads[h // groups, tok * (h % groups) : tok * (h % groups) + tok, :] = g_att[:, HD * h : HD * h + HD].astype(BF)
 
-    dn_sum.falling(2)
+    dn_sum.falling(2, False)
     dn_sum.rising(1)
 
     kv_pair = [ToMate(net, dkv.at[n, :, other], kv_mate.at[n]) for n in range(2)]
@@ -1087,13 +1106,12 @@
     for n in range(2):
         kv_sum[n].relay(0)
         kv_sum[n].relay(1)
-    gu_sum[0].stage(2)
-    gu_sum[1].stage(1)
     cut_q.take()
     pair_q = grads(0, [dot_nn(turn_n[...], cut_land[:, :, q_cols].reshape(span, 256))])
+    gu_sum[1].stage(1)
     sum_o = grads_chain(2, pair_o)
-    gu_sum[1].stage(2)
-    dn_sum.rising(2)
+    sum_q = grads_chain(0, pair_q)
+    gu_sum[0].between(2)
 
     for n in range(2):
         kv_sum[n].own()
@@ -1105,9 +1123,13 @@
         cut_send[j, :, col : col + 128] = tile.astype(BF)
     cut_l.start()
     cut_land[d, :, l_cols] = cut_send[d, :, l_cols]
-    sum_q = grads_chain(0, pair_q)
     sum_o.stage(1)
+    sum_q.stage(1)
+    gu_sum[1].between(2)
+    gu_sum[0].last()
     cut_l.take()
+    gu_sum[1].last()
+    dn_sum.rising(2, False)
     last = cut_land[:, :, 384:512].reshape(span, 128)
     cuts = cut_land[:, :, :512].reshape(span, 512)
     lane = lax.broadcasted_iota(jnp.int32, cuts.shape, 1)
@@ -1121,15 +1143,15 @@
     sum_l = grads_straight(1, pair_l)
     br[0].take()
     block_out[0] = (middle[...] + scale_mlp * plane_sum(net, br_send, br_land)).astype(BF)
-    sum_q.stage(1)
+    dn_sum.last()
     sum_o.stage(2)
+    sum_q.stage(2)
     for k in range(2):
         gu_sum[k].own()
         unsettle(wgu[z, c, :, halves[k]].astype(F32), wide, gu_land, rows, halves[k])
     back_g = Spread(net, lambda j: gu_land.at[j], lambda j: back_gu.at[j])
     back_g.start()
     back_gu[d] = gu_land[d]
-    sum_q.stage(2)
     back_o = grads_back(2, sum_o)
     back_l = grads_back(1, sum_l)
     back_q = grads_back(0, sum_q)

time: 178 us -> 172 us (0.966)
  Pallas kernels: 173 us -> 168 us
    pallas_call x1, Pallas kernels: 169 us -> 165 us  [layer(): pl.pallas_call(layer_kernel, out_shape=[jax.ShapeDtypeStruct(*o) for o in...]
where the time goes in v8:
time: 172 us; the launch traced here: 170 us
  Pallas kernels  168 us (98%)
    pallas_call x1, Pallas kernels, layer(): pl.pallas_call(layer_kernel, out_shape=[jax.ShapeDtypeStruct(*o) for o in...  165 us
    pallas_call x1, Pallas kernels, gradients(): pl.pallas_call(grads_kernel, out_shape=[jax.ShapeDtypeStruct(block.shape,...  3.66 us

profile of v8, /device:TPU:0, one launch (start us, length us, event | category | flops | bytes accessed | tf_op | source)
XLA Modules:
  0.0 170.5 jit_solution(4641310133405222072)
XLA Ops:
  0.6 0.0 copy-start
  0.7 0.7 copy-done
  1.3 0.1 copy.27
  1.4 0.6 reshape.39.keep_mask
  2.0 164.8 %k_layer.1 = (bf16[1,128,1152]{2,1,0:T(8,128)(2,1)}, f32[1,128,1152]{2,1,0:T(8,128)}, bf16[4,48,1536]{2,1,0:T(8,128)(2,1)}, bf16[4,48,768]{2,1,0:T(8,128)(2,1)}, bf16[96,1152]{1,0:T(8,128)(2,1)}) custom-call(bf16[1,128,1152]{2,1,0:T(8,128)(2,1)} %x_in.1, bf16[1,128,1152]{2,1,0:T(8,128)(2,1)} %cot_in.1, bf16[36,1152]{1,0:T(8,128)(2,1)} %query.3, ...), custom_call_target="tpu_custom_call" | custom-call | tf_op jit(solution)/shard_map/k_layer/pallas_call | solution.py:1229
  166.8 3.7 %k_grads.1 = (bf16[1,128,1152]{2,1,0:T(8,128)(2,1)}, f32[1,128,1152]{2,1,0:T(8,128)}, f32[1,36]{1,0:T(1,128)}, f32[36,1152]{1,0:T(8,128)}, f32[36,384]{1,0:T(8,1...) custom-call(bf16[36,1152]{1,0:T(8,128)(2,1)} %query.3, ...), custom_call_target="tpu_custom_call" | custom-call | tf_op jit(solution)/shard_map/k_grads/pallas_call | solution.py:1280
Async XLA Ops:
  0.6 0.7 copy-start

commit v9 on v8

--- a/solution.py
+++ b/solution.py
@@ -206,7 +206,7 @@
 
 MESH = pl.DeviceIdType.MESH
 LIMIT = 60 * 2**20
-SENDS, RECVS = 120, 202
+SENDS, RECVS = 120, 204
 BF, F32 = jnp.bfloat16, jnp.float32
 
 
@@ -362,6 +362,30 @@
             net.arrive(self.block(b, 1 - net.c), self.base + 4 + b)
 
 
+class FromLast:
+    def __init__(self, net, source, full):
+        self.net, self.source, self.full, self.base = net, source, full, net.room(2)
+
+    def start(self):
+        net = self.net
+        for kind in range(3):
+            part = self.full.at[:, net.c]
+            net.push(self, self.source.at[:, net.c, :, pl.ds(384, 128)], part, self.base, net.across(kind), net.d == 3)
+
+        @pl.when(net.d == 3)
+        def _():
+            self.full[...] = self.source[:, :, :, 384:512]
+
+    def pass_on(self):
+        net = self.net
+        part = self.full.at[:, net.c]
+        net.arrive(part, self.base, net.d < 3)
+        net.push(self, part, part, self.base + 1, net.mate, net.d < 3)
+
+    def take(self):
+        self.net.arrive(self.full.at[:, 1 - self.net.c], self.base + 1, self.net.d < 3)
+
+
 class Rising(Lines):
     def start(self):
         net = self.net
@@ -652,7 +676,7 @@
     x_in, cot_in, query, key_w, value, output, gate_w, up_w, down, gain_one, gain_two,
     doc_starts, keep_mask, keep_rate, seq_order,
     block_out, input_grad, back_gu, back_att, back_down,
-    att_land, gu_land, wide, qkv_land, kv_all, o_heads, bias, wa, wb, wgu, wd,
+    att_land, gu_land, wide, qkv_land, kv_all, o_heads, bias, wa, wb, wlast, wgu, wd,
     xn_all, gd_all, mn_all, att_all, q_heads, k_heads, v_heads, probs, middle, act, gboth, turn_x, turn_n, turn_a,
     gn_send, gn_land, br_send, br_land, gu_mate, gu_zone, dn_mate, dn_zone, gmid, do_heads, dkv, kv_mate, kv_zone, kv_tot,
     cut_land, ma_mate, ma_zone, gx_land, sends, recvs,
@@ -670,7 +694,7 @@
     att_send = qkv_send = cut_send = act.reshape(4, tok, hid)
     gu_send = gboth.reshape(4, tok, 2 * hid)
     gx_send, gs_heads = gd_all, gboth
-    m_att = wb.reshape(4, 4, 2, blk, 384)
+    m_att = wb.reshape(4, 4, 2, blk, 256)
 
     first_cols, late_cols = pl.ds(0, 256), pl.ds(256, 256)
     a2a_att = Spread(net, lambda j: att_send.at[j, pl.ds(0, padded)], lambda j: att_land.at[j])
@@ -681,6 +705,7 @@
     ]
     a = [Lines(net, lambda zz, core, cols=cols: wa.at[own_rows(zz * 2 + core, blk), cols]) for cols in (late_cols, first_cols)]
     b = Slices(net, wb, blk)
+    tail = FromLast(net, wa.reshape(4, 2, blk, 512), wlast.reshape(4, 2, blk, 128))
     gu = [Lines(net, lambda zz, core, h=h: wgu.at[zz, core, :, pl.ds(hid * h, hid)]) for h in range(2)]
     dn = Lines(net, lambda zz, core: wd.at[zz, core])
     kv = Rising(net, lambda zz, core: kv_all.at[zz, core])
@@ -737,7 +762,7 @@
     own = own_rows(s, blk)
     packed = settle(att_land, wide, rows)
     wa[own, :] = packed[:, :512]
-    wb[d, own, :] = packed[:, 384:]
+    wb[d, own, :] = packed[:, 512:]
     for line in a:
         line.start()
     for k in (1, 2, 3):
@@ -835,6 +860,7 @@
         return carry
 
     net.finish(xs, *a, a2a_gu)
+    tail.start()
     lax.fori_loop(0, 2, attend, 0)
     dn.step(2)
     gu[0].step(1)
@@ -844,13 +870,15 @@
     dn.step(3)
     gu[0].step(2)
     gu[1].step(1)
+    tail.pass_on()
     lax.fori_loop(4, 6, attend, 0)
     b.corner(3)
     b.take()
+    tail.take()
     for j in range(H // 2):
         att_all[d, :, 128 * j : 128 * j + 128] = joined(o_heads, j, tok).astype(BF)
     full = att_all[d]
-    branch = [dot_nn(full, wb[j, :, 128:]) for j in range(4)] + [dot_nn(full, wb[3, :, :128])]
+    branch = [dot_nn(full, wb[j]) for j in range(4)] + [dot_nn(full, wlast[...])]
     mid = x_in[0].astype(F32) + scale_attn * jnp.concatenate(branch, axis=1)
     middle[...] = mid
     mn_all[d] = (mid * norm_scale(mid)).astype(BF)
@@ -871,7 +899,7 @@
     dn.take()
     gu[0].take()
     ats.start()
-    net.finish(b, kv, gs, *a2a_qkv)
+    net.finish(b, tail, kv, gs, *a2a_qkv)
 
     def by_cols(send, land, width):
         return [
@@ -956,13 +984,13 @@
             part = dot_nt(gboth[:, halves[h]], wgu_flat[cols, halves[h]]).reshape(4, tok, 384)
             if h == 0:
                 gn_send[:, :, cols] = part.astype(BF)
+                if n == 1:
+                    pair_dn(h)
+                    dn_sum.falling(0)
+                    dn_sum.falling(1, True)
             else:
                 gn_send[:, :, cols] = (gn_send[:, :, cols].astype(F32) + part).astype(BF)
                 gn[n].start()
-        if h == 0:
-            pair_dn(h)
-            dn_sum.falling(0)
-            dn_sum.falling(1, True)
 
     def grads_gu(h):
         net.finish(gu[h])
@@ -995,9 +1023,9 @@
     cut_o.start()
     ats.pass_on()
     cut_land[d, :, 512:768] = cut_send[d, :, 512:768]
-    g_att = dot_nt(gba[:, 1024:1152], wb[3, :, :128])
+    g_att = dot_nt(gba[:, 1024:1152], wlast[...])
     for j in range(4):
-        g_att = g_att + dot_nt(gba[:, 256 * j : 256 * j + 256], wb[j, :, 128:])
+        g_att = g_att + dot_nt(gba[:, 256 * j : 256 * j + 256], wb[j])
     for h in range(H):
         do_heads[h // groups, tok * (h % groups) : tok * (h % groups) + tok, :] = g_att[:, HD * h : HD * h + HD].astype(BF)
 
@@ -1103,6 +1131,8 @@
     turn_x[...] = att_all[...].reshape(span, dim).T
     pair_o = grads(2, [dot_nn(turn_x[...], cut_land[:, :, o_cols].reshape(span, 256))])
     turn_n[...] = xn_all[...].reshape(span, dim).T
+    dn_sum.rising(2, False)
+    gu_sum[0].rising(2, False)
     for n in range(2):
         kv_sum[n].relay(0)
         kv_sum[n].relay(1)
@@ -1111,7 +1141,7 @@
     gu_sum[1].stage(1)
     sum_o = grads_chain(2, pair_o)
     sum_q = grads_chain(0, pair_q)
-    gu_sum[0].between(2)
+    gu_sum[0].falling(2, False)
 
     for n in range(2):
         kv_sum[n].own()
@@ -1127,9 +1157,8 @@
     sum_q.stage(1)
     gu_sum[1].between(2)
     gu_sum[0].last()
+    gu_sum[1].last()
     cut_l.take()
-    gu_sum[1].last()
-    dn_sum.rising(2, False)
     last = cut_land[:, :, 384:512].reshape(span, 128)
     cuts = cut_land[:, :, :512].reshape(span, 512)
     lane = lax.broadcasted_iota(jnp.int32, cuts.shape, 1)
@@ -1143,9 +1172,9 @@
     sum_l = grads_straight(1, pair_l)
     br[0].take()
     block_out[0] = (middle[...] + scale_mlp * plane_sum(net, br_send, br_land)).astype(BF)
-    dn_sum.last()
     sum_o.stage(2)
     sum_q.stage(2)
+    dn_sum.last()
     for k in range(2):
         gu_sum[k].own()
         unsettle(wgu[z, c, :, halves[k]].astype(F32), wide, gu_land, rows, halves[k])
@@ -1190,7 +1219,8 @@
         ((KV, 3 * tok, HD), F32),
         ((tok, length), F32),
         ((dim, 512), BF),
-        ((4, dim, 384), BF),
+        ((4, dim, 256), BF),
+        ((dim, 128), BF),
         ((4, 2, blk, 2 * hid), BF),
         ((4, 2, ffr, dim), BF),
         plane,

time: 172 us -> 170 us (0.988)
    pallas_call x1, Pallas kernels: 165 us -> 163 us  [layer(): pl.pallas_call(layer_kernel, out_shape=[jax.ShapeDtypeStruct(*o) for o in...]
where the time goes in v9:
time: 170 us; the launch traced here: 169 us
  Pallas kernels  167 us (98%)
    pallas_call x1, Pallas kernels, layer(): pl.pallas_call(layer_kernel, out_shape=[jax.ShapeDtypeStruct(*o) for o in...  163 us
    pallas_call x1, Pallas kernels, gradients(): pl.pallas_call(grads_kernel, out_shape=[jax.ShapeDtypeStruct(block.shape,...  3.66 us

profile of v9, /device:TPU:0, one launch (start us, length us, event | category | flops | bytes accessed | tf_op | source)
XLA Modules:
  0.0 168.7 jit_solution(14601771266762887225)
XLA Ops:
  0.6 0.0 copy-start
  0.7 0.7 copy-done
  1.3 0.1 copy.27
  1.4 0.6 reshape.39.keep_mask
  2.0 163.0 %k_layer.1 = (bf16[1,128,1152]{2,1,0:T(8,128)(2,1)}, f32[1,128,1152]{2,1,0:T(8,128)}, bf16[4,48,1536]{2,1,0:T(8,128)(2,1)}, bf16[4,48,768]{2,1,0:T(8,128)(2,1)}, bf16[96,1152]{1,0:T(8,128)(2,1)}) custom-call(bf16[1,128,1152]{2,1,0:T(8,128)(2,1)} %x_in.1, bf16[1,128,1152]{2,1,0:T(8,128)(2,1)} %cot_in.1, bf16[36,1152]{1,0:T(8,128)(2,1)} %query.3, ...), custom_call_target="tpu_custom_call" | custom-call | tf_op jit(solution)/shard_map/k_layer/pallas_call | solution.py:1259
  165.0 3.7 %k_grads.1 = (bf16[1,128,1152]{2,1,0:T(8,128)(2,1)}, f32[1,128,1152]{2,1,0:T(8,128)}, f32[1,36]{1,0:T(1,128)}, f32[36,1152]{1,0:T(8,128)}, f32[36,384]{1,0:T(8,1...) custom-call(bf16[36,1152]{1,0:T(8,128)(2,1)} %query.3, ...), custom_call_target="tpu_custom_call" | custom-call | tf_op jit(solution)/shard_map/k_grads/pallas_call | solution.py:1310
Async XLA Ops:
  0.6 0.7 copy-start

commit v10 on v9

--- a/solution.py
+++ b/solution.py
@@ -206,7 +206,7 @@
 
 MESH = pl.DeviceIdType.MESH
 LIMIT = 60 * 2**20
-SENDS, RECVS = 120, 204
+SENDS, RECVS = 92, 204
 BF, F32 = jnp.bfloat16, jnp.float32
 
 
@@ -749,7 +749,7 @@
     gu_land[d] = gu_send[d, :padded, :]
     sample = seq_order[d]
     scale_attn, scale_mlp = [
-        jnp.full((1, 1), keep_mask[2 * sample + i].astype(F32), F32) / jnp.full((1, 1), keep_rate[i], F32) for i in range(2)
+        jnp.full((1, 1), keep_mask[i, sample].astype(F32), F32) / jnp.full((1, 1), keep_rate[i], F32) for i in range(2)
     ]
     gd_all[d] = (cot_in[0].astype(F32) * scale_mlp).astype(BF)
     wd[z, c] = down[...]
@@ -875,6 +875,7 @@
     b.corner(3)
     b.take()
     tail.take()
+    net.finish(b, tail, kv, *a2a_qkv)
     for j in range(H // 2):
         att_all[d, :, 128 * j : 128 * j + 128] = joined(o_heads, j, tok).astype(BF)
     full = att_all[d]
@@ -899,7 +900,7 @@
     dn.take()
     gu[0].take()
     ats.start()
-    net.finish(b, tail, kv, gs, *a2a_qkv)
+    net.finish(gs)
 
     def by_cols(send, land, width):
         return [
@@ -1113,6 +1114,7 @@
 
     q_cols, l_cols, o_cols = pl.ds(0, 256), pl.ds(256, 256), pl.ds(512, 256)
     quarter = pl.ds(0, 256)
+    net.finish(ms, *gn, *gu_pair, *dn_pair)
     lax.fori_loop(0, 3, pull, 0)
     kv_pair[0].start()
     lax.fori_loop(3, 4, pull, 0)
@@ -1158,6 +1160,7 @@
     gu_sum[1].between(2)
     gu_sum[0].last()
     gu_sum[1].last()
+    net.finish(ats, cut_o, cut_q, *kv_pair)
     cut_l.take()
     last = cut_land[:, :, 384:512].reshape(span, 128)
     cuts = cut_land[:, :, :512].reshape(span, 512)
@@ -1337,7 +1340,7 @@
     gains = (attn_norm.reshape(1, rows), mlp_norm.reshape(1, rows))
     weights = (query_weight, key_weight, value_weight, output_weight, gate_weight, up_weight)
     results = layer(
-        hidden_in, cotangent, weights, down_weight, gains, doc_starts, keep_mask.reshape(-1), keep_rate, seq_order
+        hidden_in, cotangent, weights, down_weight, gains, doc_starts, keep_mask.T, keep_rate, seq_order
     )
     outs = list(gradients(*weights, gains, results))
     outs[2], outs[7] = outs[2].reshape(rows), outs[7].reshape(rows)

time: 170 us -> 168 us (0.988)
  no operation moved by 1% of the time
where the time goes in v10:
time: 168 us; the launch traced here: 167 us
  Pallas kernels  166 us (99%)
    pallas_call x1, Pallas kernels, layer(): pl.pallas_call(layer_kernel, out_shape=[jax.ShapeDtypeStruct(*o) for o in...  163 us
    pallas_call x1, Pallas kernels, gradients(): pl.pallas_call(grads_kernel, out_shape=[jax.ShapeDtypeStruct(block.shape,...  3.66 us

profile of v10, /device:TPU:0, one launch (start us, length us, event | category | flops | bytes accessed | tf_op | source)
XLA Modules:
  0.0 167.1 jit_solution(5142250963227695278)
XLA Ops:
  0.6 162.7 %k_layer.1 = (bf16[1,128,1152]{2,1,0:T(8,128)(2,1)}, f32[1,128,1152]{2,1,0:T(8,128)}, bf16[4,48,1536]{2,1,0:T(8,128)(2,1)}, bf16[4,48,768]{2,1,0:T(8,128)(2,1)}, bf16[96,1152]{1,0:T(8,128)(2,1)}) custom-call(bf16[1,128,1152]{2,1,0:T(8,128)(2,1)} %x_in.1, bf16[1,128,1152]{2,1,0:T(8,128)(2,1)} %cot_in.1, bf16[36,1152]{1,0:T(8,128)(2,1)} %query.3, ...), custom_call_target="tpu_custom_call" | custom-call | tf_op jit(solution)/shard_map/k_layer/pallas_call | solution.py:1262
  163.4 3.7 %k_grads.1 = (bf16[1,128,1152]{2,1,0:T(8,128)(2,1)}, f32[1,128,1152]{2,1,0:T(8,128)}, f32[1,36]{1,0:T(1,128)}, f32[36,1152]{1,0:T(8,128)}, f32[36,384]{1,0:T(8,1...) custom-call(bf16[36,1152]{1,0:T(8,128)(2,1)} %query.3, ...), custom_call_target="tpu_custom_call" | custom-call | tf_op jit(solution)/shard_map/k_grads/pallas_call | solution.py:1313

commit v11 on v10

--- a/solution.py
+++ b/solution.py
@@ -206,7 +206,7 @@
 
 MESH = pl.DeviceIdType.MESH
 LIMIT = 60 * 2**20
-SENDS, RECVS = 92, 204
+SENDS, RECVS = 100, 212
 BF, F32 = jnp.bfloat16, jnp.float32
 
 
@@ -708,7 +708,9 @@
     tail = FromLast(net, wa.reshape(4, 2, blk, 512), wlast.reshape(4, 2, blk, 128))
     gu = [Lines(net, lambda zz, core, h=h: wgu.at[zz, core, :, pl.ds(hid * h, hid)]) for h in range(2)]
     dn = Lines(net, lambda zz, core: wd.at[zz, core])
-    kv = Rising(net, lambda zz, core: kv_all.at[zz, core])
+    kv = [
+        Rising(net, lambda zz, core, i=i: kv_all.at[zz, core, :, pl.ds(KV * HD * i, KV * HD)]) for i in range(2)
+    ]
     xs = Plane(net, xn_all)
     gs = Plane(net, gd_all)
     ms = Plane(net, mn_all)
@@ -808,7 +810,8 @@
     places = [(0, 256), (0, 384), (1, 256), (1, 384), (2, 256), (3, 256)]
     for i, (j, col) in enumerate(places):
         kv_all[z, c, :, 128 * i : 128 * i + 128] = qkv_land[j, :, col : col + 128]
-    kv.start()
+    for line in kv:
+        line.start()
     b.step(2)
     b.spread(2)
     a2a_gu.take()
@@ -818,7 +821,8 @@
     b.spread(3)
     for half in gu:
         half.start(True)
-    kv.step(1)
+    for line in kv:
+        line.step(1)
     b.pass_on(0)
     b.pass_on(1)
     a2a_qkv[1].take()
@@ -835,15 +839,18 @@
     key = lax.broadcasted_iota(jnp.int32, bias.shape, 1)
     bias[...] = jnp.where((key <= position) & (key >= first), 0.0, MASKED)
 
-    kv.step(2)
+    for line in kv:
+        line.step(2)
     gu[0].start(False)
     b.pass_on(2)
     b.pass_on(3)
     b.corner(0)
     b.corner(1)
-    kv.step(3)
+    for line in kv:
+        line.step(3)
     dn.step(1)
-    kv.take()
+    for line in kv:
+        line.take()
     for j in range(8):
         for k in range(KV):
             k_heads[k, pl.ds(tok * j, tok), :] = kv_all[j // 2, j % 2, :, HD * k : HD * k + HD]
@@ -875,7 +882,7 @@
     b.corner(3)
     b.take()
     tail.take()
-    net.finish(b, tail, kv, *a2a_qkv)
+    net.finish(b, tail, *kv, *a2a_qkv)
     for j in range(H // 2):
         att_all[d, :, 128 * j : 128 * j + 128] = joined(o_heads, j, tok).astype(BF)
     full = att_all[d]

time: 168 us -> 167 us (level)
  no operation moved by 1% of the time
where the time goes in v11:
time: 167 us; the launch traced here: 166 us
  Pallas kernels  165 us (99%)
    pallas_call x1, Pallas kernels, layer(): pl.pallas_call(layer_kernel, out_shape=[jax.ShapeDtypeStruct(*o) for o in...  162 us
    pallas_call x1, Pallas kernels, gradients(): pl.pallas_call(grads_kernel, out_shape=[jax.ShapeDtypeStruct(block.shape,...  3.66 us

profile of v11, /device:TPU:0, one launch (start us, length us, event | category | flops | bytes accessed | tf_op | source)
XLA Modules:
  0.0 166.1 jit_solution(13779056137944832199)
XLA Ops:
  0.6 161.8 %k_layer.1 = (bf16[1,128,1152]{2,1,0:T(8,128)(2,1)}, f32[1,128,1152]{2,1,0:T(8,128)}, bf16[4,48,1536]{2,1,0:T(8,128)(2,1)}, bf16[4,48,768]{2,1,0:T(8,128)(2,1)}, bf16[96,1152]{1,0:T(8,128)(2,1)}) custom-call(bf16[1,128,1152]{2,1,0:T(8,128)(2,1)} %x_in.1, bf16[1,128,1152]{2,1,0:T(8,128)(2,1)} %cot_in.1, bf16[36,1152]{1,0:T(8,128)(2,1)} %query.3, ...), custom_call_target="tpu_custom_call" | custom-call | tf_op jit(solution)/shard_map/k_layer/pallas_call | solution.py:1269
  162.4 3.7 %k_grads.1 = (bf16[1,128,1152]{2,1,0:T(8,128)(2,1)}, f32[1,128,1152]{2,1,0:T(8,128)}, f32[1,36]{1,0:T(1,128)}, f32[36,1152]{1,0:T(8,128)}, f32[36,384]{1,0:T(8,1...) custom-call(bf16[36,1152]{1,0:T(8,128)(2,1)} %query.3, ...), custom_call_target="tpu_custom_call" | custom-call | tf_op jit(solution)/shard_map/k_grads/pallas_call | solution.py:1320
